TPU v7x, 32 devices: a whole 2x2x4 slice. The times are simulated.
32 devices in a mesh: prow: 2 (over x), pcol: 16 (over z, y, core).
Axes of the slice: x: 2, y: 2, z: 4, core: 2. Of those that a mesh axis runs over, the one named last changes fastest.
Arguments:
- segment: float32 [8, 2, 512, 8192], P(None, 'prow', None, 'pcol'), as said below
- above_rows: float32 [2048, 8192], P('prow', 'pcol'), may hold values from -6 to 6
- basis_rows: float32 [2048, 8192], P('prow', 'pcol'), may hold values from -6 to 6
- factors: float32 [2, 16, 512, 512], P(None, 'pcol'), as said below
- swap_counts: int32 [2, 16], replicated, may hold values from 0 to 256, as said below
Outputs:
- segment_out: float32 [8, 2, 512, 8192], P(None, 'prow', None, 'pcol')
- above_out: float32 [2048, 8192], P('prow', 'pcol')
- basis_out: float32 [2048, 8192], P('prow', 'pcol')
Inputs may be any that keep to these rules, and one draw needn't show every extreme that they name: segment is upper quasi-triangular: below the diagonal it is nonzero only just under the diagonal, at odd rows, never in two rows in a row. Each factors[phase, k] is an orthogonal 512 x 512 matrix. `swap_counts`: a window is applied where its count is positive and left out where it is 0; the second phase's window 16 - 1 always has count 0.
All inputs are finite; a program needn't handle non-finite values.
Results may differ from a plain program's by a relative error of at most 0.000088.
Values sent between devices are 32-bit elements; how exact they have to be, the bound alone decides.
No kernel may reach another device: no remote copies, remote signals or barrier semaphores. Data moves between devices by JAX's collectives and lax.ppermute only.
A program may use at most 128 MiB of HBM per device.

v0:
```python
import jax
import jax.numpy as jnp
from jax import lax
from jax.sharding import PartitionSpec as P

HIGHEST = lax.Precision.HIGHEST


def spread(block, axis, source):
    block = jnp.where(lax.axis_index(axis) == source, block, jnp.zeros_like(block))
    return lax.psum(block, axis)


def padded_2(block, sides, width):
    for axis, dim in sides:
        count = lax.axis_size(axis)
        forward = [(i, i + 1) for i in range(count - 1)]
        backward = [(target, source) for source, target in forward]
        low = lax.ppermute(
            lax.slice_in_dim(block, block.shape[dim] - width, None, axis=dim), axis, forward
        )
        high = lax.ppermute(lax.slice_in_dim(block, 0, width, axis=dim), axis, backward)
        block = jnp.concatenate([low, block, high], axis=dim)
    return block


def passed_along(block, axis, distance):
    devices = range(lax.axis_size(axis))
    route = [(i - distance, i) for i in devices if i - distance in devices]
    return lax.ppermute(block, axis, route)


def shifted(x, axis, by):
    peers = lax.axis_size(axis)
    return lax.ppermute(x, axis, [(i, (i + by) % peers) for i in range(peers)])


def product(left, right):
    return jnp.dot(left, right, precision=HIGHEST, preferred_element_type=jnp.float32)


def transposed(factor_stack, blocks):
    return jnp.einsum(
        "kwv,kwc->kvc", factor_stack, blocks, precision=HIGHEST, preferred_element_type=jnp.float32
    )


def body(segment, above_rows, basis_rows, factors, swap_counts):
    tile_count = segment.shape[0]
    window = segment.shape[2]
    half_width = window // 2
    grid_rows = lax.axis_size("prow")
    grid_cols = lax.axis_size("pcol")
    row_place = lax.axis_index("prow")
    col_place = lax.axis_index("pcol")
    identity = jnp.eye(window, dtype=jnp.float32)
    first_counts = swap_counts[0]
    second_counts = swap_counts[1]
    tile_index = jnp.arange(tile_count, dtype=jnp.int32) * grid_rows + row_place
    own_first = factors[0, 0]
    own_second = factors[1, 0]
    seg_rows = tile_count * window
    above_count = above_rows.shape[0]
    stacked = jnp.concatenate([segment.reshape(seg_rows, window), above_rows, basis_rows], axis=0)
    first_here = first_counts[col_place] > 0
    stacked = product(stacked, jnp.where(first_here, own_first, identity))
    first_active = first_counts[tile_index] > 0
    lower_active = (second_counts[tile_index] > 0) & (tile_index < grid_cols - 1)
    upper_active = (second_counts[jnp.maximum(tile_index - 1, 0)] > 0) & (tile_index >= 1)
    first_list = []
    lower_list = []
    upper_list = []
    joined = jnp.concatenate([own_first, own_second[:, :half_width]], axis=1)
    upper_part = own_second[:, half_width:]
    for tile_slot in range(tile_count):
        received = spread(joined, "pcol", tile_index[tile_slot])
        first_list.append(received[:, :window])
        lower_list.append(received[:, window:])
        upper_root = (tile_index[tile_slot] - 1 + grid_cols) % grid_cols
        upper_list.append(spread(upper_part, "pcol", upper_root))
    upper_stack = jnp.stack(upper_list)
    first_stack = jnp.where(first_active[:, None, None], jnp.stack(first_list), identity)
    lower_stack = jnp.where(
        lower_active[:, None, None], jnp.stack(lower_list), identity[:, :half_width]
    )
    upper_stack = jnp.where(upper_active[:, None, None], upper_stack, identity[:, half_width:])
    blocks = transposed(first_stack, stacked[:seg_rows].reshape(tile_count, window, window))
    stacked = jnp.concatenate([blocks.reshape(seg_rows, window), stacked[seg_rows:]], axis=0)
    padded = padded_2(stacked, (("pcol", 1),), half_width)
    left_rim = padded[:, :half_width]
    mine_left = padded[:, half_width:window]
    mine_right = padded[:, window : window + half_width]
    right_rim = padded[:, window + half_width :]
    current_on = (second_counts[col_place] > 0) & (col_place < grid_cols - 1)
    current = jnp.where(current_on, own_second, identity)
    previous = passed_along(own_second[:, half_width:], "pcol", 1)
    previous_on = (second_counts[jnp.maximum(col_place - 1, 0)] > 0) & (col_place >= 1)
    previous = jnp.where(previous_on, previous, identity[:, half_width:])
    new_left = product(left_rim, previous[:half_width]) + product(mine_left, previous[half_width:])
    new_right = product(mine_right, current[:half_width, :half_width]) + product(
        right_rim, current[half_width:, :half_width]
    )
    stacked = jnp.concatenate([new_left, new_right], axis=1)
    blocks = stacked[:seg_rows].reshape(tile_count, window, window)
    top_halves = blocks[:, :half_width]
    bottoms = blocks[:, half_width:]
    next_tops = shifted(top_halves, "prow", -1)
    next_tops = jnp.where(row_place == grid_rows - 1, jnp.roll(next_tops, -1, axis=0), next_tops)
    prev_bottoms = shifted(bottoms, "prow", 1)
    prev_bottoms = jnp.where(row_place == 0, jnp.roll(prev_bottoms, 1, axis=0), prev_bottoms)
    new_bottoms = transposed(lower_stack[:, :half_width], bottoms) + transposed(
        lower_stack[:, half_width:], next_tops
    )
    new_tops = transposed(upper_stack[:, :half_width], prev_bottoms) + transposed(
        upper_stack[:, half_width:], top_halves
    )
    segment_out = jnp.concatenate([new_tops, new_bottoms], axis=1).reshape(segment.shape)
    return (
        segment_out,
        stacked[seg_rows : seg_rows + above_count],
        stacked[seg_rows + above_count :],
    )


def solution(mesh):
    placed = (
        P(None, "prow", None, "pcol"),
        P("prow", "pcol"),
        P("prow", "pcol"),
        P(None, "pcol", None, None),
        P(),
    )
    return jax.shard_map(
        body,
        mesh=mesh,
        in_specs=placed,
        out_specs=(P(None, "prow", None, "pcol"), P("prow", "pcol"), P("prow", "pcol")),
        check_vma=False,
    )
```

profile of v0, /device:TPU:25, one launch (start us, length us, event | category | flops | bytes accessed | tf_op | source)
XLA Modules:
  0.0 724.5 jit_solution(14679690069257002088)
XLA Ops:
  7.2 0.7 fusion.72
  18.1 1.7 fusion.68
  20.5 2.4 fusion.70
  22.9 2.1 broadcast_select_fusion.3
  24.9 3.8 broadcast_select_fusion.2
  28.8 0.7 copy-done.20
  30.0 27.1 %fusion = f32[6144,512]{1,0:T(8,128)S(1)} fusion(f32[1024,512]{1,0:T(8,128)} %param.7, f32[1024,512]{1,0:T(8,128)} %param.6, f32[4096,512]{1,0:T(8,128)} %bitcast.131, pred[]{:T(512)} %bitcast.31, f32[1,1,512,512]{2,3,1,0:T(8,128)S(1)} %copy.24), kind=kOutput, calls=%fused_computation.7 | convolution fusion | flops 19334430720 | bytes 26214400 | tf_op jit(solution)/shard_map/dot_general | solution.py:39
  57.2 2.5 slice.249
  59.7 4.4 slice.248
  64.8 273.7 %all-reduce.3.cloned.1.call-done = (f32[512,768]{0,1:T(8,128)}, f32[512,768]{0,1:T(8,128)}, f32[512,768]{0,1:T(8,128)}, f32[512,768]{0,1:T(8,128)}, f32[512,768]...) async-done(((f32[512,768]{0,1:T(8,128)}, ...) | async-done | bytes 16777232 | tf_op jit(solution)/shard_map/psum | solution.py:11
  338.5 1.4 fusion.40
  340.0 1.6 fusion.39
  342.3 0.8 copy-done.11
  343.6 3.3 copy-done.5
  346.9 17.3 %fusion.7 = f32[8,512,512]{2,1,0:T(8,128)S(1)} fusion(f32[8,512,512]{2,1,0:T(8,128)} %bitcast.127, f32[8,512,512]{1,2,0:T(8,128)} %copy-done.5, f32[512,512]{0,1:T(8,128)S(1)} %fusion.42, pred[8]{0:T(512)(128)(4,1)S(1)} %broadcast_compare_fusion), kind=kOutput, calls=%fused_computation.17 | convolution fusion | flops 12886999040 | bytes 26214408 | tf_op jit(solution)/shard_map/kwv,kwc->kvc/dot_general | solution.py:43
  364.2 5.9 fusion.9
  370.1 3.5 collective-permute-start
  373.7 1.9 collective-permute-start.2
  375.6 3.6 collective-permute-start.1
  379.3 0.6 gather_fusion.2
  381.8 0.6 gather_fusion
  382.7 64.8 %collective-permute-done.1 = f32[512,256]{0,1:T(8,128)} collective-permute-done((f32[512,256]{0,1:T(8,128)}, f32[512,256]{0,1:T(8,128)}, u32[]{:S(2)}, u32[]{:S(2)}) %collective-permute-start.1) | collective-permute-done | bytes 524320 | tf_op jit(solution)/shard_map/ppermute | solution.py:30
  447.5 1.2 fusion.69
  448.7 0.8 constant_dynamic-update-slice_fusion.7
  449.6 0.9 constant_dynamic-update-slice_fusion.6
  450.4 0.9 constant_dynamic-update-slice_fusion.5
  451.3 0.8 constant_dynamic-update-slice_fusion.4
  452.2 0.8 constant_dynamic-update-slice_fusion.3
  453.0 0.9 constant_dynamic-update-slice_fusion.2
  453.8 8.2 %fusion.55 = f32[6144,256]{0,1:T(8,128)S(1)} fusion(f32[6144,256]{1,0:T(8,128)} %get-tuple-element.27, f32[512,512]{0,1:T(8,128)S(1)} %fusion.43), kind=kOutput, calls=%fused_computation.102 | convolution fusion | flops 4831838208 | bytes 12845056 | tf_op jit(solution)/shard_map/dot_general | solution.py:39
  462.0 8.2 %fusion.57 = f32[6144,256]{0,1:T(8,128)S(1)} fusion(f32[6144,256]{1,0:T(8,128)} %get-tuple-element.28, f32[512,256]{0,1:T(8,128)S(1)} %get-tuple-element.42), kind=kOutput, calls=%fused_computation.104 | convolution fusion | flops 4831838208 | bytes 12845056 | tf_op jit(solution)/shard_map/dot_general | solution.py:39
  470.2 8.3 %convolution_add_fusion.1 = f32[6144,256]{0,1:T(8,128)S(1)} fusion(f32[6144,256]{0,1:T(8,128)S(1)} %fusion.57, f32[6144,256]{1,0:T(8,128)} %collective-permute-done, f32[512,256]{0,1:T(8,128)S(1)} %get-tuple-element.42), kind=kOutput, calls=%fused_computation.20 | convolution fusion | flops 4833411072 | bytes 19136512 | tf_op jit(solution)/shard_map/dot_general | solution.py:39
  478.5 38.0 %collective-permute-done.2 = f32[6144,256]{1,0:T(8,128)} collective-permute-done((f32[6144,256]{1,0:T(8,128)}, f32[6144,256]{1,0:T(8,128)}, u32[]{:S(2)}, u32[]{:S(2)}) %collective-permute-start.2) | collective-permute-done | bytes 6291488 | tf_op jit(solution)/shard_map/ppermute | solution.py:22
  516.5 8.3 %convolution_add_fusion = f32[6144,256]{0,1:T(8,128)S(1)} fusion(f32[6144,256]{0,1:T(8,128)S(1)} %fusion.55, f32[6144,256]{1,0:T(8,128)} %collective-permute-done.2, f32[512,512]{0,1:T(8,128)S(1)} %fusion.43), kind=kOutput, calls=%fused_computation.19 | convolution fusion | flops 4833411072 | bytes 19136512 | tf_op jit(solution)/shard_map/dot_general | solution.py:39
  524.8 2.6 copy-done.1
  527.5 3.8 fusion.6
  531.3 9.1 %copy.22 = f32[4096,512]{1,0:T(8,128)} copy(f32[4096,512]{0,1:T(8,128)} %fusion.6) | data formatting | bytes 16777216 | tf_op jit(solution)/shard_map/reshape | solution.py:104
  540.4 8.2 %fusion.67 = (f32[8,256,512]{2,1,0:T(8,128)}, f32[8,256,512]{2,1,0:T(8,128)}) fusion(f32[8,512,512]{2,1,0:T(8,128)} %bitcast.119), kind=kLoop, calls=%fused_computation.137 | loop fusion | bytes 16777216 | tf_op jit(solution)/shard_map/slice | solution.py:106
  548.5 1.2 collective-permute-start.3
  550.0 1.1 fusion.52
  551.1 1.1 fusion.51
  552.2 1.1 fusion.50
  553.3 1.1 fusion.49
  554.3 1.1 fusion.48
  555.4 1.1 fusion.47
  556.5 1.9 fusion.46
  558.4 0.8 constant_dynamic-update-slice_fusion
  559.3 1.2 fusion.45
  560.5 2.8 broadcast_select_fusion
  563.3 5.7 broadcast_select_fusion.1
  569.0 1.7 pad_maximum_fusion.1
  570.8 2.9 copy.21
  573.6 1.8 copy.20
  575.4 6.8 fusion.22
  582.3 5.8 fusion.20
  588.1 53.4 %collective-permute-done.3 = f32[8,256,512]{2,1,0:T(8,128)} collective-permute-done((f32[8,256,512]{2,1,0:T(8,128)}, f32[8,256,512]{2,1,0:T(8,128)}, u32[]{:S(2)}, u32[]{:S(2)}) %collective-permute-start.3) | collective-permute-done | bytes 4194336 | tf_op jit(solution)/shard_map/ppermute | solution.py:35
  641.5 1.1 slice.259
  642.6 2.5 slice.260
  645.1 52.1 %collective-permute-done.4 = f32[8,256,512]{2,1,0:T(8,128)} collective-permute-done((f32[8,256,512]{2,1,0:T(8,128)}, f32[8,256,512]{2,1,0:T(8,128)}, u32[]{:S(2)}, u32[]{:S(2)}) %collective-permute-start.4) | collective-permute-done | bytes 4194336 | tf_op jit(solution)/shard_map/ppermute | solution.py:35
  697.2 1.9 slice.275
  699.0 2.5 slice.274
  701.5 4.6 fusion.30
  706.1 6.9 fusion.26
  713.0 4.4 maximum_bitcast_fusion
  (73 shorter events, 4.4 us)
Async XLA Ops:
  7.2 331.3 %all-reduce.3.cloned.1.call-start = ((), (), s32[]{:S(2)}) async-start(), calls=%async_computation | async-start | bytes 33554432 | tf_op jit(solution)/shard_map/psum | solution.py:11
  28.8 0.7 copy-start.20
  338.5 3.0 copy-start.10
  338.5 3.1 copy-start.9
  338.5 3.2 copy-start.8
  339.9 2.2 copy-start.7
  341.5 1.5 copy-start.11
  341.6 1.9 copy-start.6
  343.6 3.3 copy-start.5
  346.9 17.3 %copy-start.2 = (f32[2048,512]{1,0:T(8,128)S(1)}, f32[2048,512]{1,0:T(8,128)}, u32[]{:S(2)}) copy-start(f32[2048,512]{1,0:T(8,128)} %slice.249) | copy-start | bytes 12582916
  370.1 79.4 %copy-start.17 = (f32[1,512,256]{1,2,0:T(8,128)S(1)}, f32[1,512,256]{1,2,0:T(8,128)}, u32[]{:S(2)}) copy-start(f32[1,512,256]{1,2,0:T(8,128)} %get-tuple-element.18) | copy-start | bytes 1572868
  370.1 100.1 %collective-permute-start = (f32[6144,256]{1,0:T(8,128)}, f32[6144,256]{1,0:T(8,128)}, u32[]{:S(2)}, u32[]{:S(2)}) collective-permute-start(f32[6144,256]{1,0:T(8,128)} %get-tuple-element.27), channel_id=1, source_target_pairs={{0,1},{1,2},{2,3},{3,4},{4,5},{5,6},{6,7},{7,8},{8,9},{9,10},{10,1... | collective-permute-start | bytes 18874376 | tf_op jit(solution)/shard_map/ppermute | solution.py:19
  373.7 142.9 %collective-permute-start.2 = (f32[6144,256]{1,0:T(8,128)}, f32[6144,256]{1,0:T(8,128)}, u32[]{:S(2)}, u32[]{:S(2)}) collective-permute-start(f32[6144,256]{1,0:T(8,128)} %get-tuple-element.28), channel_id=1, source_target_pairs={{1,0},{2,1},{3,2},{4,3},{5,4},{6,5},{7,6},{8,7},{9,8},{10,9},{11,1... | collective-permute-start | bytes 18874376 | tf_op jit(solution)/shard_map/ppermute | solution.py:22
  375.6 71.9 %collective-permute-start.1 = (f32[512,256]{0,1:T(8,128)}, f32[512,256]{0,1:T(8,128)}, u32[]{:S(2)}, u32[]{:S(2)}) collective-permute-start(f32[512,256]{0,1:T(8,128)} %get-tuple-element.44), channel_id=1, source_target_pairs={{0,1},{1,2},{2,3},{3,4},{4,5},{5,6},{6,7},{7,8},{8,9},{9,10},{10,1... | collective-permute-start | bytes 1572872 | tf_op jit(solution)/shard_map/ppermute | solution.py:30
  379.3 71.2 %copy-start.16 = (f32[1,512,256]{1,2,0:T(8,128)S(1)}, f32[1,512,256]{1,2,0:T(8,128)}, u32[]{:S(2)}) copy-start(f32[1,512,256]{1,2,0:T(8,128)} %get-tuple-element.19) | copy-start | bytes 1572868
  382.5 66.2 %copy-start.18 = (f32[1,512,256]{1,2,0:T(8,128)S(1)}, f32[1,512,256]{1,2,0:T(8,128)}, u32[]{:S(2)}) copy-start(f32[1,512,256]{1,2,0:T(8,128)} %get-tuple-element.17) | copy-start | bytes 1572868
  382.5 68.8 %copy-start.15 = (f32[1,512,256]{1,2,0:T(8,128)S(1)}, f32[1,512,256]{1,2,0:T(8,128)}, u32[]{:S(2)}) copy-start(f32[1,512,256]{1,2,0:T(8,128)} %get-tuple-element.20) | copy-start | bytes 1572868
  382.7 69.5 %copy-start.14 = (f32[1,512,256]{1,2,0:T(8,128)S(1)}, f32[1,512,256]{1,2,0:T(8,128)}, u32[]{:S(2)}) copy-start(f32[1,512,256]{1,2,0:T(8,128)} %get-tuple-element.21) | copy-start | bytes 1572868
  382.7 70.3 %copy-start.13 = (f32[1,512,256]{1,2,0:T(8,128)S(1)}, f32[1,512,256]{1,2,0:T(8,128)}, u32[]{:S(2)}) copy-start(f32[1,512,256]{1,2,0:T(8,128)} %get-tuple-element.22) | copy-start | bytes 1572868
  478.5 46.3 %copy-start = (f32[6144,256]{0,1:T(8,128)}, f32[6144,256]{0,1:T(8,128)S(1)}, u32[]{:S(2)}) copy-start(f32[6144,256]{0,1:T(8,128)S(1)} %convolution_add_fusion.1) | copy-start | bytes 18874372
  524.8 2.7 copy-start.1
  548.5 8.0 %copy-start.19 = (f32[1,512,256]{1,2,0:T(8,128)S(1)}, f32[1,512,256]{1,2,0:T(8,128)}, u32[]{:S(2)}) copy-start(f32[1,512,256]{1,2,0:T(8,128)} %get-tuple-element.23) | copy-start | bytes 1572868
  548.5 93.0 %collective-permute-start.3 = (f32[8,256,512]{2,1,0:T(8,128)}, f32[8,256,512]{2,1,0:T(8,128)}, u32[]{:S(2)}, u32[]{:S(2)}) collective-permute-start(f32[8,256,512]{2,1,0:T(8,128)} %get-tuple-element.29), channel_id=1, source_target_pairs={{0,16},{16,0},{1,17},{17,1},{2,18},{18,2},{3,19},{19,3},{4,20},{20... | collective-permute-start | bytes 12582920 | tf_op jit(solution)/shard_map/ppermute | solution.py:35
  549.7 8.7 %copy-start.12 = (f32[1,512,256]{1,2,0:T(8,128)S(1)}, f32[1,512,256]{1,2,0:T(8,128)}, u32[]{:S(2)}) copy-start(f32[1,512,256]{1,2,0:T(8,128)} %get-tuple-element.24) | copy-start | bytes 1572868
  549.7 147.4 %collective-permute-start.4 = (f32[8,256,512]{2,1,0:T(8,128)}, f32[8,256,512]{2,1,0:T(8,128)}, u32[]{:S(2)}, u32[]{:S(2)}) collective-permute-start(f32[8,256,512]{2,1,0:T(8,128)} %get-tuple-element.30), channel_id=1, source_target_pairs={{0,16},{16,0},{1,17},{17,1},{2,18},{18,2},{3,19},{19,3},{4,20},{20... | collective-permute-start | bytes 12582920 | tf_op jit(solution)/shard_map/ppermute | solution.py:35
  559.3 9.7 %slice-start.2 = ((s8[6291456]{0:T(1024)(128)(4,1)}), s8[4194304]{0:T(1024)(128)(4,1)S(1)}, s32[]{:S(2)}) async-start(s8[6291456]{0:T(1024)(128)(4,1)} %bitcast.124), calls=%async_computation.3 | async-start | bytes 8388608
  560.5 8.5 %slice-start = ((s8[6291456]{0:T(1024)(128)(4,1)}), s8[4194304]{0:T(1024)(128)(4,1)S(1)}, s32[]{:S(2)}) async-start(s8[6291456]{0:T(1024)(128)(4,1)} %bitcast.122), calls=%async_computation.1 | async-start | bytes 8388608
  560.5 8.5 %slice-start.3 = ((s8[6291456]{0:T(1024)(128)(4,1)}), s8[2097152]{0:T(1024)(128)(4,1)S(1)}, s32[]{:S(2)}) async-start(s8[6291456]{0:T(1024)(128)(4,1)} %bitcast.124), calls=%async_computation.4 | async-start | bytes 4194304
  563.3 5.7 slice-start.1
  575.4 6.8 copy-start.3
  645.1 56.4 %copy-start.4 = (f32[8,512,256]{1,2,0:T(8,128)S(1)}, f32[8,512,256]{1,2,0:T(8,128)}, u32[]{:S(2)}) copy-start(f32[8,512,256]{1,2,0:T(8,128)} %broadcast_select_fusion.1) | copy-start | bytes 12582916
Sparse Core Ops, SparseCore 0:
  28.9 309.5 all-reduce.2
where the time goes:
time: 731 us; the launch traced here: 724 us
  waiting for transfers between devices  482 us (66%)
  matrix products  101 us (14%)
  local copies, waits for them, and re-layouts  69.5 us (10%)
  other arithmetic  34.7 us (5%)
  between operations  26.3 us (4%)
  starting transfers between devices  10.6 us (1%)
    psum x1, waiting for transfers between devices, spread(): return lax.psum(block, axis)  274 us
    ppermute x2, waiting for transfers between devices, shifted(): return lax.ppermute(x, axis, [(i, (i + by) % peers) for i in range(peers)])  106 us
    ppermute x1, waiting for transfers between devices, passed_along(): return lax.ppermute(block, axis, route)  64.8 us
    dot_general x5, matrix products, product(): jnp.dot(left, right, precision=HIGHEST, preferred_element_type=jnp.float32)  60.1 us
    dot_general x5, matrix products, transposed(): jnp.einsum('kwv,kwc->kvc', factor_stack, blocks, precision=HIGHEST, prefe...  41.4 us
    ppermute x1, waiting for transfers between devices, padded_2(): lax.ppermute(lax.slice_in_dim(block, 0, width, axis=dim), axis, backward)  38 us
    unnamed x74, local copies, waits for them, and re-layouts  30.4 us
  transfers between devices with their start and end apart: 6, of which 5 were waited for; matrix products, arithmetic and copies ran while one was open for 15% of the time, Pallas kernels for 0%

commit v1 on v0

v1 whole, which is shorter than its diff:
```python
import functools

import jax
import jax.numpy as jnp
from jax import lax
from jax.experimental import pallas as pl
from jax.experimental.pallas import tpu as pltpu
from jax.sharding import PartitionSpec as P

GRID = ("prow", "pcol")
VMEM_LIMIT = 60 * 1024 * 1024


def split(value):
    high = value.astype(jnp.bfloat16)
    return high, (value - high.astype(jnp.float32)).astype(jnp.bfloat16)


def dot3(left, right):
    (lh, ll), (rh, rl) = left, right
    dot = functools.partial(jnp.dot, preferred_element_type=jnp.float32)
    return dot(lh, rh) + (dot(lh, rl) + dot(ll, rh))


PLANE, COL, PLANE0, NEWEST, MEMBER, SWAP_B, FIRST_IN, LAST_IN, LAST_LEVEL, USE_LAST, OWNS, COUNTS = range(12)


def call(kernel, info, grid, in_specs, out_specs, out_shape, scratch, args, alias=None, after=(), opens=False):
    count = len(args)
    after = [a for a in after if all(a is not arg for arg in args)]

    def run(*refs):
        kernel(*refs[: count + 1], *refs[count + 1 + len(after) :])

    return pl.pallas_call(
        run,
        grid_spec=pltpu.PrefetchScalarGridSpec(
            num_scalar_prefetch=1,
            grid=grid,
            in_specs=in_specs + [pl.BlockSpec(memory_space=pl.ANY)] * len(after),
            out_specs=out_specs,
            scratch_shapes=scratch,
        ),
        out_shape=out_shape,
        input_output_aliases=alias or {},
        compiler_params=pltpu.CompilerParams(vmem_limit_bytes=VMEM_LIMIT),
        cost_estimate=pl.CostEstimate(flops=10**14 if opens else 1, bytes_accessed=1, transcendentals=0),
    )(info, *args, *after)


def factor_kernel(paired, cols, info, factors, came, first, first_t, half_a, chain_b, prev, cur):
    window = first.shape[0]
    half = window // 2
    at = info[COL]
    rows = lax.broadcasted_iota(jnp.int32, (window, window), 0)
    lanes = lax.broadcasted_iota(jnp.int32, (window, window), 1)
    identity = (rows == lanes).astype(jnp.float32)
    own = jnp.where(info[COUNTS + at] > 0, factors[0, 0], identity)
    first[...] = own
    if paired:
        owner = at - lax.rem(at, 2) + info[PLANE]
        there = jnp.where(info[COUNTS + owner] > 0, came[...], identity)
        own = jnp.where(info[OWNS] == 1, own, there)
    own = own.T
    first_t[0] = own[:half]
    first_t[1] = own[half:]
    half_a[...] = jnp.where(info[MEMBER] == 1, own[half:], own[:half])
    on = (info[COUNTS + cols + at] > 0) & (at < cols - 1)
    own = jnp.where(on, factors[1, 0], identity)
    prev[...] = own[:, half:]
    cur[...] = own[:, :half]
    chain_b[...] = jnp.where(info[OWNS] == 1, own[:, :half], own[:, half:]).T


def gather_kernel(info, *refs):
    for place, piece in enumerate(refs[:-1]):
        refs[-1][place] = piece[...]


def first_kernel(joint, info, seg, col, factor, prev_top, *rest):
    sends, (last_top, col_h, col_l, carry) = rest[: 2 - joint], rest[2 - joint :]
    half = prev_top.shape[0]
    i = pl.program_id(0)

    @pl.when(i == 0)
    def _():
        col_h[...], col_l[...] = split(col[...])
        carry[...] = prev_top[...]

    mid = split(dot3(split(seg[...]), (col_h[...], col_l[...])))
    out = dot3(split(jnp.concatenate([factor[0], factor[1]], axis=0)), mid)
    sent = jnp.where(info[PLANE0] == 1, carry[...], out[:half])
    if joint:
        sends[0][0] = out[half:]
        sends[0][1] = sent
    else:
        sends[0][...] = out[half:]
        sends[1][...] = sent
    carry[...] = out[:half]
    last_top[...] = out[:half]


def second_kernel(begin, count, tail, info, factor, bottom, sent, got_bottom, got_top, *rest):
    left, right = rest[-2:]
    half = bottom.shape[0]

    @pl.when(pl.program_id(0) < count)
    def _():
        lower, upper = split(factor[info[SWAP_B]]), split(factor[1 - info[SWAP_B]])

        def stacked(one, other):
            return split(jnp.concatenate([one, other], axis=0))

        new_bottom = dot3(lower, stacked(bottom[...], got_top[...]))
        new_top = dot3(upper, stacked(got_bottom[...], sent[...]))
        passing = (info[PLANE0] == 1) & (begin + pl.program_id(0) == info[NEWEST] + 1)
        new_top = jnp.where(passing, sent[...], new_top)
        left[0] = new_bottom[:, :half]
        left[1] = new_top[:, :half]
        right[0] = new_bottom[:, half:]
        right[1] = new_top[:, half:]

    if tail:

        @pl.when(pl.program_id(0) == count)
        def _():
            left[0] = left[1] = rest[0][:, :half]
            right[0] = right[1] = rest[0][:, half:]


def split_columns(prev, cur, scratch):
    prev_h, prev_l, cur_h, cur_l = scratch
    prev_h[...], prev_l[...] = split(prev[...])
    cur_h[...], cur_l[...] = split(cur[...])


def columns(left_in, mine_left, mine_right, right_in, scratch, out):
    prev_h, prev_l, cur_h, cur_l = scratch
    half = mine_left.shape[1]

    def wide(one, other):
        return split(jnp.concatenate([one, other], axis=1))

    out[:, :half] = dot3(wide(left_in, mine_left), (prev_h[...], prev_l[...]))
    out[:, half:] = dot3(wide(mine_right, right_in), (cur_h[...], cur_l[...]))


def third_kernel(begin, last_unit, info, left, right, up_far, up_near, down_near, down_far, down_last, prev, cur, held, out, *scratch):
    del held
    e, h = pl.program_id(0), pl.program_id(1)

    @pl.when((e == 0) & (h == 0))
    def _():
        split_columns(prev, cur, scratch)

    left_in = jnp.where(info[FIRST_IN] == 1, up_far[...], up_near[...])
    far = jnp.where((info[USE_LAST] == 1) & (begin + e == last_unit) & (h == 1), down_last[...], down_far[...])
    right_in = jnp.where(info[LAST_IN] == 1, far, down_near[...])
    columns(left_in, left[...], right[...], right_in, scratch, out)


def last_kernel(info, top, up_far, up_near, down_near, prev, cur, held, out, *scratch):
    del held
    half = top.shape[0]
    split_columns(prev, cur, scratch)
    left_in = jnp.where(info[FIRST_IN] == 1, up_far[...], up_near[...])
    columns(left_in, top[:, :half], top[:, half:], down_near[...], scratch, out)

def rows_kernel(above_blocks, info, above, basis, col, left, right, col_h, col_l):
    half = left.shape[1]
    i = pl.program_id(0)

    @pl.when(i == 0)
    def _():
        col_h[...], col_l[...] = split(col[...])

    rows = jnp.where(i < above_blocks, above[...], basis[...])
    out = dot3(split(rows), (col_h[...], col_l[...]))
    left[...] = out[:, :half]
    right[...] = out[:, half:]


def rows_end_kernel(info, left, right, left_in, right_in, prev, cur, out, *scratch):
    @pl.when(pl.program_id(0) == 0)
    def _():
        split_columns(prev, cur, scratch)

    columns(left_in[...], left[...], right[...], right_in[...], scratch, out)


def whole(shape):
    return pl.BlockSpec(shape, lambda *_: (0,) * len(shape))


def body(segment, above_rows, basis_rows, factors, swap_counts):
    slots = segment.shape[0]
    window = segment.shape[2]
    half = window // 2
    planes = lax.axis_size("prow")
    cols = lax.axis_size("pcol")
    plane = lax.axis_index("prow")
    col = lax.axis_index("pcol")
    f32, bf = jnp.float32, jnp.bfloat16
    paired = planes == 2
    fold = next(size for size in (4, 2, 1) if slots % size == 0) if paired else 1
    group = planes * fold
    levels = slots // fold
    level = col // group
    newest = fold * level + fold - 1
    owner = plane if paired else (plane + planes - 1) % planes
    member = col % planes
    place = [
        plane,
        col,
        plane == 0,
        newest,
        member,
        (plane == 1) & paired,
        col % group == 0,
        col % group == group - 1,
        level == levels - 1,
        (plane == 0) & (level == levels - 2),
        member == plane,
    ]
    info = jnp.concatenate([jnp.stack([jnp.asarray(v, jnp.int32) for v in place]), swap_counts.reshape(-1)])

    def send(value, route):
        return lax.ppermute(value, GRID, [(a * cols + b, c * cols + d) for (a, b), (c, d) in route])

    everyone = [(p, c) for p in range(planes) for c in range(cols)]

    def along(value, step, wanted=lambda c: True):
        route = [((p, c), (p, c + step)) for p, c in everyone if 0 <= c + step < cols and wanted(c)]
        return send(value, route)

    def shape(*dims):
        return jax.ShapeDtypeStruct(dims, f32)

    last = []

    if paired:
        raw = factors[0, 0]
        came = send(raw, [((p, c), (p, c + 1 - 2 * p)) for p, c in everyone if c % 2 == p])
    else:
        came = factors[0, 0]
    own_first, full_first, half_a, chain_b, prev_own, cur = call(
        functools.partial(factor_kernel, paired, cols),
        info,
        (1,),
        [whole((2, 1, window, window)), whole((window, window))],
        [whole((window, window)), whole((2, half, window))]
        + [whole((half, window))] * 2
        + [whole((window, half))] * 2,
        [shape(window, window), shape(2, half, window)] + [shape(half, window)] * 2 + [shape(window, half)] * 2,
        [],
        (factors, came),
    )
    last.append(own_first)
    rows = lax.broadcasted_iota(jnp.int32, (window, half), 0)
    lanes = lax.broadcasted_iota(jnp.int32, (window, half), 1)

    def hopped(value, hop):
        return along(value, group, lambda c: c // group >= hop - 1)

    def chained(value):
        values = [value]
        for hop in range(1, levels):
            values.append(hopped(values[-1], hop))
        return values

    teams = [list(range(g * group, (g + 1) * group)) for g in range(cols // group)]
    if paired:
        pieces_b = chained(chain_b)
        first_factors = [lax.all_gather(v, "pcol", axis_index_groups=teams) for v in chained(half_a)]
    else:

        def shared(value, holder):
            value = jnp.where(member == holder, value, jnp.zeros_like(value))
            return lax.psum(value, "pcol", axis_index_groups=teams)

        full_first = shared(full_first, plane)
        first_factors = chained(full_first)
        both = jnp.stack([shared(chain_b, plane), shared(chain_b, owner)])
        second_factors = jnp.stack(chained(both), axis=1)

    def gather_second():
        out = call(
            gather_kernel,
            info,
            (1,),
            [whole((half, window))] * levels,
            whole((levels, half, window)),
            shape(levels, half, window),
            [],
            pieces_b,
            after=last[-1:],
        )
        last.append(out)
        return lax.all_gather(out, "pcol", axis_index_groups=teams)

    came_prev = along(prev_own, 1)
    prev = jnp.where(col == 0, (rows == lanes + half).astype(f32), came_prev)

    seg = segment.reshape(slots * window, window)

    def slot_of(t, f):
        return lax.rem(f[NEWEST] - t + slots, slots)

    def first_step(batch, prev_top, joint, after, opens):
        count, begin = len(batch), batch[0]
        factor = full_first if begin == 0 else first_factors[begin // fold]
        place = 0 if begin == 0 else fold - 1 - begin % fold
        if joint:
            specs = [pl.BlockSpec((None, 2, half, window), lambda i, f: (i, 0, 0, 0))]
            shapes = [shape(count, 2, half, window)]
        else:
            specs = [pl.BlockSpec((None, None, half, window), lambda i, f: (i, 0, 0, 0))] * 2
            shapes = [shape(count, 1, half, window)] * 2
        outs = call(
            functools.partial(first_kernel, joint),
            info,
            (count,),
            [
                pl.BlockSpec((window, window), lambda i, f: (slot_of(begin + i, f), 0)),
                whole((window, window)),
                pl.BlockSpec((2, half, window), lambda i, f: (place - i, 0, 0)),
                whole((half, window)),
            ],
            specs + [whole((half, window))],
            shapes + [shape(half, window)],
            [pltpu.VMEM((window, window), bf)] * 2 + [pltpu.VMEM((half, window), f32)],
            (seg, own_first, factor, prev_top),
            after=[*last[-1:], *after],
            opens=opens,
        )
        return outs[:-1], outs[-1]

    def exchange(batch, sends):
        down, up = [], []
        for p, c in everyone:
            places = [fold * (c // group) + fold - 1 - t for t in batch]
            tiles = [at * planes + p for at in places if at >= 0]
            if any(tile <= c and tile < cols - 1 for tile in tiles):
                down.append(((p, c), ((p + 1) % planes, c)))
            if any((tile if p else tile + planes) <= c for tile in tiles):
                up.append(((p, c), ((p - 1) % planes, c)))
        if len(sends) == 1:
            return [send(sends[0], sorted(set(down + up)))]
        return [send(sends[0], down), send(sends[1], up)]

    def second_step(batch, size, at, sends, gots, held, ended, after, opens):
        count, begin = len(batch), batch[0]
        hop, place = begin // fold, fold - 1 - begin % fold
        inner = lambda i: jnp.minimum(i, count - 1)
        piece = lambda k: pl.BlockSpec((None, None, half, window), lambda i, f: (inner(i), k, 0, 0))
        pieces = [piece(0), piece(len(sends) % 2)]
        ends = [pl.BlockSpec((2, half, half), lambda i, f: (at + i, 0, 0))] * 2
        extra = [whole((half, window))] if ended else [pl.BlockSpec(memory_space=pl.ANY)] * len(held)
        return call(
            functools.partial(second_kernel, begin, count, bool(ended)),
            info,
            (count + len(ended),),
            [pl.BlockSpec((2, None, half, window), lambda i, f: (place - inner(i), hop, 0, 0))] + pieces + pieces + extra,
            ends,
            [shape(2 * size, half, half)] * 2,
            [],
            (second_factors, sends[0], sends[-1], gots[0], gots[-1], *ended, *held),
            {6 + k: k for k in range(len(held))},
            [*last[-1:], *after],
            opens,
        )

    split_scratch = [pltpu.VMEM((window, half), bf)] * 4

    counts = (above_rows.shape[0], basis_rows.shape[0])
    deep = window if all(n % window == 0 for n in counts) else half
    above_blocks, basis_blocks = (n // deep for n in counts)

    def rows_step(after=(), opens=False):
        tall = pl.BlockSpec((deep, half), lambda i, f: (i, 0))
        blocks = above_blocks + basis_blocks
        return call(
            functools.partial(rows_kernel, above_blocks),
            info,
            (blocks,),
            [
                pl.BlockSpec((deep, window), lambda i, f: (jnp.minimum(i, above_blocks - 1), 0)),
                pl.BlockSpec((deep, window), lambda i, f: (jnp.maximum(i - above_blocks, 0), 0)),
                whole((window, window)),
            ],
            [tall] * 2,
            [shape(blocks * deep, half)] * 2,
            [pltpu.VMEM((window, window), bf)] * 2,
            (above_rows, basis_rows, own_first),
            after=[*last[-1:], *after],
            opens=opens,
        )

    def rows_end(first, blocks, parts):
        tall = pl.BlockSpec((deep, half), lambda i, f: (first + i, 0))
        return call(
            rows_end_kernel,
            info,
            (blocks,),
            [tall] * 4 + [whole((window, half))] * 2,
            pl.BlockSpec((deep, window), lambda i, f: (i, 0)),
            shape(blocks * deep, window),
            split_scratch,
            (*parts, prev, cur),
            after=last[-1:],
        )

    lefts, rights, ups, downs = ([None] * slots for _ in range(4))

    def third_step(batch, held, after, opens):
        begin = batch[0]
        fresh = held is None
        parts = [lefts[begin], rights[begin]]
        parts.append(ups[begin - fold] if begin >= fold else (no_strips, 0))
        parts += [ups[begin], downs[begin], downs[(begin + fold) % slots]]
        piece = lambda at: pl.BlockSpec((None, half, half), lambda e, h, f: (2 * (at + e) + h, 0, 0))

        def out_block(e, h, f):
            slot = slot_of(begin + e, f)
            upper = lax.rem(slot + f[PLANE0], slots)
            return (jnp.where(h == 0, 2 * slot + 1, 2 * upper), 0)

        args = [array for array, _ in parts]
        ending = slots - fold in batch
        tail_row = 2 * ending_strips[2] if ending else 0
        return call(
            functools.partial(third_kernel, begin, slots - fold),
            info,
            (len(batch), 2),
            [piece(at) for _, at in parts]
            + [pl.BlockSpec((None, half, half), lambda e, h, f: (tail_row, 0, 0))]
            + [whole((window, half))] * 2
            + [pl.BlockSpec(memory_space=pl.ANY)],
            pl.BlockSpec((half, window), out_block),
            shape(*seg.shape),
            split_scratch,
            (*args, ending_strips[1] if ending else args[0], prev, cur, args[0] if fresh else held),
            None if fresh else {10: 0},
            [*last[-1:], *after],
            opens,
        )

    def last_step(held):
        quarter = lambda at: pl.BlockSpec((None, half, half), lambda i, f: (at, 0, 0))
        array, at = ups[slots - fold]

        def out_block(i, f):
            return (jnp.where((f[LAST_LEVEL] == 1) & (f[PLANE0] == 1), 0, 2 * slot_of(slots - 1, f) + 1), 0)

        return call(
            last_kernel,
            info,
            (1,),
            [whole((half, window)), quarter(2 * at + 1)] + [quarter(2 * ending_strips[2])] * 2
            + [whole((window, half))] * 2
            + [pl.BlockSpec(memory_space=pl.ANY)],
            pl.BlockSpec((half, window), out_block),
            shape(*seg.shape),
            split_scratch,
            (tops[-1], array, *ending_strips[:2], prev, cur, held),
            {7: 0},
            last[-1:],
        )

    tops, sent, got, made = [jnp.zeros((half, window), f32)], {}, {}, {}
    no_strips = jnp.zeros((2 * slots, half, half), f32)

    def do_first(batch, after=(), opens=False):
        sent[batch[0]], top = first_step(batch, tops[-1], paired and batch[0] > 0, after, opens)
        tops.append(top)
        last.append(top)
        got[batch[0]] = exchange(batch, sent[batch[0]])

    def do_second(batch, strip, ended=(), after=(), opens=False):
        begin = batch[0]
        held = made.get(strip[0], ())
        made[strip[0]] = second_step(
            batch, len(strip) + len(ended), begin - strip[0], sent[begin], got[begin], held, ended, after, opens
        )
        last.append(made[strip[0]][0])
        if batch[-1] == strip[-1]:
            left, right = made[strip[0]]
            up, down = along(right, 1), along(left, -1)
            for place, t in enumerate(strip):
                lefts[t], rights[t] = (left, place), (right, place)
                ups[t], downs[t] = (up, place), (down, place)
            return up, down, len(strip)

    out = [None]

    def do_third(batch, after=(), opens=False):
        out[0] = third_step(batch, out[0], after, opens)
        last.append(out[0])

    def do_last():
        out[0] = last_step(out[0])
        last.append(out[0])

    def do_rows():
        left, right = rows_step(opens=True)
        last.append(left)
        return left, right, along(right, 1), along(left, -1)

    def do_rows_end():
        for first, blocks in ((0, above_blocks), (above_blocks, basis_blocks)):
            row_ends.append(rows_end(first, blocks, parts))
            last.append(row_ends[-1])

    row_ends = []
    if paired and fold == 4 and levels == 2:
        do_first([0])
        parts = do_rows()
        do_first([1], [came_prev, *got[0]])
        do_first([2, 3], opens=True)
        do_first([4, 5], got[1], opens=True)
        second_factors = gather_second()
        do_first([6, 7], [*got[2], *parts[2:]], opens=True)
        for batch in ([0], [1], [2, 3]):
            do_second(batch, [0, 1, 2, 3])
        ending_strips = do_second([4, 5], [4, 5], ended=[tops[-1]], opens=True)
        do_rows_end()
        do_second([6, 7], [6, 7], after=[*ups[0][:1], *downs[0][:1]])
        do_third([0, 1], opens=True)
        do_third([4, 5])
        do_last()
        do_third([2, 3])
        do_third([6, 7])
    else:
        parts = do_rows()
        for t in range(slots):
            do_first([t])
        if paired:
            second_factors = gather_second()
        for t in range(slots):
            ending_strips = do_second([t], [t], ended=[tops[-1]] if t == slots - 1 else ())
        for t in range(slots - 1):
            do_third([t])
        do_last()
        do_third([slots - 1])
        do_rows_end()
    return (out[0].reshape(segment.shape), *row_ends)


def solution(mesh):
    placed = (
        P(None, "prow", None, "pcol"),
        P("prow", "pcol"),
        P("prow", "pcol"),
        P(None, "pcol", None, None),
        P(),
    )
    return jax.shard_map(
        body,
        mesh=mesh,
        in_specs=placed,
        out_specs=(P(None, "prow", None, "pcol"), P("prow", "pcol"), P("prow", "pcol")),
        check_vma=False,
    )
```

time: 731 us -> 331 us (0.45)
  waiting for transfers between devices: 482 us -> 135 us
  Pallas kernels: 0 us -> 121 us
  matrix products: 101 us -> 0 us
  local copies, waits for them, and re-layouts: 69.5 us -> 6.34 us
  starting transfers between devices: 10.6 us -> 46.4 us
  other arithmetic: 34.7 us -> 1.95 us
  between operations: 26.3 us -> 14 us
    psum x1 -> x0, waiting for transfers between devices: 274 us -> none  [spread(): return lax.psum(block, axis)]
    ppermute x5 -> x18, waiting for transfers between devices: 208 us -> 59.7 us  [send(): lax.ppermute(value, GRID, [(a * cols + b, c * cols + d) for (a, b), (c, d...]
    pallas_call x0 -> x20, Pallas kernels: none -> 121 us  [call(): pl.pallas_call(run, grid_spec=pltpu.PrefetchScalarGridSpec(num_scalar_pre...]
    dot_general x10 -> x0, matrix products: 101 us -> none  [the longest x5 60.1 us: product(): jnp.dot(left, right, precision=HIGHEST, preferred_element_type=jnp.float32)]
    all_gather x0 -> x3, waiting for transfers between devices: none -> 75.1 us  [the longest x2 49.8 us: body(): lax.all_gather(v, 'pcol', axis_index_groups=teams)]
    ppermute x5 -> x18, starting transfers between devices: 10.5 us -> 46.3 us  [send(): lax.ppermute(value, GRID, [(a * cols + b, c * cols + d) for (a, b), (c, d...]
    unnamed x74 -> x6, local copies, waits for them, and re-layouts: 30.4 us -> 0.98 us
    slice x10 -> x0, local copies, waits for them, and re-layouts: 25.3 us -> none  [the longest x1 8.17 us: body(): bottoms = blocks[:, half_width:]]
  transfers between devices with their start and end apart: 6 -> 21, of which waited for: 5 -> 10; matrix products, arithmetic and copies ran while one was open for 15% -> 2% of each run, Pallas kernels for 0% -> 34%
where the time goes in v1:
time: 331 us; the launch traced here: 325 us
  waiting for transfers between devices  135 us (41%)
  Pallas kernels  121 us (37%)
  starting transfers between devices  46.4 us (14%)
  between operations  14 us (4%)
  local copies, waits for them, and re-layouts  6.34 us (2%)
    pallas_call x20, Pallas kernels, call(): pl.pallas_call(run, grid_spec=pltpu.PrefetchScalarGridSpec(num_scalar_pre...  121 us
    ppermute x18, waiting for transfers between devices, send(): lax.ppermute(value, GRID, [(a * cols + b, c * cols + d) for (a, b), (c, d...  59.7 us
    all_gather x2, waiting for transfers between devices, body(): lax.all_gather(v, 'pcol', axis_index_groups=teams)  49.8 us
    ppermute x18, starting transfers between devices, send(): lax.ppermute(value, GRID, [(a * cols + b, c * cols + d) for (a, b), (c, d...  46.3 us
    all_gather x1, waiting for transfers between devices, gather_second(): return lax.all_gather(out, 'pcol', axis_index_groups=teams)  25.3 us
  transfers between devices with their start and end apart: 21, of which 10 were waited for; matrix products, arithmetic and copies ran while one was open for 2% of the time, Pallas kernels for 34%

profile of v1, /device:TPU:25, one launch (start us, length us, event | category | flops | bytes accessed | tf_op | source)
XLA Modules:
  0.0 324.9 jit_solution(8748809935783766348)
XLA Ops:
  7.2 0.0 all-gather.9.cloned.1.call-start
  7.2 1.3 slice_bitcast_fusion
  8.5 1.3 collective-permute-start
  9.9 0.1 reshape.15
  10.0 0.7 concatenate.3.refs_0_
  10.6 2.5 collective-permute-done.refs_2_
  13.1 1.0 copy-done.1
  14.0 4.9 %shard_map.76 = (f32[512,512]{1,0:T(8,128)}, f32[2,256,512]{2,1,0:T(8,128)}, f32[256,512]{1,0:T(8,128)}, f32[256,512]{1,0:T(8,128)}, f32[512,256]{1,0:T(8,128)}, /*index=5*/f32[512,256]{1,0:T(8,128)}) custom-call(s32[43]{0:T(128)} %concatenate.3.refs_0_, f32[2,1,512,512]{3,2,1,0:T(8,128)} %refs_1_.2, f32[512,512]{1,0:T(8,128)} %copy-done.1), custom_call_target="tpu_custom_call" | custom-call | flops 1 | bytes 1 | tf_op jit(solution)/shard_map/pallas_call | solution.py:35
  18.9 0.0 all-gather.9.cloned.1.call-update
  19.0 0.0 all-gather.7.cloned.1.call-start
  19.0 1.3 collective-permute-start.2
  20.3 0.9 broadcast_in_dim.6.refs_4_
  21.2 5.6 %shard_map.77 = (f32[1,1,256,512]{3,2,1,0:T(8,128)}, f32[1,1,256,512]{3,2,1,0:T(8,128)}, f32[256,512]{1,0:T(8,128)}) custom-call(s32[43]{0:T(128)} %concatenate.3.refs_0_, f32[4096,512]{1,0:T(8,128)} %bitcast.26, f32[512,512]{1,0:T(8,128)} %get-tuple-element.33.refs_2_.refs_3_, f32[2,256,512]{2,1,0:T(8,128)} %get-tuple-element.35.refs_3_, ...), custom_call_target="tpu_custom_call" | custom-call | flops 1 | bytes 1 | tf_op jit(solution)/shard_map/pallas_call | solution.py:35
  26.7 1.5 collective-permute-start.4
  28.2 1.5 collective-permute-start.5
  29.7 6.5 %collective-permute-start.3 = (f32[512,256]{1,0:T(8,128)}, f32[512,256]{1,0:T(8,128)}, u32[]{:S(2)}, u32[]{:S(2)}) collective-permute-start(f32[512,256]{1,0:T(8,128)} %get-tuple-element.38), channel_id=1, source_target_pairs={{0,1},{1,2},{2,3},{3,4},{4,5},{5,6},{6,7},{7,8},{8,9},{9,10},{10,1... | collective-permute-start | bytes 1572872 | tf_op jit(solution)/shard_map/ppermute | solution.py:228
  36.1 1.3 collective-permute-start.1
  37.4 8.4 %shard_map.78 = (f32[2048,256]{1,0:T(8,128)}, f32[2048,256]{1,0:T(8,128)}) custom-call(s32[43]{0:T(128)} %concatenate.3.refs_0_, f32[1024,512]{1,0:T(8,128)} %refs_1_.3, f32[1024,512]{1,0:T(8,128)} %refs_2_.1, f32[512,512]{1,0:T(8,128)} %get-tuple-element.33.refs_2_.refs_3_, f32[256,512]{1,0:T(8,128)} %get-tuple-element.36.refs_4_), custom_call_target="tpu_custom_call" | custom-call | flops 100000000376832 | bytes 1 | tf_op jit(solution)/shard_map/pallas_call | solution.py:35
  45.8 6.5 %collective-permute-done.2 = f32[256,512]{1,0:T(8,128)} collective-permute-done((f32[256,512]{1,0:T(8,128)}, f32[256,512]{1,0:T(8,128)}, u32[]{:S(2)}, u32[]{:S(2)}) %collective-permute-start.2) | collective-permute-done | bytes 524320 | tf_op jit(solution)/shard_map/ppermute | solution.py:228
  52.3 1.9 collective-permute-start.8
  54.3 0.0 all-gather.7.cloned.1.call-update
  54.3 0.0 all-gather.11.cloned.1.call-start
  54.3 2.5 collective-permute-start.9
  56.9 0.0 collective-permute-done.5.refs_8_.refs_5_
  56.9 12.5 %all-gather.9.cloned.1.call-done = f32[2048,512]{1,0:T(8,128)} async-done(((f32[256,512]{1,0:T(8,128)}), f32[2048,512]{1,0:T(8,128)}) %all-gather.9.cloned.1.call-update) | async-done | bytes 4194320 | tf_op jit(solution)/shard_map/all_gather | solution.py:274
  69.4 5.6 %shard_map.79 = (f32[1,2,256,512]{3,2,1,0:T(8,128)}, f32[256,512]{1,0:T(8,128)}) custom-call(s32[43]{0:T(128)} %concatenate.3.refs_0_, f32[4096,512]{1,0:T(8,128)} %bitcast.27, f32[512,512]{1,0:T(8,128)} %get-tuple-element.33.refs_2_.refs_3_, f32[8,256,512]{2,1,0:T(8,128)} %bitcast.31, f32[256,512]{1,0:T(8,128)} %get-tuple-element.36.refs_4_, ...), custom_call_target="tpu_custom_call" | custom-call | flops 1 | bytes 1 | tf_op jit(solution)/shard_map/pallas_call | solution.py:35
  75.0 2.8 collective-permute-start.6
  77.7 7.8 %shard_map.80 = (f32[2,2,256,512]{3,2,1,0:T(8,128)}, f32[256,512]{1,0:T(8,128)}) custom-call(s32[43]{0:T(128)} %concatenate.3.refs_0_, f32[4096,512]{1,0:T(8,128)} %bitcast.28, f32[512,512]{1,0:T(8,128)} %get-tuple-element.33.refs_2_.refs_3_, f32[8,256,512]{2,1,0:T(8,128)} %bitcast.32, f32[256,512]{1,0:T(8,128)} %get-tuple-element.41.refs_4_), custom_call_target="tpu_custom_call" | custom-call | flops 100000000376832 | bytes 1 | tf_op jit(solution)/shard_map/pallas_call | solution.py:35
  85.5 2.5 collective-permute-start.7
  88.0 37.3 %all-gather.7.cloned.1.call-done = f32[2048,512]{1,0:T(8,128)} async-done(((f32[256,512]{1,0:T(8,128)}), f32[2048,512]{1,0:T(8,128)}) %all-gather.7.cloned.1.call-update) | async-done | bytes 4194320 | tf_op jit(solution)/shard_map/all_gather | solution.py:274
  125.3 0.0 collective-permute-done.6.refs_5_.refs_4_
  125.3 7.7 %shard_map.81 = (f32[2,2,256,512]{3,2,1,0:T(8,128)}, f32[256,512]{1,0:T(8,128)}) custom-call(s32[43]{0:T(128)} %concatenate.3.refs_0_, f32[4096,512]{1,0:T(8,128)} %bitcast.29, f32[512,512]{1,0:T(8,128)} %get-tuple-element.33.refs_2_.refs_3_, f32[8,256,512]{2,1,0:T(8,128)} %bitcast.33, f32[256,512]{1,0:T(8,128)} %get-tuple-element.42.refs_4_, ...), custom_call_target="tpu_custom_call" | custom-call | flops 100000000376832 | bytes 1 | tf_op jit(solution)/shard_map/pallas_call | solution.py:35
  133.1 0.0 collective-permute-done.1.refs_2_
  133.1 2.9 shard_map.82.refs_5_
  136.0 0.0 all-gather.11.cloned.1.call-update
  136.0 3.1 collective-permute-start.11
  139.1 6.2 %collective-permute-done.7.refs_6_.refs_4_.refs_5_ = f32[2,2,256,512]{3,2,1,0:T(8,128)} collective-permute-done((f32[2,2,256,512]{3,2,1,0:T(8,128)}, f32[2,2,256,512]{3,2,1,0:T(8,128)}, u32[]{:S(2)}, u32[]{:S(2)}) %collective-permute-start.7) | collective-permute-done | bytes 2097184 | tf_op jit(solution)/shard_map/ppermute | solution.py:228
  145.3 7.9 %shard_map.83 = (f32[2,2,256,512]{3,2,1,0:T(8,128)}, f32[256,512]{1,0:T(8,128)}) custom-call(s32[43]{0:T(128)} %concatenate.3.refs_0_, f32[4096,512]{1,0:T(8,128)} %bitcast.30, f32[512,512]{1,0:T(8,128)} %get-tuple-element.33.refs_2_.refs_3_, f32[8,256,512]{2,1,0:T(8,128)} %bitcast.34, f32[256,512]{1,0:T(8,128)} %get-tuple-element.44.refs_3_.refs_4_, ...), custom_call_target="tpu_custom_call" | custom-call | flops 100000000376832 | bytes 1 | tf_op jit(solution)/shard_map/pallas_call | solution.py:35
  153.2 4.1 %collective-permute-start.10 = (f32[2,2,256,512]{3,2,1,0:T(8,128)}, f32[2,2,256,512]{3,2,1,0:T(8,128)}, u32[]{:S(2)}, u32[]{:S(2)}) collective-permute-start(f32[2,2,256,512]{3,2,1,0:T(8,128)} %get-tuple-element.47.refs_2_.refs_3_), channel_id=1, source_target_pairs={{8,24},{9,25},{10,26},{11,27},{12,28},{13,29},{14,30},{15,31},{24,... | collective-permute-start | bytes 6291464 | tf_op jit(solution)/shard_map/ppermute | solution.py:228
  157.3 25.3 %all-gather.11.cloned.1.call-done = f32[16,256,512]{2,1,0:T(8,128)} async-done(((f32[2,256,512]{2,1,0:T(8,128)}), f32[16,256,512]{2,1,0:T(8,128)}) %all-gather.11.cloned.1.call-update) | async-done | bytes 8388624 | tf_op jit(solution)/shard_map/all_gather | solution.py:299
  182.7 4.5 %shard_map.84 = (f32[8,256,256]{2,1,0:T(8,128)}, f32[8,256,256]{2,1,0:T(8,128)}) custom-call(s32[43]{0:T(128)} %concatenate.3.refs_0_, f32[8,2,256,512]{3,2,1,0:T(8,128)} %bitcast.20, f32[1,1,256,512]{3,2,1,0:T(8,128)} %get-tuple-element.39.refs_2_, f32[1,1,256,512]{3,2,1,0:T(8,128)} %get-tuple-element.40.refs_3_, ...), custom_call_target="tpu_custom_call" | custom-call | flops 1 | bytes 1 | tf_op jit(solution)/shard_map/pallas_call | solution.py:35
  187.2 4.5 %shard_map.85 = (f32[8,256,256]{2,1,0:T(8,128)}, f32[8,256,256]{2,1,0:T(8,128)}) custom-call(s32[43]{0:T(128)} %concatenate.3.refs_0_, f32[8,2,256,512]{3,2,1,0:T(8,128)} %bitcast.21, f32[1,2,256,512]{3,2,1,0:T(8,128)} %get-tuple-element.43.refs_2_.refs_3_, ...), custom_call_target="tpu_custom_call", output_to_operand_aliasing={{0}: (6, {}), {1}: (7, {})} | custom-call | flops 1 | bytes 1 | tf_op jit(solution)/shard_map/pallas_call | solution.py:35
  191.7 5.6 %shard_map.86 = (f32[8,256,256]{2,1,0:T(8,128)}, f32[8,256,256]{2,1,0:T(8,128)}) custom-call(s32[43]{0:T(128)} %concatenate.3.refs_0_, f32[8,2,256,512]{3,2,1,0:T(8,128)} %bitcast.22, f32[2,2,256,512]{3,2,1,0:T(8,128)} %get-tuple-element.45.refs_2_.refs_3_, ...), custom_call_target="tpu_custom_call", output_to_operand_aliasing={{0}: (6, {}), {1}: (7, {})} | custom-call | flops 1 | bytes 1 | tf_op jit(solution)/shard_map/pallas_call | solution.py:35
  197.3 2.8 collective-permute-start.12
  200.0 1.9 collective-permute-start.13
  201.9 6.1 %shard_map.87 = (f32[6,256,256]{2,1,0:T(8,128)}, f32[6,256,256]{2,1,0:T(8,128)}) custom-call(s32[43]{0:T(128)} %concatenate.3.refs_0_, f32[8,2,256,512]{3,2,1,0:T(8,128)} %bitcast.23, f32[2,2,256,512]{3,2,1,0:T(8,128)} %get-tuple-element.49.refs_2_.refs_3_, f32[2,2,256,512]{3,2,1,0:T(8,128)} %get-tuple-element.49.refs_2_.refs_3_, ...), custom_call_target="tpu_custom_call" | custom-call | flops 100000000376832 | bytes 1 | tf_op jit(solution)/shard_map/pallas_call | solution.py:35
  208.0 3.9 %collective-permute-start.17 = (f32[6,256,256]{2,1,0:T(8,128)}, f32[6,256,256]{2,1,0:T(8,128)S(1)}, u32[]{:S(2)}, u32[]{:S(2)}) collective-permute-start(f32[6,256,256]{2,1,0:T(8,128)} %get-tuple-element.56.refs_7_.refs_1_), channel_id=1, source_target_pairs={{1,0},{2,1},{3,2},{4,3},{5,4},{6,5},{7,6},{8,7},{9,8},{10,9},{11,1... | collective-permute-start | bytes 4718600 | tf_op jit(solution)/shard_map/ppermute | solution.py:228
  212.0 1.9 convert_select_fusion.refs_5_.refs_8_
  213.9 6.0 %shard_map.88.refs_7_ = f32[1024,512]{1,0:T(8,128)} custom-call(s32[43]{0:T(128)} %concatenate.3.refs_0_, f32[2048,256]{1,0:T(8,128)} %get-tuple-element.37.refs_5_.refs_1_, f32[2048,256]{1,0:T(8,128)} %get-tuple-element.46.refs_2_, f32[2048,256]{1,0:T(8,128)} %collective-permute-done.8.refs_7_.refs_3_, f32[2048,256]{1,0:T(8,128)} %collective-permute-done.9.refs_8_.refs_4_, ...), custom_call_target="tpu_custom_call" | custom-call | flops 1 | bytes 1 | tf_op jit(solution)/shard_map/pallas_call | solution.py:35
  219.9 1.9 collective-permute-start.16
  221.8 6.0 %shard_map.89.refs_6_ = f32[1024,512]{1,0:T(8,128)} custom-call(s32[43]{0:T(128)} %concatenate.3.refs_0_, f32[2048,256]{1,0:T(8,128)} %get-tuple-element.37.refs_5_.refs_1_, f32[2048,256]{1,0:T(8,128)} %get-tuple-element.46.refs_2_, f32[2048,256]{1,0:T(8,128)} %collective-permute-done.8.refs_7_.refs_3_, f32[2048,256]{1,0:T(8,128)} %collective-permute-done.9.refs_8_.refs_4_, ...), custom_call_target="tpu_custom_call" | custom-call | flops 1 | bytes 1 | tf_op jit(solution)/shard_map/pallas_call | solution.py:35
  227.9 7.3 %collective-permute-done.10.refs_4_.refs_5_ = f32[2,2,256,512]{3,2,1,0:T(8,128)} collective-permute-done((f32[2,2,256,512]{3,2,1,0:T(8,128)}, f32[2,2,256,512]{3,2,1,0:T(8,128)}, u32[]{:S(2)}, u32[]{:S(2)}) %collective-permute-start.10) | collective-permute-done | bytes 2097184 | tf_op jit(solution)/shard_map/ppermute | solution.py:228
  235.2 29.5 %collective-permute-done.13.refs_8_.refs_5_.refs_6_ = f32[8,256,256]{2,1,0:T(8,128)} collective-permute-done((f32[8,256,256]{2,1,0:T(8,128)}, f32[8,256,256]{2,1,0:T(8,128)}, u32[]{:S(2)}, u32[]{:S(2)}) %collective-permute-start.13) | collective-permute-done | bytes 2097184 | tf_op jit(solution)/shard_map/ppermute | solution.py:228
  264.7 5.6 %shard_map.90 = (f32[4,256,256]{2,1,0:T(8,128)}, f32[4,256,256]{2,1,0:T(8,128)}) custom-call(s32[43]{0:T(128)} %concatenate.3.refs_0_, f32[8,2,256,512]{3,2,1,0:T(8,128)} %bitcast.24, f32[2,2,256,512]{3,2,1,0:T(8,128)} %get-tuple-element.47.refs_2_.refs_3_, f32[2,2,256,512]{3,2,1,0:T(8,128)} %get-tuple-element.47.refs_2_.refs_3_, ...), custom_call_target="tpu_custom_call" | custom-call | flops 1 | bytes 1 | tf_op jit(solution)/shard_map/pallas_call | solution.py:35
  270.2 1.9 collective-permute-start.15
  272.2 3.6 %collective-permute-start.14 = (f32[4,256,256]{2,1,0:T(8,128)}, f32[4,256,256]{2,1,0:T(8,128)}, u32[]{:S(2)}, u32[]{:S(2)}) collective-permute-start(f32[4,256,256]{2,1,0:T(8,128)} %get-tuple-element.59.refs_2_), channel_id=1, source_target_pairs={{0,1},{1,2},{2,3},{3,4},{4,5},{5,6},{6,7},{7,8},{8,9},{9,10},{10,1... | collective-permute-start | bytes 3145736 | tf_op jit(solution)/shard_map/ppermute | solution.py:228
  275.8 5.6 %collective-permute-done.17.refs_6_.refs_5_.refs_7_.refs_4_ = f32[6,256,256]{2,1,0:T(8,128)S(1)} collective-permute-done((f32[6,256,256]{2,1,0:T(8,128)}, f32[6,256,256]{2,1,0:T(8,128)S(1)}, u32[]{:S(2)}, u32[]{:S(2)}) %collective-permute-start.17) | collective-permute-done | bytes 1572896 | tf_op jit(solution)/shard_map/ppermute | solution.py:228
  281.4 2.5 broadcast_in_dim.7.refs_3_
  283.9 7.3 %shard_map.91.refs_10_ = f32[4096,512]{1,0:T(8,128)} custom-call(s32[43]{0:T(128)} %concatenate.3.refs_0_, f32[8,256,256]{2,1,0:T(8,128)} %get-tuple-element.55.refs_7_.refs_1_.refs_10_, f32[8,256,256]{2,1,0:T(8,128)} %get-tuple-element.57.refs_2_, f32[16,256,256]{2,1,0:T(8,128)} %broadcast_in_dim.7.refs_3_, ...), custom_call_target="tpu_custom_call" | custom-call | flops 100000000376832 | bytes 1 | tf_op jit(solution)/shard_map/pallas_call | solution.py:35
  291.2 7.1 %shard_map.92.refs_7_ = f32[4096,512]{1,0:T(8,128)} custom-call(s32[43]{0:T(128)} %concatenate.3.refs_0_, f32[6,256,256]{2,1,0:T(8,128)} %get-tuple-element.56.refs_7_.refs_1_, f32[6,256,256]{2,1,0:T(8,128)} %get-tuple-element.60.refs_2_, f32[8,256,256]{2,1,0:T(8,128)} %collective-permute-done.12.refs_7_.refs_4_.refs_3_, ...), custom_call_target="tpu_custom_call", output_to_operand_aliasing={{}: (10, {})} | custom-call | flops 1 | bytes 1 | tf_op jit(solution)/shard_map/pallas_call | solution.py:35
  298.3 3.7 %shard_map.93.refs_10_ = f32[4096,512]{1,0:T(8,128)} custom-call(s32[43]{0:T(128)} %concatenate.3.refs_0_, f32[256,512]{1,0:T(8,128)} %get-tuple-element.50.refs_6_.refs_1_, f32[6,256,256]{2,1,0:T(8,128)} %collective-permute-done.16.refs_4_.refs_2_.refs_3_, ...), custom_call_target="tpu_custom_call", output_to_operand_aliasing={{}: (7, {})} | custom-call | flops 1 | bytes 1 | tf_op jit(solution)/shard_map/pallas_call | solution.py:35
  301.9 2.1 collective-permute-done.15.refs_6_.refs_5_
  304.0 7.1 %shard_map.94.refs_10_ = f32[4096,512]{1,0:T(8,128)} custom-call(s32[43]{0:T(128)} %concatenate.3.refs_0_, f32[8,256,256]{2,1,0:T(8,128)} %get-tuple-element.55.refs_7_.refs_1_.refs_10_, f32[8,256,256]{2,1,0:T(8,128)} %get-tuple-element.57.refs_2_, f32[16,256,256]{2,1,0:T(8,128)} %broadcast_in_dim.7.refs_3_, ...), custom_call_target="tpu_custom_call", output_to_operand_aliasing={{}: (10, {})} | custom-call | flops 1 | bytes 1 | tf_op jit(solution)/shard_map/pallas_call | solution.py:35
  311.1 7.3 %shard_map.95 = f32[4096,512]{1,0:T(8,128)} custom-call(s32[43]{0:T(128)} %concatenate.3.refs_0_, f32[4,256,256]{2,1,0:T(8,128)} %get-tuple-element.58.refs_11_.refs_1_.refs_7_, f32[4,256,256]{2,1,0:T(8,128)} %get-tuple-element.59.refs_2_, f32[8,256,256]{2,1,0:T(8,128)} %collective-permute-done.12.refs_7_.refs_4_.refs_3_, ...), custom_call_target="tpu_custom_call", output_to_operand_aliasing={{}: (10, {})} | custom-call | flops 1 | bytes 1 | tf_op jit(solution)/shard_map/pallas_call | solution.py:35
  (14 shorter events, 0.0 us)
Async XLA Ops:
  7.2 2.7 copy-start.2
  7.2 62.2 %all-gather.9.cloned.1.call-start = ((), (), s32[]{:S(2)}) async-start(), calls=%async_computation.1 | async-start | bytes 4718592 | tf_op jit(solution)/shard_map/all_gather | solution.py:274
  8.5 4.6 %collective-permute-start = (f32[512,512]{1,0:T(8,128)S(1)}, f32[512,512]{1,0:T(8,128)S(1)}, u32[]{:S(2)}, u32[]{:S(2)}) collective-permute-start(f32[512,512]{1,0:T(8,128)S(1)} %slice_bitcast_fusion), channel_id=1, source_target_pairs={{0,1},{2,3},{4,5},{6,7},{8,9},{10,11},{12,13},{14,15},{17,16},{19,... | collective-permute-start | bytes 3145736 | tf_op jit(solution)/shard_map/ppermute | solution.py:228
  13.1 1.0 copy-start.1
  19.0 106.4 %all-gather.7.cloned.1.call-start = ((), (), s32[]{:S(2)}) async-start(), calls=%async_computation | async-start | bytes 4718592 | tf_op jit(solution)/shard_map/all_gather | solution.py:274
  19.0 33.3 %collective-permute-start.2 = (f32[256,512]{1,0:T(8,128)}, f32[256,512]{1,0:T(8,128)}, u32[]{:S(2)}, u32[]{:S(2)}) collective-permute-start(f32[256,512]{1,0:T(8,128)} %get-tuple-element.34), channel_id=1, source_target_pairs={{0,8},{1,9},{2,10},{3,11},{4,12},{5,13},{6,14},{7,15},{16,24},{17,... | collective-permute-start | bytes 1572872 | tf_op jit(solution)/shard_map/ppermute | solution.py:228
  26.7 27.6 %collective-permute-start.4 = (f32[1,1,256,512]{3,2,1,0:T(8,128)}, f32[1,1,256,512]{3,2,1,0:T(8,128)}, u32[]{:S(2)}, u32[]{:S(2)}) collective-permute-start(f32[1,1,256,512]{3,2,1,0:T(8,128)} %get-tuple-element.39.refs_2_), channel_id=1, source_target_pairs={{6,22},{7,23},{14,30},{15,31},{23,7}} | collective-permute-start | bytes 1572872 | tf_op jit(solution)/shard_map/ppermute | solution.py:228
  28.2 28.7 %collective-permute-start.5 = (f32[1,1,256,512]{3,2,1,0:T(8,128)}, f32[1,1,256,512]{3,2,1,0:T(8,128)}, u32[]{:S(2)}, u32[]{:S(2)}) collective-permute-start(f32[1,1,256,512]{3,2,1,0:T(8,128)} %get-tuple-element.40.refs_3_), channel_id=1, source_target_pairs={{23,7},{31,15}} | collective-permute-start | bytes 1572872 | tf_op jit(solution)/shard_map/ppermute | solution.py:228
  29.7 27.2 %collective-permute-start.3 = (f32[512,256]{1,0:T(8,128)}, f32[512,256]{1,0:T(8,128)}, u32[]{:S(2)}, u32[]{:S(2)}) collective-permute-start(f32[512,256]{1,0:T(8,128)} %get-tuple-element.38), channel_id=1, source_target_pairs={{0,1},{1,2},{2,3},{3,4},{4,5},{5,6},{6,7},{7,8},{8,9},{9,10},{10,1... | collective-permute-start | bytes 1572872 | tf_op jit(solution)/shard_map/ppermute | solution.py:228
  36.1 96.9 %collective-permute-start.1 = (f32[256,512]{1,0:T(8,128)}, f32[256,512]{1,0:T(8,128)}, u32[]{:S(2)}, u32[]{:S(2)}) collective-permute-start(f32[256,512]{1,0:T(8,128)} %get-tuple-element.32.refs_1_), channel_id=1, source_target_pairs={{0,8},{1,9},{2,10},{3,11},{4,12},{5,13},{6,14},{7,15},{16,24},{17,... | collective-permute-start | bytes 1572872 | tf_op jit(solution)/shard_map/ppermute | solution.py:228
  52.3 86.8 %collective-permute-start.8 = (f32[2048,256]{1,0:T(8,128)}, f32[2048,256]{1,0:T(8,128)}, u32[]{:S(2)}, u32[]{:S(2)}) collective-permute-start(f32[2048,256]{1,0:T(8,128)} %get-tuple-element.46.refs_2_), channel_id=1, source_target_pairs={{0,1},{1,2},{2,3},{3,4},{4,5},{5,6},{6,7},{7,8},{8,9},{9,10},{10,1... | collective-permute-start | bytes 6291464 | tf_op jit(solution)/shard_map/ppermute | solution.py:228
  54.3 128.4 %all-gather.11.cloned.1.call-start = ((), (), s32[]{:S(2)}) async-start(), calls=%async_computation.2 | async-start | bytes 9437184 | tf_op jit(solution)/shard_map/all_gather | solution.py:299
  54.3 84.8 %collective-permute-start.9 = (f32[2048,256]{1,0:T(8,128)}, f32[2048,256]{1,0:T(8,128)}, u32[]{:S(2)}, u32[]{:S(2)}) collective-permute-start(f32[2048,256]{1,0:T(8,128)} %get-tuple-element.37.refs_5_.refs_1_), channel_id=1, source_target_pairs={{1,0},{2,1},{3,2},{4,3},{5,4},{6,5},{7,6},{8,7},{9,8},{10,9},{11,1... | collective-permute-start | bytes 6291464 | tf_op jit(solution)/shard_map/ppermute | solution.py:228
  75.0 50.4 %collective-permute-start.6 = (f32[1,2,256,512]{3,2,1,0:T(8,128)}, f32[1,2,256,512]{3,2,1,0:T(8,128)}, u32[]{:S(2)}, u32[]{:S(2)}) collective-permute-start(f32[1,2,256,512]{3,2,1,0:T(8,128)} %get-tuple-element.43.refs_2_.refs_3_), channel_id=1, source_target_pairs={{4,20},{5,21},{6,22},{7,23},{12,28},{13,29},{14,30},{15,31},{21,5}... | collective-permute-start | bytes 3145736 | tf_op jit(solution)/shard_map/ppermute | solution.py:228
  85.5 59.8 %collective-permute-start.7 = (f32[2,2,256,512]{3,2,1,0:T(8,128)}, f32[2,2,256,512]{3,2,1,0:T(8,128)}, u32[]{:S(2)}, u32[]{:S(2)}) collective-permute-start(f32[2,2,256,512]{3,2,1,0:T(8,128)} %get-tuple-element.45.refs_2_.refs_3_), channel_id=1, source_target_pairs={{0,16},{1,17},{2,18},{3,19},{4,20},{5,21},{6,22},{7,23},{8,24},{9,... | collective-permute-start | bytes 6291464 | tf_op jit(solution)/shard_map/ppermute | solution.py:228
  136.0 65.9 %collective-permute-start.11 = (f32[2,2,256,512]{3,2,1,0:T(8,128)}, f32[2,2,256,512]{3,2,1,0:T(8,128)}, u32[]{:S(2)}, u32[]{:S(2)}) collective-permute-start(f32[2,2,256,512]{3,2,1,0:T(8,128)} %get-tuple-element.49.refs_2_.refs_3_), channel_id=1, source_target_pairs={{8,24},{9,25},{10,26},{11,27},{12,28},{13,29},{14,30},{15,31},{24,... | collective-permute-start | bytes 6291464 | tf_op jit(solution)/shard_map/ppermute | solution.py:228
  153.2 82.0 %collective-permute-start.10 = (f32[2,2,256,512]{3,2,1,0:T(8,128)}, f32[2,2,256,512]{3,2,1,0:T(8,128)}, u32[]{:S(2)}, u32[]{:S(2)}) collective-permute-start(f32[2,2,256,512]{3,2,1,0:T(8,128)} %get-tuple-element.47.refs_2_.refs_3_), channel_id=1, source_target_pairs={{8,24},{9,25},{10,26},{11,27},{12,28},{13,29},{14,30},{15,31},{24,... | collective-permute-start | bytes 6291464 | tf_op jit(solution)/shard_map/ppermute | solution.py:228
  197.3 37.9 %collective-permute-start.12 = (f32[8,256,256]{2,1,0:T(8,128)}, f32[8,256,256]{2,1,0:T(8,128)}, u32[]{:S(2)}, u32[]{:S(2)}) collective-permute-start(f32[8,256,256]{2,1,0:T(8,128)} %get-tuple-element.57.refs_2_), channel_id=1, source_target_pairs={{0,1},{1,2},{2,3},{3,4},{4,5},{5,6},{6,7},{7,8},{8,9},{9,10},{10,1... | collective-permute-start | bytes 6291464 | tf_op jit(solution)/shard_map/ppermute | solution.py:228
  200.0 64.7 %collective-permute-start.13 = (f32[8,256,256]{2,1,0:T(8,128)}, f32[8,256,256]{2,1,0:T(8,128)}, u32[]{:S(2)}, u32[]{:S(2)}) collective-permute-start(f32[8,256,256]{2,1,0:T(8,128)} %get-tuple-element.55.refs_7_.refs_1_.refs_10_), channel_id=1, source_target_pairs={{1,0},{2,1},{3,2},{4,3},{5,4},{6,5},{7,6},{8,7},{9,8},{10,9},{11,1... | collective-permute-start | bytes 6291464 | tf_op jit(solution)/shard_map/ppermute | solution.py:228
  208.0 73.4 %collective-permute-start.17 = (f32[6,256,256]{2,1,0:T(8,128)}, f32[6,256,256]{2,1,0:T(8,128)S(1)}, u32[]{:S(2)}, u32[]{:S(2)}) collective-permute-start(f32[6,256,256]{2,1,0:T(8,128)} %get-tuple-element.56.refs_7_.refs_1_), channel_id=1, source_target_pairs={{1,0},{2,1},{3,2},{4,3},{5,4},{6,5},{7,6},{8,7},{9,8},{10,9},{11,1... | collective-permute-start | bytes 4718600 | tf_op jit(solution)/shard_map/ppermute | solution.py:228
  219.9 71.2 %collective-permute-start.16 = (f32[6,256,256]{2,1,0:T(8,128)}, f32[6,256,256]{2,1,0:T(8,128)}, u32[]{:S(2)}, u32[]{:S(2)}) collective-permute-start(f32[6,256,256]{2,1,0:T(8,128)} %get-tuple-element.60.refs_2_), channel_id=1, source_target_pairs={{0,1},{1,2},{2,3},{3,4},{4,5},{5,6},{6,7},{7,8},{8,9},{9,10},{10,1... | collective-permute-start | bytes 4718600 | tf_op jit(solution)/shard_map/ppermute | solution.py:228
  270.2 33.8 %collective-permute-start.15 = (f32[4,256,256]{2,1,0:T(8,128)}, f32[4,256,256]{2,1,0:T(8,128)}, u32[]{:S(2)}, u32[]{:S(2)}) collective-permute-start(f32[4,256,256]{2,1,0:T(8,128)} %get-tuple-element.58.refs_11_.refs_1_.refs_7_), channel_id=1, source_target_pairs={{1,0},{2,1},{3,2},{4,3},{5,4},{6,5},{7,6},{8,7},{9,8},{10,9},{11,1... | collective-permute-start | bytes 3145736 | tf_op jit(solution)/shard_map/ppermute | solution.py:228
  272.2 38.9 %collective-permute-start.14 = (f32[4,256,256]{2,1,0:T(8,128)}, f32[4,256,256]{2,1,0:T(8,128)}, u32[]{:S(2)}, u32[]{:S(2)}) collective-permute-start(f32[4,256,256]{2,1,0:T(8,128)} %get-tuple-element.59.refs_2_), channel_id=1, source_target_pairs={{0,1},{1,2},{2,3},{3,4},{4,5},{5,6},{6,7},{7,8},{8,9},{9,10},{10,1... | collective-permute-start | bytes 3145736 | tf_op jit(solution)/shard_map/ppermute | solution.py:228
  281.4 2.5 copy-start
Sparse Core Ops, SparseCore 0:
  19.1 50.2 all-gather.8
  71.0 54.2 all-gather.6
  136.1 46.5 all-gather.10

commit v2 on v1

--- a/solution.py
+++ b/solution.py
@@ -22,10 +22,10 @@
     return dot(lh, rh) + (dot(lh, rl) + dot(ll, rh))
 
 
-PLANE, COL, PLANE0, NEWEST, MEMBER, SWAP_B, FIRST_IN, LAST_IN, LAST_LEVEL, USE_LAST, OWNS, COUNTS = range(12)
-
-
-def call(kernel, info, grid, in_specs, out_specs, out_shape, scratch, args, alias=None, after=(), opens=False):
+PLANE, COL, PLANE0, NEWEST, MEMBER, SWAP_B, FIRST_IN, LAST_IN, LAST_LEVEL, USE_LAST, OWNS, ODD, LATE, COUNTS = range(14)
+
+
+def call(kernel, info, grid, in_specs, out_specs, out_shape, scratch, args, alias=None, after=(), short=False):
     count = len(args)
     after = [a for a in after if all(a is not arg for arg in args)]
 
@@ -44,7 +44,7 @@
         out_shape=out_shape,
         input_output_aliases=alias or {},
         compiler_params=pltpu.CompilerParams(vmem_limit_bytes=VMEM_LIMIT),
-        cost_estimate=pl.CostEstimate(flops=10**14 if opens else 1, bytes_accessed=1, transcendentals=0),
+        cost_estimate=pl.CostEstimate(flops=1 if short else 10**14, bytes_accessed=1, transcendentals=0),
     )(info, *args, *after)
 
 
@@ -72,12 +72,17 @@
     chain_b[...] = jnp.where(info[OWNS] == 1, own[:, :half], own[:, half:]).T
 
 
-def gather_kernel(info, *refs):
-    for place, piece in enumerate(refs[:-1]):
-        refs[-1][place] = piece[...]
-
-
-def first_kernel(joint, info, seg, col, factor, prev_top, *rest):
+def pair_kernel(info, own, across, out):
+    odd = info[ODD] == 1
+    out[0] = jnp.where(odd, across[...], own[...])
+    out[1] = jnp.where(odd, own[...], across[...])
+
+
+def rest_kernel(info, value, out):
+    del info, value, out
+
+
+def first_kernel(joint, info, seg, col, near, far, prev_top, *rest):
     sends, (last_top, col_h, col_l, carry) = rest[: 2 - joint], rest[2 - joint :]
     half = prev_top.shape[0]
     i = pl.program_id(0)
@@ -88,7 +93,7 @@
         carry[...] = prev_top[...]
 
     mid = split(dot3(split(seg[...]), (col_h[...], col_l[...])))
-    out = dot3(split(jnp.concatenate([factor[0], factor[1]], axis=0)), mid)
+    out = dot3(split(jnp.concatenate([near[...], far[...]], axis=0)), mid)
     sent = jnp.where(info[PLANE0] == 1, carry[...], out[:half])
     if joint:
         sends[0][0] = out[half:]
@@ -100,13 +105,18 @@
     last_top[...] = out[:half]
 
 
-def second_kernel(begin, count, tail, info, factor, bottom, sent, got_bottom, got_top, *rest):
+def second_kernel(begin, count, tail, older, turn, info, near, far, bottom, sent, got_bottom, got_top, *rest):
     left, right = rest[-2:]
     half = bottom.shape[0]
 
     @pl.when(pl.program_id(0) < count)
     def _():
-        lower, upper = split(factor[info[SWAP_B]]), split(factor[1 - info[SWAP_B]])
+        a, b = near[...], far[...]
+        if older:
+            late = info[LATE] == 1
+            a, b = jnp.where(late, rest[-4][...], a), jnp.where(late, rest[-3][...], b)
+        turned = info[turn] == 1
+        lower, upper = split(jnp.where(turned, b, a)), split(jnp.where(turned, a, b))
 
         def stacked(one, other):
             return split(jnp.concatenate([one, other], axis=0))
@@ -145,18 +155,44 @@
     out[:, half:] = dot3(wide(mine_right, right_in), (cur_h[...], cur_l[...]))
 
 
-def third_kernel(begin, last_unit, info, left, right, up_far, up_near, down_near, down_far, down_last, prev, cur, held, out, *scratch):
+def third_kernel(begin, last_unit, slots, info, left, right, up_far, up_near, down_near, down_far, down_last, prev, cur, held, out, *scratch):
     del held
-    e, h = pl.program_id(0), pl.program_id(1)
-
-    @pl.when((e == 0) & (h == 0))
+    *scratch, made, sems = scratch
+    e, count = pl.program_id(0), made.shape[0]
+    half = left.shape[1]
+
+    def copies(unit):
+        slot = lax.rem(info[NEWEST] - begin - unit + slots, slots)
+        upper = lax.rem(slot + info[PLANE0], slots)
+        for h, row in enumerate(((2 * slot + 1) * half, 2 * upper * half)):
+            place = pl.ds(pl.multiple_of(row, half), half)
+            yield pltpu.make_async_copy(made.at[unit, pl.ds(h * half, half)], out.at[place], sems.at[unit, h])
+
+    @pl.when(e == 0)
     def _():
         split_columns(prev, cur, scratch)
 
-    left_in = jnp.where(info[FIRST_IN] == 1, up_far[...], up_near[...])
-    far = jnp.where((info[USE_LAST] == 1) & (begin + e == last_unit) & (h == 1), down_last[...], down_far[...])
-    right_in = jnp.where(info[LAST_IN] == 1, far, down_near[...])
-    columns(left_in, left[...], right[...], right_in, scratch, out)
+    def flat(ref):
+        return ref[...].reshape(2 * half, half)
+
+    left_in = jnp.where(info[FIRST_IN] == 1, flat(up_far), flat(up_near))
+    far = flat(down_far)
+    ends_here = (info[USE_LAST] == 1) & (begin + e == last_unit)
+    far = jnp.concatenate([far[:half], jnp.where(ends_here, down_last[...], far[half:])], axis=0)
+    right_in = jnp.where(info[LAST_IN] == 1, far, flat(down_near))
+    for unit in range(count):
+
+        @pl.when(e == unit)
+        def _():
+            columns(left_in, flat(left), flat(right), right_in, scratch, made.at[unit])
+            for copy in copies(unit):
+                copy.start()
+
+    @pl.when(e == count - 1)
+    def _():
+        for unit in range(count):
+            for copy in copies(unit):
+                copy.wait()
 
 
 def last_kernel(info, top, up_far, up_near, down_near, prev, cur, held, out, *scratch):
@@ -215,12 +251,14 @@
         plane == 0,
         newest,
         member,
-        (plane == 1) & paired,
+        (member != plane) & paired,
         col % group == 0,
         col % group == group - 1,
         level == levels - 1,
         (plane == 0) & (level == levels - 2),
         member == plane,
+        (col // 2) % 2,
+        (col // 4) % 2 == 0,
     ]
     info = jnp.concatenate([jnp.stack([jnp.asarray(v, jnp.int32) for v in place]), swap_counts.reshape(-1)])
 
@@ -269,46 +307,68 @@
         return values
 
     teams = [list(range(g * group, (g + 1) * group)) for g in range(cols // group)]
-    if paired:
-        pieces_b = chained(chain_b)
-        first_factors = [lax.all_gather(v, "pcol", axis_index_groups=teams) for v in chained(half_a)]
-    else:
+
+    def gathered(value):
+        mine = lax.all_gather(value, "pcol", axis_index_groups=teams)
+        return (mine, lambda q: 2 * q, mine, lambda q: 2 * q + 1)
+
+    def placed(value, *after):
+        anywhere = pl.BlockSpec(memory_space=pl.ANY)
+        value = call(
+            rest_kernel, info, (1,), [anywhere], anywhere, shape(*value.shape), [], (value,), {1: 0}, [*last[-1:], *after]
+        )
+        last.append(value)
+        return value
+
+    def paired_up(own, across, *after):
+        out = call(
+            pair_kernel,
+            info,
+            (1,),
+            [whole((half, window))] * 2,
+            whole((2, half, window)),
+            shape(2, half, window),
+            [],
+            (own, across),
+            after=[*last[-1:], *after],
+        )
+        last.append(out)
+        return out
+
+    def with_swapped(mine):
+        other = send(mine, [((p, c), (p, c + 1 - 2 * (c % 2))) for p, c in everyone])
+        return (mine, lambda q: q % 2, other, lambda q: q % 2)
+
+    if not paired:
 
         def shared(value, holder):
             value = jnp.where(member == holder, value, jnp.zeros_like(value))
             return lax.psum(value, "pcol", axis_index_groups=teams)
 
         full_first = shared(full_first, plane)
-        first_factors = chained(full_first)
         both = jnp.stack([shared(chain_b, plane), shared(chain_b, owner)])
-        second_factors = jnp.stack(chained(both), axis=1)
-
-    def gather_second():
-        out = call(
-            gather_kernel,
-            info,
-            (1,),
-            [whole((half, window))] * levels,
-            whole((levels, half, window)),
-            shape(levels, half, window),
-            [],
-            pieces_b,
-            after=last[-1:],
-        )
-        last.append(out)
-        return lax.all_gather(out, "pcol", axis_index_groups=teams)
-
-    came_prev = along(prev_own, 1)
-    prev = jnp.where(col == 0, (rows == lanes + half).astype(f32), came_prev)
+        first_factors = [(value, lambda q: 0, value, lambda q: 1) for value in chained(full_first)]
+        second_factors = [(value, lambda q: 0, value, lambda q: 1) for value in chained(both) for _ in range(fold)]
+
+    def previous(value):
+        came_prev = along(value, 1)
+        return came_prev, jnp.where(col == 0, (rows == lanes + half).astype(f32), came_prev)
 
     seg = segment.reshape(slots * window, window)
 
     def slot_of(t, f):
         return lax.rem(f[NEWEST] - t + slots, slots)
 
-    def first_step(batch, prev_top, joint, after, opens):
+    def factor_specs(factor, at):
+
+        def spec(array, first):
+            return pl.BlockSpec((None, half, window), lambda i, f: (first(at(i)), 0, 0))
+
+        return [spec(*factor[:2]), spec(*factor[2:])]
+
+    def first_step(batch, prev_top, joint, after):
         count, begin = len(batch), batch[0]
-        factor = full_first if begin == 0 else first_factors[begin // fold]
+        factor = first_factors[begin // fold] if begin or not paired else (full_first, lambda q: 0, full_first, lambda q: 1)
         place = 0 if begin == 0 else fold - 1 - begin % fold
         if joint:
             specs = [pl.BlockSpec((None, 2, half, window), lambda i, f: (i, 0, 0, 0))]
@@ -323,15 +383,14 @@
             [
                 pl.BlockSpec((window, window), lambda i, f: (slot_of(begin + i, f), 0)),
                 whole((window, window)),
-                pl.BlockSpec((2, half, window), lambda i, f: (place - i, 0, 0)),
+                *factor_specs(factor, lambda i: place - i),
                 whole((half, window)),
             ],
             specs + [whole((half, window))],
             shapes + [shape(half, window)],
             [pltpu.VMEM((window, window), bf)] * 2 + [pltpu.VMEM((half, window), f32)],
-            (seg, own_first, factor, prev_top),
+            (seg, own_first, factor[0], factor[2], prev_top),
             after=[*last[-1:], *after],
-            opens=opens,
         )
         return outs[:-1], outs[-1]
 
@@ -348,26 +407,28 @@
             return [send(sends[0], sorted(set(down + up)))]
         return [send(sends[0], down), send(sends[1], up)]
 
-    def second_step(batch, size, at, sends, gots, held, ended, after, opens):
+    def second_step(batch, size, at, sends, gots, held, ended, after):
         count, begin = len(batch), batch[0]
-        hop, place = begin // fold, fold - 1 - begin % fold
+        factor, place = second_factors[begin], fold - 1 - begin % fold
+        older = second_factors[begin - 2] if by_level and begin == 2 else ()
+        turn = PLANE if paired and not (by_level and begin < fold) else SWAP_B
+        specs = lambda factor: factor_specs(factor, lambda i: place - inner(i)) if factor else []
         inner = lambda i: jnp.minimum(i, count - 1)
         piece = lambda k: pl.BlockSpec((None, None, half, window), lambda i, f: (inner(i), k, 0, 0))
         pieces = [piece(0), piece(len(sends) % 2)]
         ends = [pl.BlockSpec((2, half, half), lambda i, f: (at + i, 0, 0))] * 2
         extra = [whole((half, window))] if ended else [pl.BlockSpec(memory_space=pl.ANY)] * len(held)
         return call(
-            functools.partial(second_kernel, begin, count, bool(ended)),
+            functools.partial(second_kernel, begin, count, bool(ended), bool(older), turn),
             info,
             (count + len(ended),),
-            [pl.BlockSpec((2, None, half, window), lambda i, f: (place - inner(i), hop, 0, 0))] + pieces + pieces + extra,
+            specs(factor) + pieces + pieces + extra + specs(older),
             ends,
             [shape(2 * size, half, half)] * 2,
             [],
-            (second_factors, sends[0], sends[-1], gots[0], gots[-1], *ended, *held),
-            {6 + k: k for k in range(len(held))},
+            (factor[0], factor[2], sends[0], sends[-1], gots[0], gots[-1], *ended, *held, *older[::2]),
+            {7 + k: k for k in range(len(held))},
             [*last[-1:], *after],
-            opens,
         )
 
     split_scratch = [pltpu.VMEM((window, half), bf)] * 4
@@ -376,7 +437,7 @@
     deep = window if all(n % window == 0 for n in counts) else half
     above_blocks, basis_blocks = (n // deep for n in counts)
 
-    def rows_step(after=(), opens=False):
+    def rows_step(after=()):
         tall = pl.BlockSpec((deep, half), lambda i, f: (i, 0))
         blocks = above_blocks + basis_blocks
         return call(
@@ -393,10 +454,9 @@
             [pltpu.VMEM((window, window), bf)] * 2,
             (above_rows, basis_rows, own_first),
             after=[*last[-1:], *after],
-            opens=opens,
-        )
-
-    def rows_end(first, blocks, parts):
+        )
+
+    def rows_end(first, blocks, parts, after):
         tall = pl.BlockSpec((deep, half), lambda i, f: (first + i, 0))
         return call(
             rows_end_kernel,
@@ -407,42 +467,36 @@
             shape(blocks * deep, window),
             split_scratch,
             (*parts, prev, cur),
-            after=last[-1:],
+            after=[*last[-1:], *after],
         )
 
     lefts, rights, ups, downs = ([None] * slots for _ in range(4))
 
-    def third_step(batch, held, after, opens):
+    def third_step(batch, held, after):
         begin = batch[0]
         fresh = held is None
         parts = [lefts[begin], rights[begin]]
         parts.append(ups[begin - fold] if begin >= fold else (no_strips, 0))
         parts += [ups[begin], downs[begin], downs[(begin + fold) % slots]]
-        piece = lambda at: pl.BlockSpec((None, half, half), lambda e, h, f: (2 * (at + e) + h, 0, 0))
-
-        def out_block(e, h, f):
-            slot = slot_of(begin + e, f)
-            upper = lax.rem(slot + f[PLANE0], slots)
-            return (jnp.where(h == 0, 2 * slot + 1, 2 * upper), 0)
-
+        piece = lambda at: pl.BlockSpec((2, half, half), lambda e, f: (at + e, 0, 0))
         args = [array for array, _ in parts]
         ending = slots - fold in batch
         tail_row = 2 * ending_strips[2] if ending else 0
         return call(
-            functools.partial(third_kernel, begin, slots - fold),
+            functools.partial(third_kernel, begin, slots - fold, slots),
             info,
-            (len(batch), 2),
+            (len(batch),),
             [piece(at) for _, at in parts]
-            + [pl.BlockSpec((None, half, half), lambda e, h, f: (tail_row, 0, 0))]
+            + [pl.BlockSpec((None, half, half), lambda e, f: (tail_row, 0, 0))]
             + [whole((window, half))] * 2
             + [pl.BlockSpec(memory_space=pl.ANY)],
-            pl.BlockSpec((half, window), out_block),
+            pl.BlockSpec(memory_space=pl.ANY),
             shape(*seg.shape),
-            split_scratch,
+            split_scratch
+            + [pltpu.VMEM((len(batch), window, window), f32), pltpu.SemaphoreType.DMA((len(batch), 2))],
             (*args, ending_strips[1] if ending else args[0], prev, cur, args[0] if fresh else held),
             None if fresh else {10: 0},
             [*last[-1:], *after],
-            opens,
         )
 
     def last_step(held):
@@ -470,22 +524,28 @@
     tops, sent, got, made = [jnp.zeros((half, window), f32)], {}, {}, {}
     no_strips = jnp.zeros((2 * slots, half, half), f32)
 
-    def do_first(batch, after=(), opens=False):
-        sent[batch[0]], top = first_step(batch, tops[-1], paired and batch[0] > 0, after, opens)
+    def do_first(batch, after=()):
+        sent[batch[0]], top = first_step(batch, tops[-1], paired, after)
         tops.append(top)
         last.append(top)
         got[batch[0]] = exchange(batch, sent[batch[0]])
 
-    def do_second(batch, strip, ended=(), after=(), opens=False):
+    def do_second(batch, strip, ended=(), after=()):
         begin = batch[0]
         held = made.get(strip[0], ())
         made[strip[0]] = second_step(
-            batch, len(strip) + len(ended), begin - strip[0], sent[begin], got[begin], held, ended, after, opens
+            batch, len(strip) + len(ended), begin - strip[0], sent[begin], got[begin], held, ended, after
         )
         last.append(made[strip[0]][0])
         if batch[-1] == strip[-1]:
             left, right = made[strip[0]]
-            up, down = along(right, 1), along(left, -1)
+
+
+            def filled(c):
+                first = fold * (c // group) + fold - 1
+                return any(-1 <= first - t <= c // planes for t in strip)
+
+            up, down = along(right, 1, filled), along(left, -1, filled)
             for place, t in enumerate(strip):
                 lefts[t], rights[t] = (left, place), (right, place)
                 ups[t], downs[t] = (up, place), (down, place)
@@ -493,56 +553,76 @@
 
     out = [None]
 
-    def do_third(batch, after=(), opens=False):
-        out[0] = third_step(batch, out[0], after, opens)
+    def do_third(batch, after=()):
+        out[0] = third_step(batch, out[0], after)
         last.append(out[0])
 
     def do_last():
         out[0] = last_step(out[0])
         last.append(out[0])
 
-    def do_rows():
-        left, right = rows_step(opens=True)
+    def do_rows(after=()):
+        left, right = rows_step(after)
         last.append(left)
         return left, right, along(right, 1), along(left, -1)
 
-    def do_rows_end():
-        for first, blocks in ((0, above_blocks), (above_blocks, basis_blocks)):
-            row_ends.append(rows_end(first, blocks, parts))
-            last.append(row_ends[-1])
+    def do_rows_end(which, after=()):
+        first, blocks = ((0, above_blocks), (above_blocks, basis_blocks))[which]
+        row_ends.append(rows_end(first, blocks, parts, after))
+        last.append(row_ends[-1])
 
     row_ends = []
-    if paired and fold == 4 and levels == 2:
+    def hop(value, distance):
+        return along(value, group // 2, lambda c: c // (group // 2) >= distance - 1)
+
+    by_level = paired and fold == 4 and levels == 2
+    if by_level:
+        first_factors = [gathered(half_a)]
+        hop_a = hopped(half_a, 1)
+        across = send(chain_b, [((p, c), (p, c // 4 * 4 + (c + 2) % 4)) for p, c in everyone])
         do_first([0])
-        parts = do_rows()
-        do_first([1], [came_prev, *got[0]])
-        do_first([2, 3], opens=True)
-        do_first([4, 5], got[1], opens=True)
-        second_factors = gather_second()
-        do_first([6, 7], [*got[2], *parts[2:]], opens=True)
-        for batch in ([0], [1], [2, 3]):
-            do_second(batch, [0, 1, 2, 3])
-        ending_strips = do_second([4, 5], [4, 5], ended=[tops[-1]], opens=True)
-        do_rows_end()
-        do_second([6, 7], [6, 7], after=[*ups[0][:1], *downs[0][:1]])
-        do_third([0, 1], opens=True)
+        came_prev, prev = previous(prev_own)
+        pieces = paired_up(chain_b, across, came_prev)
+        second_factors = [with_swapped(pieces)] * 2
+        pieces = hop(pieces, 1)
+        do_first([1], got[0])
+        first_factors.append(gathered(placed(hop_a)))
+        do_first([2, 3], [second_factors[0][2]])
+        second_factors += [with_swapped(placed(pieces))] * 2
+        hop_b = hopped(placed(chain_b), 1)
+        do_second([0], [0, 1, 2, 3], after=got[1])
+        parts = do_rows([second_factors[2][2]])
+        do_second([1], [0, 1, 2, 3])
+        do_first([4, 5], got[2])
+        second_factors += [gathered(placed(hop_b))] * fold
+        do_second([2, 3], [0, 1, 2, 3], after=parts[2:3])
+        do_first([6, 7], parts[3:])
+        do_rows_end(0)
+        do_rows_end(1)
+        got[4] = [placed(got[4][0])]
+        ending_strips = do_second([4, 5], [4, 5], ended=[tops[-1]])
+        do_second([6, 7], [6, 7], after=[ups[0][0], downs[0][0]])
+        do_third([0, 1])
         do_third([4, 5])
         do_last()
         do_third([2, 3])
         do_third([6, 7])
     else:
+        _, prev = previous(prev_own)
         parts = do_rows()
+        if paired:
+            first_factors = [gathered(value) for value in chained(half_a)]
+            second_factors = [gathered(value) for value in chained(chain_b) for _ in range(fold)]
         for t in range(slots):
             do_first([t])
-        if paired:
-            second_factors = gather_second()
         for t in range(slots):
             ending_strips = do_second([t], [t], ended=[tops[-1]] if t == slots - 1 else ())
         for t in range(slots - 1):
             do_third([t])
         do_last()
         do_third([slots - 1])
-        do_rows_end()
+        do_rows_end(0)
+        do_rows_end(1)
     return (out[0].reshape(segment.shape), *row_ends)
 
 

time: 331 us -> 319 us (0.964); the launches traced: 325 us -> 318 us
  waiting for transfers between devices: 135 us -> 113 us
  starting transfers between devices: 46.4 us -> 55.1 us
  Pallas kernels: 121 us -> 126 us
    all_gather x3, waiting for transfers between devices: 75.1 us -> 26.8 us  [gathered(): mine = lax.all_gather(value, 'pcol', axis_index_groups=teams)]
    ppermute x18 -> x21, waiting for transfers between devices: 59.7 us -> 86.6 us  [send(): lax.ppermute(value, GRID, [(a * cols + b, c * cols + d) for (a, b), (c, d...]
    ppermute x18 -> x21, starting transfers between devices: 46.3 us -> 55 us  [send(): lax.ppermute(value, GRID, [(a * cols + b, c * cols + d) for (a, b), (c, d...]
    pallas_call x20 -> x25, Pallas kernels: 121 us -> 126 us  [call(): pl.pallas_call(run, grid_spec=pltpu.PrefetchScalarGridSpec(num_scalar_pre...]
  transfers between devices with their start and end apart: 21 -> 24, of which waited for: 10 -> 12; matrix products, arithmetic and copies ran while one was open for 2% -> 2% of each run, Pallas kernels for 34% -> 36%
where the time goes in v2:
time: 319 us; the launch traced here: 318 us
  Pallas kernels  126 us (39%)
  waiting for transfers between devices  113 us (35%)
  starting transfers between devices  55.1 us (17%)
  between operations  14.2 us (4%)
  local copies, waits for them, and re-layouts  6.21 us (2%)
    pallas_call x25, Pallas kernels, call(): pl.pallas_call(run, grid_spec=pltpu.PrefetchScalarGridSpec(num_scalar_pre...  126 us
    ppermute x21, waiting for transfers between devices, send(): lax.ppermute(value, GRID, [(a * cols + b, c * cols + d) for (a, b), (c, d...  86.6 us
    ppermute x21, starting transfers between devices, send(): lax.ppermute(value, GRID, [(a * cols + b, c * cols + d) for (a, b), (c, d...  55 us
    all_gather x3, waiting for transfers between devices, gathered(): mine = lax.all_gather(value, 'pcol', axis_index_groups=teams)  26.8 us
  transfers between devices with their start and end apart: 24, of which 12 were waited for; matrix products, arithmetic and copies ran while one was open for 2% of the time, Pallas kernels for 36%

profile of v2, /device:TPU:25, one launch (start us, length us, event | category | flops | bytes accessed | tf_op | source)
XLA Modules:
  0.0 317.6 jit_solution(11119973667207300665)
XLA Ops:
  7.2 1.3 slice_bitcast_fusion
  8.5 1.3 collective-permute-start
  10.0 0.6 concatenate.3.refs_0_
  10.6 0.6 iota_add_fusion
  11.2 1.8 collective-permute-done.refs_2_
  13.1 1.0 copy-done.1
  14.0 4.9 %shard_map.76 = (f32[512,512]{1,0:T(8,128)}, f32[2,256,512]{2,1,0:T(8,128)}, f32[256,512]{1,0:T(8,128)}, f32[256,512]{1,0:T(8,128)}, f32[512,256]{1,0:T(8,128)}, /*index=5*/f32[512,256]{1,0:T(8,128)}) custom-call(s32[45]{0:T(128)} %concatenate.3.refs_0_, f32[2,1,512,512]{3,2,1,0:T(8,128)} %refs_1_.2, f32[512,512]{1,0:T(8,128)} %copy-done.1), custom_call_target="tpu_custom_call" | custom-call | flops 100000000376832 | bytes 1 | tf_op jit(solution)/shard_map/pallas_call | solution.py:35
  19.0 1.3 collective-permute-start.5
  20.3 1.3 collective-permute-start.1
  21.6 2.4 collective-permute-start.2
  24.0 0.9 broadcast_in_dim.6.refs_5_
  24.9 5.7 %shard_map.77 = (f32[1,2,256,512]{3,2,1,0:T(8,128)}, f32[256,512]{1,0:T(8,128)}) custom-call(s32[45]{0:T(128)} %concatenate.3.refs_0_, f32[4096,512]{1,0:T(8,128)} %bitcast.22, f32[512,512]{1,0:T(8,128)} %get-tuple-element.32.refs_2_.refs_3_, f32[2,256,512]{2,1,0:T(8,128)} %get-tuple-element.33.refs_3_.refs_4_, ...), custom_call_target="tpu_custom_call" | custom-call | flops 100000000376832 | bytes 1 | tf_op jit(solution)/shard_map/pallas_call | solution.py:35
  30.6 1.6 collective-permute-start.4
  32.2 13.1 %collective-permute-done.1.refs_2_ = f32[256,512]{1,0:T(8,128)} collective-permute-done((f32[256,512]{1,0:T(8,128)}, f32[256,512]{1,0:T(8,128)}, u32[]{:S(2)}, u32[]{:S(2)}) %collective-permute-start.1) | collective-permute-done | bytes 524320 | tf_op jit(solution)/shard_map/ppermute | solution.py:266
  45.3 7.5 %collective-permute-done.2.refs_4_ = f32[512,256]{1,0:T(8,128)} collective-permute-done((f32[512,256]{1,0:T(8,128)}, f32[512,256]{1,0:T(8,128)}, u32[]{:S(2)}, u32[]{:S(2)}) %collective-permute-start.2) | collective-permute-done | bytes 524320 | tf_op jit(solution)/shard_map/ppermute | solution.py:266
  52.8 3.1 shard_map.78.refs_6_.refs_1_.refs_9_
  55.9 1.3 collective-permute-start.3
  57.2 1.9 convert_select_fusion.refs_5_.refs_8_
  59.1 1.6 all-gather.7.cloned.1.call-done
  60.7 5.6 %shard_map.79 = (f32[1,2,256,512]{3,2,1,0:T(8,128)}, f32[256,512]{1,0:T(8,128)}) custom-call(s32[45]{0:T(128)} %concatenate.3.refs_0_, f32[4096,512]{1,0:T(8,128)} %bitcast.23, f32[512,512]{1,0:T(8,128)} %get-tuple-element.32.refs_2_.refs_3_, f32[8,256,512]{2,1,0:T(8,128)} %bitcast.35, f32[8,256,512]{2,1,0:T(8,128)} %bitcast.36, ...), custom_call_target="tpu_custom_call" | custom-call | flops 100000000376832 | bytes 1 | tf_op jit(solution)/shard_map/pallas_call | solution.py:35
  66.4 3.6 %collective-permute-start.8 = (f32[1,2,256,512]{3,2,1,0:T(8,128)}, f32[1,2,256,512]{3,2,1,0:T(8,128)}, u32[]{:S(2)}, u32[]{:S(2)}) collective-permute-start(f32[1,2,256,512]{3,2,1,0:T(8,128)} %get-tuple-element.40.refs_3_.refs_4_), channel_id=1, source_target_pairs={{4,20},{5,21},{6,22},{7,23},{12,28},{13,29},{14,30},{15,31},{21,5}... | collective-permute-start | bytes 3145736 | tf_op jit(solution)/shard_map/ppermute | solution.py:266
  70.0 0.7 shard_map.80.refs_6_
  70.7 7.9 %shard_map.81 = (f32[2,2,256,512]{3,2,1,0:T(8,128)}, f32[256,512]{1,0:T(8,128)}) custom-call(s32[45]{0:T(128)} %concatenate.3.refs_0_, f32[4096,512]{1,0:T(8,128)} %bitcast.24, f32[512,512]{1,0:T(8,128)} %get-tuple-element.32.refs_2_.refs_3_, f32[8,256,512]{2,1,0:T(8,128)} %bitcast.37, f32[8,256,512]{2,1,0:T(8,128)} %bitcast.38, ...), custom_call_target="tpu_custom_call" | custom-call | flops 100000000376832 | bytes 1 | tf_op jit(solution)/shard_map/pallas_call | solution.py:35
  78.6 4.4 %collective-permute-done.3.refs_1_ = f32[2,256,512]{2,1,0:T(8,128)} collective-permute-done((f32[2,256,512]{2,1,0:T(8,128)}, f32[2,256,512]{2,1,0:T(8,128)}, u32[]{:S(2)}, u32[]{:S(2)}) %collective-permute-start.3) | collective-permute-done | bytes 1048608 | tf_op jit(solution)/shard_map/ppermute | solution.py:266
  83.0 0.7 shard_map.82.refs_2_.refs_1_
  83.7 0.7 shard_map.83.refs_7_
  84.4 1.1 collective-permute-start.9
  85.6 3.7 %collective-permute-start.10 = (f32[2,2,256,512]{3,2,1,0:T(8,128)}, f32[2,2,256,512]{3,2,1,0:T(8,128)}, u32[]{:S(2)}, u32[]{:S(2)}) collective-permute-start(f32[2,2,256,512]{3,2,1,0:T(8,128)} %get-tuple-element.45.refs_3_.refs_4_), channel_id=1, source_target_pairs={{0,16},{1,17},{2,18},{3,19},{4,20},{5,21},{6,22},{7,23},{8,24},{9,... | collective-permute-start | bytes 6291464 | tf_op jit(solution)/shard_map/ppermute | solution.py:266
  89.3 1.3 collective-permute-start.7
  90.6 2.0 collective-permute-done.8.refs_8_.refs_5_.refs_6_
  92.6 4.5 %shard_map.84 = (f32[8,256,256]{2,1,0:T(8,128)}, f32[8,256,256]{2,1,0:T(8,128)}) custom-call(s32[45]{0:T(128)} %concatenate.3.refs_0_, f32[2,256,512]{2,1,0:T(8,128)} %shard_map.78.refs_6_.refs_1_.refs_9_, f32[2,256,512]{2,1,0:T(8,128)} %collective-permute-done.6.refs_7_.refs_2_.refs_10_, f32[1,2,256,512]{3,2,1,0:T(8,128)} %get-tuple-element.37.refs_3_.refs_4_, ...), custom_call_target="tpu_custom_call" | custom-call | flops 100000000376832 | bytes 1 | tf_op jit(solution)/shard_map/pallas_call | solution.py:35
  97.1 8.4 %shard_map.85 = (f32[2048,256]{1,0:T(8,128)}, f32[2048,256]{1,0:T(8,128)}) custom-call(s32[45]{0:T(128)} %concatenate.3.refs_0_, f32[1024,512]{1,0:T(8,128)} %refs_1_.3, f32[1024,512]{1,0:T(8,128)} %refs_2_.1, f32[512,512]{1,0:T(8,128)} %get-tuple-element.32.refs_2_.refs_3_, f32[8,256,256]{2,1,0:T(8,128)} %get-tuple-element.41.refs_4_.refs_7_, ...), custom_call_target="tpu_custom_call" | custom-call | flops 100000000376832 | bytes 1 | tf_op jit(solution)/shard_map/pallas_call | solution.py:35
  105.5 6.7 %collective-permute-start.11 = (f32[2048,256]{1,0:T(8,128)}, f32[2048,256]{1,0:T(8,128)}, u32[]{:S(2)}, u32[]{:S(2)}) collective-permute-start(f32[2048,256]{1,0:T(8,128)} %get-tuple-element.48.refs_2_), channel_id=1, source_target_pairs={{0,1},{1,2},{2,3},{3,4},{4,5},{5,6},{6,7},{7,8},{8,9},{9,10},{10,1... | collective-permute-start | bytes 6291464 | tf_op jit(solution)/shard_map/ppermute | solution.py:266
  112.2 1.9 collective-permute-start.12
  114.1 4.5 %shard_map.86 = (f32[8,256,256]{2,1,0:T(8,128)}, f32[8,256,256]{2,1,0:T(8,128)}) custom-call(s32[45]{0:T(128)} %concatenate.3.refs_0_, f32[2,256,512]{2,1,0:T(8,128)} %shard_map.78.refs_6_.refs_1_.refs_9_, f32[2,256,512]{2,1,0:T(8,128)} %collective-permute-done.6.refs_7_.refs_2_.refs_10_, ...), custom_call_target="tpu_custom_call", output_to_operand_aliasing={{0}: (7, {}), {1}: (8, {})} | custom-call | flops 100000000376832 | bytes 1 | tf_op jit(solution)/shard_map/pallas_call | solution.py:35
  118.6 18.9 %collective-permute-done.10.refs_7_.refs_5_.refs_6_ = f32[2,2,256,512]{3,2,1,0:T(8,128)} collective-permute-done((f32[2,2,256,512]{3,2,1,0:T(8,128)}, f32[2,2,256,512]{3,2,1,0:T(8,128)}, u32[]{:S(2)}, u32[]{:S(2)}) %collective-permute-start.10) | collective-permute-done | bytes 2097184 | tf_op jit(solution)/shard_map/ppermute | solution.py:266
  137.5 7.9 %shard_map.87 = (f32[2,2,256,512]{3,2,1,0:T(8,128)}, f32[256,512]{1,0:T(8,128)}) custom-call(s32[45]{0:T(128)} %concatenate.3.refs_0_, f32[4096,512]{1,0:T(8,128)} %bitcast.25, f32[512,512]{1,0:T(8,128)} %get-tuple-element.32.refs_2_.refs_3_, f32[8,256,512]{2,1,0:T(8,128)} %bitcast.27, f32[8,256,512]{2,1,0:T(8,128)} %bitcast.28, ...), custom_call_target="tpu_custom_call" | custom-call | flops 100000000376832 | bytes 1 | tf_op jit(solution)/shard_map/pallas_call | solution.py:35
  145.5 4.1 %collective-permute-start.14 = (f32[2,2,256,512]{3,2,1,0:T(8,128)}, f32[2,2,256,512]{3,2,1,0:T(8,128)}, u32[]{:S(2)}, u32[]{:S(2)}) collective-permute-start(f32[2,2,256,512]{3,2,1,0:T(8,128)} %get-tuple-element.51.refs_3_.refs_4_), channel_id=1, source_target_pairs={{8,24},{9,25},{10,26},{11,27},{12,28},{13,29},{14,30},{15,31},{24,... | collective-permute-start | bytes 6291464 | tf_op jit(solution)/shard_map/ppermute | solution.py:266
  149.6 0.7 shard_map.88.refs_11_
  150.3 6.2 %shard_map.89 = (f32[8,256,256]{2,1,0:T(8,128)}, f32[8,256,256]{2,1,0:T(8,128)}) custom-call(s32[45]{0:T(128)} %concatenate.3.refs_0_, f32[2,256,512]{2,1,0:T(8,128)} %shard_map.82.refs_2_.refs_1_, f32[2,256,512]{2,1,0:T(8,128)} %collective-permute-done.9.refs_5_.refs_2_, ...), custom_call_target="tpu_custom_call", output_to_operand_aliasing={{0}: (7, {}), {1}: (8, {})} | custom-call | flops 100000000376832 | bytes 1 | tf_op jit(solution)/shard_map/pallas_call | solution.py:35
  156.5 4.2 %collective-permute-start.16 = (f32[8,256,256]{2,1,0:T(8,128)}, f32[8,256,256]{2,1,0:T(8,128)}, u32[]{:S(2)}, u32[]{:S(2)}) collective-permute-start(f32[8,256,256]{2,1,0:T(8,128)} %get-tuple-element.49.refs_6_.refs_1_.refs_7_.refs_10_), channel_id=1, source_target_pairs={{1,0},{2,1},{3,2},{4,3},{5,4},{6,5},{7,6},{8,7},{9,8},{10,9},{11,1... | collective-permute-start | bytes 6291464 | tf_op jit(solution)/shard_map/ppermute | solution.py:266
  160.7 7.1 %collective-permute-done.12.refs_7_.refs_4_ = f32[2048,256]{1,0:T(8,128)} collective-permute-done((f32[2048,256]{1,0:T(8,128)}, f32[2048,256]{1,0:T(8,128)}, u32[]{:S(2)}, u32[]{:S(2)}) %collective-permute-start.12) | collective-permute-done | bytes 2097184 | tf_op jit(solution)/shard_map/ppermute | solution.py:266
  167.9 8.3 %shard_map.90 = (f32[2,2,256,512]{3,2,1,0:T(8,128)}, f32[256,512]{1,0:T(8,128)}) custom-call(s32[45]{0:T(128)} %concatenate.3.refs_0_, f32[4096,512]{1,0:T(8,128)} %bitcast.26, f32[512,512]{1,0:T(8,128)} %get-tuple-element.32.refs_2_.refs_3_, f32[8,256,512]{2,1,0:T(8,128)} %bitcast.29, f32[8,256,512]{2,1,0:T(8,128)} %bitcast.30, ...), custom_call_target="tpu_custom_call" | custom-call | flops 100000000376832 | bytes 1 | tf_op jit(solution)/shard_map/pallas_call | solution.py:35
  176.2 3.2 %collective-permute-start.13 = (f32[2,2,256,512]{3,2,1,0:T(8,128)}, f32[2,2,256,512]{3,2,1,0:T(8,128)}, u32[]{:S(2)}, u32[]{:S(2)}) collective-permute-start(f32[2,2,256,512]{3,2,1,0:T(8,128)} %get-tuple-element.50.refs_3_.refs_4_), channel_id=1, source_target_pairs={{8,24},{9,25},{10,26},{11,27},{12,28},{13,29},{14,30},{15,31},{24,... | collective-permute-start | bytes 6291464 | tf_op jit(solution)/shard_map/ppermute | solution.py:266
  179.4 1.9 collective-permute-start.15
  181.3 6.1 %shard_map.91.refs_7_ = f32[1024,512]{1,0:T(8,128)} custom-call(s32[45]{0:T(128)} %concatenate.3.refs_0_, f32[2048,256]{1,0:T(8,128)} %get-tuple-element.43.refs_9_.refs_1_, f32[2048,256]{1,0:T(8,128)} %get-tuple-element.48.refs_2_, f32[2048,256]{1,0:T(8,128)} %collective-permute-done.11.refs_12_.refs_3_, ...), custom_call_target="tpu_custom_call" | custom-call | flops 100000000376832 | bytes 1 | tf_op jit(solution)/shard_map/pallas_call | solution.py:35
  187.4 6.1 %shard_map.92.refs_2_ = f32[1024,512]{1,0:T(8,128)} custom-call(s32[45]{0:T(128)} %concatenate.3.refs_0_, f32[2048,256]{1,0:T(8,128)} %get-tuple-element.43.refs_9_.refs_1_, f32[2048,256]{1,0:T(8,128)} %get-tuple-element.48.refs_2_, f32[2048,256]{1,0:T(8,128)} %collective-permute-done.11.refs_12_.refs_3_, ...), custom_call_target="tpu_custom_call" | custom-call | flops 100000000376832 | bytes 1 | tf_op jit(solution)/shard_map/pallas_call | solution.py:35
  193.5 1.3 collective-permute-done.14.refs_1_
  194.8 0.7 shard_map.93.refs_5_.refs_6_
  195.5 25.2 %all-gather.11.cloned.1.call-done = f32[2048,512]{1,0:T(8,128)} async-done(((f32[256,512]{1,0:T(8,128)}), f32[2048,512]{1,0:T(8,128)}) %all-gather.11.cloned.1.call-update) | async-done | bytes 4194320 | tf_op jit(solution)/shard_map/all_gather | solution.py:312
  220.6 6.4 %shard_map.94 = (f32[6,256,256]{2,1,0:T(8,128)}, f32[6,256,256]{2,1,0:T(8,128)}) custom-call(s32[45]{0:T(128)} %concatenate.3.refs_0_, f32[8,256,512]{2,1,0:T(8,128)} %bitcast.31, f32[8,256,512]{2,1,0:T(8,128)} %bitcast.32, f32[2,2,256,512]{3,2,1,0:T(8,128)} %get-tuple-element.51.refs_3_.refs_4_, f32[2,2,256,512]{3,2,1,0:T(8,128)} %get-tuple-element.51.refs_3_.refs_4_, ...), custom_call_target="tpu_custom_call" | custom-call | flops 100000000376832 | bytes 1 | tf_op jit(solution)/shard_map/pallas_call | solution.py:35
  227.1 2.2 collective-permute-start.20
  229.2 3.4 %collective-permute-start.19 = (f32[6,256,256]{2,1,0:T(8,128)}, f32[6,256,256]{2,1,0:T(8,128)}, u32[]{:S(2)}, u32[]{:S(2)}) collective-permute-start(f32[6,256,256]{2,1,0:T(8,128)} %get-tuple-element.58.refs_2_), channel_id=1, source_target_pairs={{0,1},{1,2},{2,3},{3,4},{4,5},{5,6},{6,7},{7,8},{8,9},{9,10},{10,1... | collective-permute-start | bytes 4718600 | tf_op jit(solution)/shard_map/ppermute | solution.py:266
  232.6 7.1 %collective-permute-done.13.refs_5_.refs_6_ = f32[2,2,256,512]{3,2,1,0:T(8,128)} collective-permute-done((f32[2,2,256,512]{3,2,1,0:T(8,128)}, f32[2,2,256,512]{3,2,1,0:T(8,128)}, u32[]{:S(2)}, u32[]{:S(2)}) %collective-permute-start.13) | collective-permute-done | bytes 2097184 | tf_op jit(solution)/shard_map/ppermute | solution.py:266
  239.7 5.7 %shard_map.95 = (f32[4,256,256]{2,1,0:T(8,128)}, f32[4,256,256]{2,1,0:T(8,128)}) custom-call(s32[45]{0:T(128)} %concatenate.3.refs_0_, f32[8,256,512]{2,1,0:T(8,128)} %bitcast.33, f32[8,256,512]{2,1,0:T(8,128)} %bitcast.34, f32[2,2,256,512]{3,2,1,0:T(8,128)} %get-tuple-element.50.refs_3_.refs_4_, f32[2,2,256,512]{3,2,1,0:T(8,128)} %get-tuple-element.50.refs_3_.refs_4_, ...), custom_call_target="tpu_custom_call" | custom-call | flops 100000000376832 | bytes 1 | tf_op jit(solution)/shard_map/pallas_call | solution.py:35
  245.4 3.6 %collective-permute-start.18 = (f32[4,256,256]{2,1,0:T(8,128)}, f32[4,256,256]{2,1,0:T(8,128)}, u32[]{:S(2)}, u32[]{:S(2)}) collective-permute-start(f32[4,256,256]{2,1,0:T(8,128)} %get-tuple-element.56.refs_11_.refs_1_.refs_7_), channel_id=1, source_target_pairs={{8,7},{9,8},{10,9},{11,10},{12,11},{13,12},{14,13},{15,14},{24,23}... | collective-permute-start | bytes 3145736 | tf_op jit(solution)/shard_map/ppermute | solution.py:266
  249.0 4.8 %collective-permute-start.17 = (f32[4,256,256]{2,1,0:T(8,128)}, f32[4,256,256]{2,1,0:T(8,128)}, u32[]{:S(2)}, u32[]{:S(2)}) collective-permute-start(f32[4,256,256]{2,1,0:T(8,128)} %get-tuple-element.57.refs_2_), channel_id=1, source_target_pairs={{8,9},{9,10},{10,11},{11,12},{12,13},{13,14},{14,15},{24,25},{25,2... | collective-permute-start | bytes 3145736 | tf_op jit(solution)/shard_map/ppermute | solution.py:266
  253.8 23.4 %collective-permute-done.20.refs_6_.refs_5_.refs_7_.refs_4_ = f32[6,256,256]{2,1,0:T(8,128)} collective-permute-done((f32[6,256,256]{2,1,0:T(8,128)}, f32[6,256,256]{2,1,0:T(8,128)}, u32[]{:S(2)}, u32[]{:S(2)}) %collective-permute-start.20) | collective-permute-done | bytes 1572896 | tf_op jit(solution)/shard_map/ppermute | solution.py:266
  277.2 2.4 broadcast_in_dim.7.refs_3_
  279.6 7.1 %shard_map.96.refs_10_ = f32[4096,512]{1,0:T(8,128)} custom-call(s32[45]{0:T(128)} %concatenate.3.refs_0_, f32[8,256,256]{2,1,0:T(8,128)} %get-tuple-element.49.refs_6_.refs_1_.refs_7_.refs_10_, f32[8,256,256]{2,1,0:T(8,128)} %get-tuple-element.55.refs_2_, f32[16,256,256]{2,1,0:T(8,128)} %broadcast_in_dim.7.refs_3_, ...), custom_call_target="tpu_custom_call" | custom-call | flops 100000000376832 | bytes 1 | tf_op jit(solution)/shard_map/pallas_call | solution.py:35
  286.7 6.7 %shard_map.97.refs_7_ = f32[4096,512]{1,0:T(8,128)} custom-call(s32[45]{0:T(128)} %concatenate.3.refs_0_, f32[6,256,256]{2,1,0:T(8,128)} %get-tuple-element.54.refs_7_.refs_1_, f32[6,256,256]{2,1,0:T(8,128)} %get-tuple-element.58.refs_2_, f32[8,256,256]{2,1,0:T(8,128)} %collective-permute-done.15.refs_8_.refs_4_.refs_3_, ...), custom_call_target="tpu_custom_call", output_to_operand_aliasing={{}: (10, {})} | custom-call | flops 100000000376832 | bytes 1 | tf_op jit(solution)/shard_map/pallas_call | solution.py:35
  293.5 3.7 %shard_map.98.refs_10_ = f32[4096,512]{1,0:T(8,128)} custom-call(s32[45]{0:T(128)} %concatenate.3.refs_0_, f32[256,512]{1,0:T(8,128)} %get-tuple-element.53.refs_7_.refs_1_, f32[6,256,256]{2,1,0:T(8,128)} %collective-permute-done.19.refs_4_.refs_2_.refs_3_, ...), custom_call_target="tpu_custom_call", output_to_operand_aliasing={{}: (7, {})} | custom-call | flops 100000000376832 | bytes 1 | tf_op jit(solution)/shard_map/pallas_call | solution.py:35
  297.1 6.7 %shard_map.99.refs_10_ = f32[4096,512]{1,0:T(8,128)} custom-call(s32[45]{0:T(128)} %concatenate.3.refs_0_, f32[8,256,256]{2,1,0:T(8,128)} %get-tuple-element.49.refs_6_.refs_1_.refs_7_.refs_10_, f32[8,256,256]{2,1,0:T(8,128)} %get-tuple-element.55.refs_2_, f32[16,256,256]{2,1,0:T(8,128)} %broadcast_in_dim.7.refs_3_, ...), custom_call_target="tpu_custom_call", output_to_operand_aliasing={{}: (10, {})} | custom-call | flops 100000000376832 | bytes 1 | tf_op jit(solution)/shard_map/pallas_call | solution.py:35
  303.8 7.2 %shard_map.100 = f32[4096,512]{1,0:T(8,128)} custom-call(s32[45]{0:T(128)} %concatenate.3.refs_0_, f32[4,256,256]{2,1,0:T(8,128)} %get-tuple-element.56.refs_11_.refs_1_.refs_7_, f32[4,256,256]{2,1,0:T(8,128)} %get-tuple-element.57.refs_2_, f32[8,256,256]{2,1,0:T(8,128)} %collective-permute-done.15.refs_8_.refs_4_.refs_3_, ...), custom_call_target="tpu_custom_call", output_to_operand_aliasing={{}: (10, {})} | custom-call | flops 100000000376832 | bytes 1 | tf_op jit(solution)/shard_map/pallas_call | solution.py:35
  (25 shorter events, 0.3 us)
Async XLA Ops:
  7.2 2.8 copy-start.2
  7.2 53.6 %all-gather.7.cloned.1.call-start = ((), (), s32[]{:S(2)}) async-start(), calls=%async_computation | async-start | bytes 4718592 | tf_op jit(solution)/shard_map/all_gather | solution.py:312
  8.5 4.6 %collective-permute-start = (f32[512,512]{1,0:T(8,128)S(1)}, f32[512,512]{1,0:T(8,128)S(1)}, u32[]{:S(2)}, u32[]{:S(2)}) collective-permute-start(f32[512,512]{1,0:T(8,128)S(1)} %slice_bitcast_fusion), channel_id=1, source_target_pairs={{0,1},{2,3},{4,5},{6,7},{8,9},{10,11},{12,13},{14,15},{17,16},{19,... | collective-permute-start | bytes 3145736 | tf_op jit(solution)/shard_map/ppermute | solution.py:266
  13.1 1.0 copy-start.1
  18.9 118.6 %all-gather.9.cloned.1.call-start = ((), (), s32[]{:S(2)}) async-start(), calls=%async_computation.1 | async-start | bytes 4718592 | tf_op jit(solution)/shard_map/all_gather | solution.py:312
  19.0 51.0 %collective-permute-start.5 = (f32[256,512]{1,0:T(8,128)}, f32[256,512]{1,0:T(8,128)}, u32[]{:S(2)}, u32[]{:S(2)}) collective-permute-start(f32[256,512]{1,0:T(8,128)} %get-tuple-element.36), channel_id=1, source_target_pairs={{0,8},{1,9},{2,10},{3,11},{4,12},{5,13},{6,14},{7,15},{16,24},{17,... | collective-permute-start | bytes 1572872 | tf_op jit(solution)/shard_map/ppermute | solution.py:266
  20.3 25.0 %collective-permute-start.1 = (f32[256,512]{1,0:T(8,128)}, f32[256,512]{1,0:T(8,128)}, u32[]{:S(2)}, u32[]{:S(2)}) collective-permute-start(f32[256,512]{1,0:T(8,128)} %get-tuple-element.31.refs_1_), channel_id=1, source_target_pairs={{0,2},{1,3},{2,0},{3,1},{4,6},{5,7},{6,4},{7,5},{8,10},{9,11},{10,... | collective-permute-start | bytes 1572872 | tf_op jit(solution)/shard_map/ppermute | solution.py:266
  21.6 31.2 %collective-permute-start.2 = (f32[512,256]{1,0:T(8,128)}, f32[512,256]{1,0:T(8,128)}, u32[]{:S(2)}, u32[]{:S(2)}) collective-permute-start(f32[512,256]{1,0:T(8,128)} %get-tuple-element.35), channel_id=1, source_target_pairs={{0,1},{1,2},{2,3},{3,4},{4,5},{5,6},{6,7},{7,8},{8,9},{9,10},{10,1... | collective-permute-start | bytes 1572872 | tf_op jit(solution)/shard_map/ppermute | solution.py:266
  30.6 28.5 %collective-permute-start.4 = (f32[1,2,256,512]{3,2,1,0:T(8,128)}, f32[1,2,256,512]{3,2,1,0:T(8,128)}, u32[]{:S(2)}, u32[]{:S(2)}) collective-permute-start(f32[1,2,256,512]{3,2,1,0:T(8,128)} %get-tuple-element.37.refs_3_.refs_4_), channel_id=1, source_target_pairs={{6,22},{7,23},{14,30},{15,31},{23,7},{31,15}} | collective-permute-start | bytes 3145736 | tf_op jit(solution)/shard_map/ppermute | solution.py:266
  52.8 4.4 %copy-start = (s32[256]{0:T(256)S(1)}, s32[256]{0:T(256)}, u32[]{:S(2)}) copy-start(s32[256]{0:T(256)} %iota_add_fusion) | copy-start | bytes 3076
  55.9 14.8 %collective-permute-start.6 = (f32[2,256,512]{2,1,0:T(8,128)}, f32[2,256,512]{2,1,0:T(8,128)}, u32[]{:S(2)}, u32[]{:S(2)}) collective-permute-start(f32[2,256,512]{2,1,0:T(8,128)} %shard_map.78.refs_6_.refs_1_.refs_9_), channel_id=1, source_target_pairs={{0,1},{1,0},{2,3},{3,2},{4,5},{5,4},{6,7},{7,6},{8,9},{9,8},{10,11... | collective-permute-start | bytes 3145736 | tf_op jit(solution)/shard_map/ppermute | solution.py:266
  55.9 27.1 %collective-permute-start.3 = (f32[2,256,512]{2,1,0:T(8,128)}, f32[2,256,512]{2,1,0:T(8,128)}, u32[]{:S(2)}, u32[]{:S(2)}) collective-permute-start(f32[2,256,512]{2,1,0:T(8,128)} %shard_map.78.refs_6_.refs_1_.refs_9_), channel_id=1, source_target_pairs={{0,4},{1,5},{2,6},{3,7},{4,8},{5,9},{6,10},{7,11},{8,12},{9,13},{1... | collective-permute-start | bytes 3145736 | tf_op jit(solution)/shard_map/ppermute | solution.py:266
  66.4 26.2 %collective-permute-start.8 = (f32[1,2,256,512]{3,2,1,0:T(8,128)}, f32[1,2,256,512]{3,2,1,0:T(8,128)}, u32[]{:S(2)}, u32[]{:S(2)}) collective-permute-start(f32[1,2,256,512]{3,2,1,0:T(8,128)} %get-tuple-element.40.refs_3_.refs_4_), channel_id=1, source_target_pairs={{4,20},{5,21},{6,22},{7,23},{12,28},{13,29},{14,30},{15,31},{21,5}... | collective-permute-start | bytes 3145736 | tf_op jit(solution)/shard_map/ppermute | solution.py:266
  84.4 12.7 %collective-permute-start.9 = (f32[2,256,512]{2,1,0:T(8,128)}, f32[2,256,512]{2,1,0:T(8,128)}, u32[]{:S(2)}, u32[]{:S(2)}) collective-permute-start(f32[2,256,512]{2,1,0:T(8,128)} %shard_map.82.refs_2_.refs_1_), channel_id=1, source_target_pairs={{0,1},{1,0},{2,3},{3,2},{4,5},{5,4},{6,7},{7,6},{8,9},{9,8},{10,11... | collective-permute-start | bytes 3145736 | tf_op jit(solution)/shard_map/ppermute | solution.py:266
  85.5 135.1 %all-gather.11.cloned.1.call-start = ((), (), s32[]{:S(2)}) async-start(), calls=%async_computation.2 | async-start | bytes 4718592 | tf_op jit(solution)/shard_map/all_gather | solution.py:312
  85.6 52.0 %collective-permute-start.10 = (f32[2,2,256,512]{3,2,1,0:T(8,128)}, f32[2,2,256,512]{3,2,1,0:T(8,128)}, u32[]{:S(2)}, u32[]{:S(2)}) collective-permute-start(f32[2,2,256,512]{3,2,1,0:T(8,128)} %get-tuple-element.45.refs_3_.refs_4_), channel_id=1, source_target_pairs={{0,16},{1,17},{2,18},{3,19},{4,20},{5,21},{6,22},{7,23},{8,24},{9,... | collective-permute-start | bytes 6291464 | tf_op jit(solution)/shard_map/ppermute | solution.py:266
  89.3 60.3 %collective-permute-start.7 = (f32[256,512]{1,0:T(8,128)}, f32[256,512]{1,0:T(8,128)}, u32[]{:S(2)}, u32[]{:S(2)}) collective-permute-start(f32[256,512]{1,0:T(8,128)} %shard_map.83.refs_7_), channel_id=1, source_target_pairs={{0,8},{1,9},{2,10},{3,11},{4,12},{5,13},{6,14},{7,15},{16,24},{17,... | collective-permute-start | bytes 1572872 | tf_op jit(solution)/shard_map/ppermute | solution.py:266
  105.5 44.8 %collective-permute-start.11 = (f32[2048,256]{1,0:T(8,128)}, f32[2048,256]{1,0:T(8,128)}, u32[]{:S(2)}, u32[]{:S(2)}) collective-permute-start(f32[2048,256]{1,0:T(8,128)} %get-tuple-element.48.refs_2_), channel_id=1, source_target_pairs={{0,1},{1,2},{2,3},{3,4},{4,5},{5,6},{6,7},{7,8},{8,9},{9,10},{10,1... | collective-permute-start | bytes 6291464 | tf_op jit(solution)/shard_map/ppermute | solution.py:266
  112.2 55.7 %collective-permute-start.12 = (f32[2048,256]{1,0:T(8,128)}, f32[2048,256]{1,0:T(8,128)}, u32[]{:S(2)}, u32[]{:S(2)}) collective-permute-start(f32[2048,256]{1,0:T(8,128)} %get-tuple-element.43.refs_9_.refs_1_), channel_id=1, source_target_pairs={{1,0},{2,1},{3,2},{4,3},{5,4},{6,5},{7,6},{8,7},{9,8},{10,9},{11,1... | collective-permute-start | bytes 6291464 | tf_op jit(solution)/shard_map/ppermute | solution.py:266
  145.5 49.3 %collective-permute-start.14 = (f32[2,2,256,512]{3,2,1,0:T(8,128)}, f32[2,2,256,512]{3,2,1,0:T(8,128)}, u32[]{:S(2)}, u32[]{:S(2)}) collective-permute-start(f32[2,2,256,512]{3,2,1,0:T(8,128)} %get-tuple-element.51.refs_3_.refs_4_), channel_id=1, source_target_pairs={{8,24},{9,25},{10,26},{11,27},{12,28},{13,29},{14,30},{15,31},{24,... | collective-permute-start | bytes 6291464 | tf_op jit(solution)/shard_map/ppermute | solution.py:266
  156.5 83.2 %collective-permute-start.16 = (f32[8,256,256]{2,1,0:T(8,128)}, f32[8,256,256]{2,1,0:T(8,128)}, u32[]{:S(2)}, u32[]{:S(2)}) collective-permute-start(f32[8,256,256]{2,1,0:T(8,128)} %get-tuple-element.49.refs_6_.refs_1_.refs_7_.refs_10_), channel_id=1, source_target_pairs={{1,0},{2,1},{3,2},{4,3},{5,4},{6,5},{7,6},{8,7},{9,8},{10,9},{11,1... | collective-permute-start | bytes 6291464 | tf_op jit(solution)/shard_map/ppermute | solution.py:266
  176.2 63.5 %collective-permute-start.13 = (f32[2,2,256,512]{3,2,1,0:T(8,128)}, f32[2,2,256,512]{3,2,1,0:T(8,128)}, u32[]{:S(2)}, u32[]{:S(2)}) collective-permute-start(f32[2,2,256,512]{3,2,1,0:T(8,128)} %get-tuple-element.50.refs_3_.refs_4_), channel_id=1, source_target_pairs={{8,24},{9,25},{10,26},{11,27},{12,28},{13,29},{14,30},{15,31},{24,... | collective-permute-start | bytes 6291464 | tf_op jit(solution)/shard_map/ppermute | solution.py:266
  179.4 60.3 %collective-permute-start.15 = (f32[8,256,256]{2,1,0:T(8,128)}, f32[8,256,256]{2,1,0:T(8,128)}, u32[]{:S(2)}, u32[]{:S(2)}) collective-permute-start(f32[8,256,256]{2,1,0:T(8,128)} %get-tuple-element.55.refs_2_), channel_id=1, source_target_pairs={{0,1},{1,2},{2,3},{3,4},{4,5},{5,6},{6,7},{7,8},{8,9},{9,10},{10,1... | collective-permute-start | bytes 6291464 | tf_op jit(solution)/shard_map/ppermute | solution.py:266
  227.1 50.1 %collective-permute-start.20 = (f32[6,256,256]{2,1,0:T(8,128)}, f32[6,256,256]{2,1,0:T(8,128)}, u32[]{:S(2)}, u32[]{:S(2)}) collective-permute-start(f32[6,256,256]{2,1,0:T(8,128)} %get-tuple-element.54.refs_7_.refs_1_), channel_id=1, source_target_pairs={{1,0},{2,1},{3,2},{4,3},{5,4},{6,5},{7,6},{8,7},{9,8},{10,9},{11,1... | collective-permute-start | bytes 4718600 | tf_op jit(solution)/shard_map/ppermute | solution.py:266
  229.2 57.5 %collective-permute-start.19 = (f32[6,256,256]{2,1,0:T(8,128)}, f32[6,256,256]{2,1,0:T(8,128)}, u32[]{:S(2)}, u32[]{:S(2)}) collective-permute-start(f32[6,256,256]{2,1,0:T(8,128)} %get-tuple-element.58.refs_2_), channel_id=1, source_target_pairs={{0,1},{1,2},{2,3},{3,4},{4,5},{5,6},{6,7},{7,8},{8,9},{9,10},{10,1... | collective-permute-start | bytes 4718600 | tf_op jit(solution)/shard_map/ppermute | solution.py:266
  245.4 51.7 %collective-permute-start.18 = (f32[4,256,256]{2,1,0:T(8,128)}, f32[4,256,256]{2,1,0:T(8,128)}, u32[]{:S(2)}, u32[]{:S(2)}) collective-permute-start(f32[4,256,256]{2,1,0:T(8,128)} %get-tuple-element.56.refs_11_.refs_1_.refs_7_), channel_id=1, source_target_pairs={{8,7},{9,8},{10,9},{11,10},{12,11},{13,12},{14,13},{15,14},{24,23}... | collective-permute-start | bytes 3145736 | tf_op jit(solution)/shard_map/ppermute | solution.py:266
  249.0 54.8 %collective-permute-start.17 = (f32[4,256,256]{2,1,0:T(8,128)}, f32[4,256,256]{2,1,0:T(8,128)}, u32[]{:S(2)}, u32[]{:S(2)}) collective-permute-start(f32[4,256,256]{2,1,0:T(8,128)} %get-tuple-element.57.refs_2_), channel_id=1, source_target_pairs={{8,9},{9,10},{10,11},{11,12},{12,13},{13,14},{14,15},{24,25},{25,2... | collective-permute-start | bytes 3145736 | tf_op jit(solution)/shard_map/ppermute | solution.py:266
Sparse Core Ops, SparseCore 0:
  19.0 41.6 all-gather.6
  85.6 49.8 all-gather.8
  150.4 70.1 all-gather.10

commit v3 on v2

--- a/solution.py
+++ b/solution.py
@@ -155,8 +155,9 @@
     out[:, half:] = dot3(wide(mine_right, right_in), (cur_h[...], cur_l[...]))
 
 
-def third_kernel(begin, last_unit, slots, info, left, right, up_far, up_near, down_near, down_far, down_last, prev, cur, held, out, *scratch):
+def third_kernel(begin, last_unit, slots, none_far, again, info, left, right, up_far, up_near, down_near, down_far, down_last, prev, cur, held, out, *scratch):
     del held
+    wanted = (info[LAST_IN] == 1) | (not again)
     *scratch, made, sems = scratch
     e, count = pl.program_id(0), made.shape[0]
     half = left.shape[1]
@@ -175,20 +176,21 @@
     def flat(ref):
         return ref[...].reshape(2 * half, half)
 
-    left_in = jnp.where(info[FIRST_IN] == 1, flat(up_far), flat(up_near))
+    before = jnp.zeros((2 * half, half), jnp.float32) if none_far else flat(up_far)
+    left_in = jnp.where(info[FIRST_IN] == 1, before, flat(up_near))
     far = flat(down_far)
     ends_here = (info[USE_LAST] == 1) & (begin + e == last_unit)
     far = jnp.concatenate([far[:half], jnp.where(ends_here, down_last[...], far[half:])], axis=0)
     right_in = jnp.where(info[LAST_IN] == 1, far, flat(down_near))
     for unit in range(count):
 
-        @pl.when(e == unit)
+        @pl.when((e == unit) & wanted)
         def _():
             columns(left_in, flat(left), flat(right), right_in, scratch, made.at[unit])
             for copy in copies(unit):
                 copy.start()
 
-    @pl.when(e == count - 1)
+    @pl.when((e == count - 1) & wanted)
     def _():
         for unit in range(count):
             for copy in copies(unit):
@@ -472,18 +474,19 @@
 
     lefts, rights, ups, downs = ([None] * slots for _ in range(4))
 
-    def third_step(batch, held, after):
+    def third_step(batch, held, after, early, again):
         begin = batch[0]
         fresh = held is None
         parts = [lefts[begin], rights[begin]]
-        parts.append(ups[begin - fold] if begin >= fold else (no_strips, 0))
-        parts += [ups[begin], downs[begin], downs[(begin + fold) % slots]]
-        piece = lambda at: pl.BlockSpec((2, half, half), lambda e, f: (at + e, 0, 0))
+        parts.append(ups[begin - fold] if begin >= fold else ups[begin])
+        parts += [ups[begin], downs[begin], downs[begin if early else (begin + fold) % slots]]
+        step = lambda e, f: e * f[LAST_IN] if again else e
+        piece = lambda at: pl.BlockSpec((2, half, half), lambda e, f: (at + step(e, f), 0, 0))
         args = [array for array, _ in parts]
         ending = slots - fold in batch
         tail_row = 2 * ending_strips[2] if ending else 0
         return call(
-            functools.partial(third_kernel, begin, slots - fold, slots),
+            functools.partial(third_kernel, begin, slots - fold, slots, begin < fold, again),
             info,
             (len(batch),),
             [piece(at) for _, at in parts]
@@ -522,7 +525,6 @@
         )
 
     tops, sent, got, made = [jnp.zeros((half, window), f32)], {}, {}, {}
-    no_strips = jnp.zeros((2 * slots, half, half), f32)
 
     def do_first(batch, after=()):
         sent[batch[0]], top = first_step(batch, tops[-1], paired, after)
@@ -553,8 +555,8 @@
 
     out = [None]
 
-    def do_third(batch, after=()):
-        out[0] = third_step(batch, out[0], after)
+    def do_third(batch, early=False, again=False):
+        out[0] = third_step(batch, out[0], (), early, again)
         last.append(out[0])
 
     def do_last():
@@ -601,12 +603,14 @@
         do_rows_end(1)
         got[4] = [placed(got[4][0])]
         ending_strips = do_second([4, 5], [4, 5], ended=[tops[-1]])
-        do_second([6, 7], [6, 7], after=[ups[0][0], downs[0][0]])
-        do_third([0, 1])
+        do_third([0, 1], early=True)
+        do_second([6, 7], [6, 7])
+        do_third([2, 3], early=True)
         do_third([4, 5])
+        do_third([0, 1], again=True)
         do_last()
-        do_third([2, 3])
         do_third([6, 7])
+        do_third([2, 3], again=True)
     else:
         _, prev = previous(prev_own)
         parts = do_rows()

time: 319 us -> 312 us (0.978)
  waiting for transfers between devices: 113 us -> 97.4 us
  Pallas kernels: 126 us -> 134 us
    all_gather x3, waiting for transfers between devices: 26.8 us -> 16 us  [gathered(): mine = lax.all_gather(value, 'pcol', axis_index_groups=teams)]
    pallas_call x25 -> x27, Pallas kernels: 126 us -> 134 us  [call(): pl.pallas_call(run, grid_spec=pltpu.PrefetchScalarGridSpec(num_scalar_pre...]
    ppermute x21, waiting for transfers between devices: 86.6 us -> 81.4 us  [send(): lax.ppermute(value, GRID, [(a * cols + b, c * cols + d) for (a, b), (c, d...]
  transfers between devices with their start and end apart: 24 -> 24, of which waited for: 12 -> 10; matrix products, arithmetic and copies ran while one was open for 2% -> 1% of each run, Pallas kernels for 36% -> 38%
where the time goes in v3:
time: 312 us; the launch traced here: 310 us
  Pallas kernels  134 us (43%)
  waiting for transfers between devices  97.4 us (31%)
  starting transfers between devices  58.2 us (19%)
  between operations  14.2 us (5%)
  local copies, waits for them, and re-layouts  3.83 us (1%)
    pallas_call x27, Pallas kernels, call(): pl.pallas_call(run, grid_spec=pltpu.PrefetchScalarGridSpec(num_scalar_pre...  134 us
    ppermute x21, waiting for transfers between devices, send(): lax.ppermute(value, GRID, [(a * cols + b, c * cols + d) for (a, b), (c, d...  81.4 us
    ppermute x21, starting transfers between devices, send(): lax.ppermute(value, GRID, [(a * cols + b, c * cols + d) for (a, b), (c, d...  58 us
    all_gather x3, waiting for transfers between devices, gathered(): mine = lax.all_gather(value, 'pcol', axis_index_groups=teams)  16 us
  transfers between devices with their start and end apart: 24, of which 10 were waited for; matrix products, arithmetic and copies ran while one was open for 1% of the time, Pallas kernels for 38%

profile of v3, /device:TPU:25, one launch (start us, length us, event | category | flops | bytes accessed | tf_op | source)
XLA Modules:
  0.0 309.7 jit_solution(6566953563787064673)
XLA Ops:
  7.2 1.3 slice_bitcast_fusion
  8.5 1.3 collective-permute-start
  9.9 0.1 reshape.15
  10.0 0.6 concatenate.3.refs_0_
  10.6 0.6 iota_add_fusion
  11.2 1.9 collective-permute-done.refs_2_
  13.1 1.0 copy-done.1
  14.0 4.8 %shard_map.76 = (f32[512,512]{1,0:T(8,128)}, f32[2,256,512]{2,1,0:T(8,128)}, f32[256,512]{1,0:T(8,128)}, f32[256,512]{1,0:T(8,128)}, f32[512,256]{1,0:T(8,128)}, /*index=5*/f32[512,256]{1,0:T(8,128)}) custom-call(s32[45]{0:T(128)} %concatenate.3.refs_0_, f32[2,1,512,512]{3,2,1,0:T(8,128)} %refs_1_.2, f32[512,512]{1,0:T(8,128)} %copy-done.1), custom_call_target="tpu_custom_call" | custom-call | flops 100000000376832 | bytes 1 | tf_op jit(solution)/shard_map/pallas_call | solution.py:35
  19.0 1.3 collective-permute-start.5
  20.3 3.2 %collective-permute-start.2 = (f32[512,256]{1,0:T(8,128)}, f32[512,256]{1,0:T(8,128)}, u32[]{:S(2)}, u32[]{:S(2)}) collective-permute-start(f32[512,256]{1,0:T(8,128)} %get-tuple-element.35), channel_id=1, source_target_pairs={{0,1},{1,2},{2,3},{3,4},{4,5},{5,6},{6,7},{7,8},{8,9},{9,10},{10,1... | collective-permute-start | bytes 1572872 | tf_op jit(solution)/shard_map/ppermute | solution.py:268
  23.4 0.1 collective-permute-start.1
  23.5 0.9 broadcast_in_dim.3.refs_5_
  24.4 5.8 %shard_map.77 = (f32[1,2,256,512]{3,2,1,0:T(8,128)}, f32[256,512]{1,0:T(8,128)}) custom-call(s32[45]{0:T(128)} %concatenate.3.refs_0_, f32[4096,512]{1,0:T(8,128)} %bitcast.22, f32[512,512]{1,0:T(8,128)} %get-tuple-element.32.refs_2_.refs_3_, f32[2,256,512]{2,1,0:T(8,128)} %get-tuple-element.33.refs_3_.refs_4_, ...), custom_call_target="tpu_custom_call" | custom-call | flops 100000000376832 | bytes 1 | tf_op jit(solution)/shard_map/pallas_call | solution.py:35
  30.1 1.6 collective-permute-start.4
  31.8 7.8 %collective-permute-done.2.refs_4_ = f32[512,256]{1,0:T(8,128)} collective-permute-done((f32[512,256]{1,0:T(8,128)}, f32[512,256]{1,0:T(8,128)}, u32[]{:S(2)}, u32[]{:S(2)}) %collective-permute-start.2) | collective-permute-done | bytes 524320 | tf_op jit(solution)/shard_map/ppermute | solution.py:268
  39.5 17.9 %collective-permute-done.1.refs_2_ = f32[256,512]{1,0:T(8,128)} collective-permute-done((f32[256,512]{1,0:T(8,128)}, f32[256,512]{1,0:T(8,128)}, u32[]{:S(2)}, u32[]{:S(2)}) %collective-permute-start.1) | collective-permute-done | bytes 524320 | tf_op jit(solution)/shard_map/ppermute | solution.py:268
  57.4 3.1 shard_map.78.refs_6_.refs_1_.refs_9_
  60.5 1.3 collective-permute-start.3
  61.8 1.9 convert_select_fusion.refs_5_.refs_8_
  63.7 5.6 %shard_map.79 = (f32[1,2,256,512]{3,2,1,0:T(8,128)}, f32[256,512]{1,0:T(8,128)}) custom-call(s32[45]{0:T(128)} %concatenate.3.refs_0_, f32[4096,512]{1,0:T(8,128)} %bitcast.23, f32[512,512]{1,0:T(8,128)} %get-tuple-element.32.refs_2_.refs_3_, f32[8,256,512]{2,1,0:T(8,128)} %bitcast.35, f32[8,256,512]{2,1,0:T(8,128)} %bitcast.36, ...), custom_call_target="tpu_custom_call" | custom-call | flops 100000000376832 | bytes 1 | tf_op jit(solution)/shard_map/pallas_call | solution.py:35
  69.3 0.7 shard_map.80.refs_6_
  70.1 4.2 %collective-permute-start.9 = (f32[1,2,256,512]{3,2,1,0:T(8,128)}, f32[1,2,256,512]{3,2,1,0:T(8,128)}, u32[]{:S(2)}, u32[]{:S(2)}) collective-permute-start(f32[1,2,256,512]{3,2,1,0:T(8,128)} %get-tuple-element.41.refs_3_.refs_4_), channel_id=1, source_target_pairs={{4,20},{5,21},{6,22},{7,23},{12,28},{13,29},{14,30},{15,31},{21,5}... | collective-permute-start | bytes 3145736 | tf_op jit(solution)/shard_map/ppermute | solution.py:268
  74.3 7.9 %shard_map.81 = (f32[2,2,256,512]{3,2,1,0:T(8,128)}, f32[256,512]{1,0:T(8,128)}) custom-call(s32[45]{0:T(128)} %concatenate.3.refs_0_, f32[4096,512]{1,0:T(8,128)} %bitcast.24, f32[512,512]{1,0:T(8,128)} %get-tuple-element.32.refs_2_.refs_3_, f32[8,256,512]{2,1,0:T(8,128)} %bitcast.37, f32[8,256,512]{2,1,0:T(8,128)} %bitcast.38, ...), custom_call_target="tpu_custom_call" | custom-call | flops 100000000376832 | bytes 1 | tf_op jit(solution)/shard_map/pallas_call | solution.py:35
  82.2 4.7 %collective-permute-done.3.refs_1_ = f32[2,256,512]{2,1,0:T(8,128)} collective-permute-done((f32[2,256,512]{2,1,0:T(8,128)}, f32[2,256,512]{2,1,0:T(8,128)}, u32[]{:S(2)}, u32[]{:S(2)}) %collective-permute-start.3) | collective-permute-done | bytes 1048608 | tf_op jit(solution)/shard_map/ppermute | solution.py:268
  86.9 0.7 shard_map.82.refs_2_.refs_1_
  87.6 0.7 shard_map.83.refs_7_
  88.3 3.1 %collective-permute-start.7 = (f32[2,256,512]{2,1,0:T(8,128)}, f32[2,256,512]{2,1,0:T(8,128)}, u32[]{:S(2)}, u32[]{:S(2)}) collective-permute-start(f32[2,256,512]{2,1,0:T(8,128)} %shard_map.82.refs_2_.refs_1_), channel_id=1, source_target_pairs={{0,1},{1,0},{2,3},{3,2},{4,5},{5,4},{6,7},{7,6},{8,9},{9,8},{10,11... | collective-permute-start | bytes 3145736 | tf_op jit(solution)/shard_map/ppermute | solution.py:268
  91.4 1.3 collective-permute-start.10
  92.7 5.3 %collective-permute-start.8 = (f32[2,2,256,512]{3,2,1,0:T(8,128)}, f32[2,2,256,512]{3,2,1,0:T(8,128)}, u32[]{:S(2)}, u32[]{:S(2)}) collective-permute-start(f32[2,2,256,512]{3,2,1,0:T(8,128)} %get-tuple-element.40.refs_3_.refs_4_), channel_id=1, source_target_pairs={{0,16},{1,17},{2,18},{3,19},{4,20},{5,21},{6,22},{7,23},{8,24},{9,... | collective-permute-start | bytes 6291464 | tf_op jit(solution)/shard_map/ppermute | solution.py:268
  98.0 4.6 %shard_map.84 = (f32[8,256,256]{2,1,0:T(8,128)}, f32[8,256,256]{2,1,0:T(8,128)}) custom-call(s32[45]{0:T(128)} %concatenate.3.refs_0_, f32[2,256,512]{2,1,0:T(8,128)} %shard_map.78.refs_6_.refs_1_.refs_9_, f32[2,256,512]{2,1,0:T(8,128)} %collective-permute-done.6.refs_7_.refs_2_.refs_10_, f32[1,2,256,512]{3,2,1,0:T(8,128)} %get-tuple-element.37.refs_3_.refs_4_, ...), custom_call_target="tpu_custom_call" | custom-call | flops 100000000376832 | bytes 1 | tf_op jit(solution)/shard_map/pallas_call | solution.py:35
  102.6 8.3 %shard_map.85 = (f32[2048,256]{1,0:T(8,128)}, f32[2048,256]{1,0:T(8,128)}) custom-call(s32[45]{0:T(128)} %concatenate.3.refs_0_, f32[1024,512]{1,0:T(8,128)} %refs_1_.3, f32[1024,512]{1,0:T(8,128)} %refs_2_.1, f32[512,512]{1,0:T(8,128)} %get-tuple-element.32.refs_2_.refs_3_, f32[8,256,256]{2,1,0:T(8,128)} %get-tuple-element.42.refs_4_.refs_7_, ...), custom_call_target="tpu_custom_call" | custom-call | flops 100000000376832 | bytes 1 | tf_op jit(solution)/shard_map/pallas_call | solution.py:35
  110.9 5.5 %collective-permute-start.11 = (f32[2048,256]{1,0:T(8,128)}, f32[2048,256]{1,0:T(8,128)}, u32[]{:S(2)}, u32[]{:S(2)}) collective-permute-start(f32[2048,256]{1,0:T(8,128)} %get-tuple-element.48.refs_2_), channel_id=1, source_target_pairs={{0,1},{1,2},{2,3},{3,4},{4,5},{5,6},{6,7},{7,8},{8,9},{9,10},{10,1... | collective-permute-start | bytes 6291464 | tf_op jit(solution)/shard_map/ppermute | solution.py:268
  116.5 1.9 collective-permute-start.14
  118.4 4.5 %shard_map.86 = (f32[8,256,256]{2,1,0:T(8,128)}, f32[8,256,256]{2,1,0:T(8,128)}) custom-call(s32[45]{0:T(128)} %concatenate.3.refs_0_, f32[2,256,512]{2,1,0:T(8,128)} %shard_map.78.refs_6_.refs_1_.refs_9_, f32[2,256,512]{2,1,0:T(8,128)} %collective-permute-done.6.refs_7_.refs_2_.refs_10_, ...), custom_call_target="tpu_custom_call", output_to_operand_aliasing={{0}: (7, {}), {1}: (8, {})} | custom-call | flops 100000000376832 | bytes 1 | tf_op jit(solution)/shard_map/pallas_call | solution.py:35
  122.9 21.4 %collective-permute-done.8.refs_7_.refs_5_.refs_6_ = f32[2,2,256,512]{3,2,1,0:T(8,128)} collective-permute-done((f32[2,2,256,512]{3,2,1,0:T(8,128)}, f32[2,2,256,512]{3,2,1,0:T(8,128)}, u32[]{:S(2)}, u32[]{:S(2)}) %collective-permute-start.8) | collective-permute-done | bytes 2097184 | tf_op jit(solution)/shard_map/ppermute | solution.py:268
  144.3 8.0 %shard_map.87 = (f32[2,2,256,512]{3,2,1,0:T(8,128)}, f32[256,512]{1,0:T(8,128)}) custom-call(s32[45]{0:T(128)} %concatenate.3.refs_0_, f32[4096,512]{1,0:T(8,128)} %bitcast.25, f32[512,512]{1,0:T(8,128)} %get-tuple-element.32.refs_2_.refs_3_, f32[8,256,512]{2,1,0:T(8,128)} %bitcast.27, f32[8,256,512]{2,1,0:T(8,128)} %bitcast.28, ...), custom_call_target="tpu_custom_call" | custom-call | flops 100000000376832 | bytes 1 | tf_op jit(solution)/shard_map/pallas_call | solution.py:35
  152.2 0.7 shard_map.88.refs_11_
  152.9 3.2 %collective-permute-start.16 = (f32[2,2,256,512]{3,2,1,0:T(8,128)}, f32[2,2,256,512]{3,2,1,0:T(8,128)}, u32[]{:S(2)}, u32[]{:S(2)}) collective-permute-start(f32[2,2,256,512]{3,2,1,0:T(8,128)} %get-tuple-element.53.refs_3_.refs_4_), channel_id=1, source_target_pairs={{8,24},{9,25},{10,26},{11,27},{12,28},{13,29},{14,30},{15,31},{24,... | collective-permute-start | bytes 6291464 | tf_op jit(solution)/shard_map/ppermute | solution.py:268
  156.1 6.1 %shard_map.89 = (f32[8,256,256]{2,1,0:T(8,128)}, f32[8,256,256]{2,1,0:T(8,128)}) custom-call(s32[45]{0:T(128)} %concatenate.3.refs_0_, f32[2,256,512]{2,1,0:T(8,128)} %shard_map.82.refs_2_.refs_1_, f32[2,256,512]{2,1,0:T(8,128)} %collective-permute-done.7.refs_5_.refs_2_, ...), custom_call_target="tpu_custom_call", output_to_operand_aliasing={{0}: (7, {}), {1}: (8, {})} | custom-call | flops 100000000376832 | bytes 1 | tf_op jit(solution)/shard_map/pallas_call | solution.py:35
  162.2 6.4 %collective-permute-start.12 = (f32[8,256,256]{2,1,0:T(8,128)}, f32[8,256,256]{2,1,0:T(8,128)}, u32[]{:S(2)}, u32[]{:S(2)}) collective-permute-start(f32[8,256,256]{2,1,0:T(8,128)} %get-tuple-element.50.refs_2_), channel_id=1, source_target_pairs={{0,1},{1,2},{2,3},{3,4},{4,5},{5,6},{6,7},{7,8},{8,9},{9,10},{10,1... | collective-permute-start | bytes 6291464 | tf_op jit(solution)/shard_map/ppermute | solution.py:268
  168.6 2.1 collective-permute-start.13
  170.7 8.2 %shard_map.90 = (f32[2,2,256,512]{3,2,1,0:T(8,128)}, f32[256,512]{1,0:T(8,128)}) custom-call(s32[45]{0:T(128)} %concatenate.3.refs_0_, f32[4096,512]{1,0:T(8,128)} %bitcast.26, f32[512,512]{1,0:T(8,128)} %get-tuple-element.32.refs_2_.refs_3_, f32[8,256,512]{2,1,0:T(8,128)} %bitcast.29, f32[8,256,512]{2,1,0:T(8,128)} %bitcast.30, ...), custom_call_target="tpu_custom_call" | custom-call | flops 100000000376832 | bytes 1 | tf_op jit(solution)/shard_map/pallas_call | solution.py:35
  178.9 2.2 collective-permute-start.15
  181.1 6.0 %shard_map.91.refs_7_ = f32[1024,512]{1,0:T(8,128)} custom-call(s32[45]{0:T(128)} %concatenate.3.refs_0_, f32[2048,256]{1,0:T(8,128)} %get-tuple-element.44.refs_9_.refs_1_, f32[2048,256]{1,0:T(8,128)} %get-tuple-element.48.refs_2_, f32[2048,256]{1,0:T(8,128)} %collective-permute-done.11.refs_12_.refs_3_, ...), custom_call_target="tpu_custom_call" | custom-call | flops 100000000376832 | bytes 1 | tf_op jit(solution)/shard_map/pallas_call | solution.py:35
  187.2 6.0 %shard_map.92.refs_2_ = f32[1024,512]{1,0:T(8,128)} custom-call(s32[45]{0:T(128)} %concatenate.3.refs_0_, f32[2048,256]{1,0:T(8,128)} %get-tuple-element.44.refs_9_.refs_1_, f32[2048,256]{1,0:T(8,128)} %get-tuple-element.48.refs_2_, f32[2048,256]{1,0:T(8,128)} %collective-permute-done.11.refs_12_.refs_3_, ...), custom_call_target="tpu_custom_call" | custom-call | flops 100000000376832 | bytes 1 | tf_op jit(solution)/shard_map/pallas_call | solution.py:35
  193.2 8.5 %collective-permute-done.16.refs_1_ = f32[2,2,256,512]{3,2,1,0:T(8,128)} collective-permute-done((f32[2,2,256,512]{3,2,1,0:T(8,128)}, f32[2,2,256,512]{3,2,1,0:T(8,128)}, u32[]{:S(2)}, u32[]{:S(2)}) %collective-permute-start.16) | collective-permute-done | bytes 2097184 | tf_op jit(solution)/shard_map/ppermute | solution.py:268
  201.7 0.7 shard_map.93.refs_5_.refs_6_
  202.4 16.0 %all-gather.11.cloned.1.call-done = f32[2048,512]{1,0:T(8,128)} async-done(((f32[256,512]{1,0:T(8,128)}), f32[2048,512]{1,0:T(8,128)}) %all-gather.11.cloned.1.call-update) | async-done | bytes 4194320 | tf_op jit(solution)/shard_map/all_gather | solution.py:314
  218.4 6.4 %shard_map.94 = (f32[6,256,256]{2,1,0:T(8,128)}, f32[6,256,256]{2,1,0:T(8,128)}) custom-call(s32[45]{0:T(128)} %concatenate.3.refs_0_, f32[8,256,512]{2,1,0:T(8,128)} %bitcast.31, f32[8,256,512]{2,1,0:T(8,128)} %bitcast.32, f32[2,2,256,512]{3,2,1,0:T(8,128)} %get-tuple-element.53.refs_3_.refs_4_, f32[2,2,256,512]{3,2,1,0:T(8,128)} %get-tuple-element.53.refs_3_.refs_4_, ...), custom_call_target="tpu_custom_call" | custom-call | flops 100000000376832 | bytes 1 | tf_op jit(solution)/shard_map/pallas_call | solution.py:35
  224.8 3.3 %collective-permute-start.19 = (f32[6,256,256]{2,1,0:T(8,128)}, f32[6,256,256]{2,1,0:T(8,128)}, u32[]{:S(2)}, u32[]{:S(2)}) collective-permute-start(f32[6,256,256]{2,1,0:T(8,128)} %get-tuple-element.58.refs_2_), channel_id=1, source_target_pairs={{0,1},{1,2},{2,3},{3,4},{4,5},{5,6},{6,7},{7,8},{8,9},{9,10},{10,1... | collective-permute-start | bytes 4718600 | tf_op jit(solution)/shard_map/ppermute | solution.py:268
  228.2 1.9 collective-permute-start.20
  230.1 0.7 collective-permute-done.13.refs_5_.refs_6_
  230.8 7.5 %shard_map.95.refs_7_.refs_10_ = f32[4096,512]{1,0:T(8,128)} custom-call(s32[45]{0:T(128)} %concatenate.3.refs_0_, f32[8,256,256]{2,1,0:T(8,128)} %get-tuple-element.49.refs_6_.refs_1_.refs_7_.refs_10_, f32[8,256,256]{2,1,0:T(8,128)} %get-tuple-element.50.refs_2_, f32[8,256,256]{2,1,0:T(8,128)} %collective-permute-done.12.refs_3_.refs_4_, ...), custom_call_target="tpu_custom_call" | custom-call | flops 100000000376832 | bytes 1 | tf_op jit(solution)/shard_map/pallas_call | solution.py:35
  238.3 8.3 %collective-permute-done.15.refs_5_.refs_6_ = f32[2,2,256,512]{3,2,1,0:T(8,128)} collective-permute-done((f32[2,2,256,512]{3,2,1,0:T(8,128)}, f32[2,2,256,512]{3,2,1,0:T(8,128)}, u32[]{:S(2)}, u32[]{:S(2)}) %collective-permute-start.15) | collective-permute-done | bytes 2097184 | tf_op jit(solution)/shard_map/ppermute | solution.py:268
  246.7 5.6 %shard_map.96 = (f32[4,256,256]{2,1,0:T(8,128)}, f32[4,256,256]{2,1,0:T(8,128)}) custom-call(s32[45]{0:T(128)} %concatenate.3.refs_0_, f32[8,256,512]{2,1,0:T(8,128)} %bitcast.33, f32[8,256,512]{2,1,0:T(8,128)} %bitcast.34, f32[2,2,256,512]{3,2,1,0:T(8,128)} %get-tuple-element.51.refs_3_.refs_4_, f32[2,2,256,512]{3,2,1,0:T(8,128)} %get-tuple-element.51.refs_3_.refs_4_, ...), custom_call_target="tpu_custom_call" | custom-call | flops 100000000376832 | bytes 1 | tf_op jit(solution)/shard_map/pallas_call | solution.py:35
  252.3 6.7 %collective-permute-start.18 = (f32[4,256,256]{2,1,0:T(8,128)}, f32[4,256,256]{2,1,0:T(8,128)}, u32[]{:S(2)}, u32[]{:S(2)}) collective-permute-start(f32[4,256,256]{2,1,0:T(8,128)} %get-tuple-element.57.refs_2_), channel_id=1, source_target_pairs={{8,9},{9,10},{10,11},{11,12},{12,13},{13,14},{14,15},{24,25},{25,2... | collective-permute-start | bytes 3145736 | tf_op jit(solution)/shard_map/ppermute | solution.py:268
  259.0 2.1 collective-permute-start.17
  261.1 7.0 %shard_map.97.refs_10_ = f32[4096,512]{1,0:T(8,128)} custom-call(s32[45]{0:T(128)} %concatenate.3.refs_0_, f32[8,256,256]{2,1,0:T(8,128)} %get-tuple-element.49.refs_6_.refs_1_.refs_7_.refs_10_, f32[8,256,256]{2,1,0:T(8,128)} %get-tuple-element.50.refs_2_, f32[8,256,256]{2,1,0:T(8,128)} %collective-permute-done.12.refs_3_.refs_4_, ...), custom_call_target="tpu_custom_call", output_to_operand_aliasing={{}: (10, {})} | custom-call | flops 100000000376832 | bytes 1 | tf_op jit(solution)/shard_map/pallas_call | solution.py:35
  268.2 10.1 %collective-permute-done.20.refs_5_.refs_7_.refs_6_.refs_4_ = f32[6,256,256]{2,1,0:T(8,128)} collective-permute-done((f32[6,256,256]{2,1,0:T(8,128)}, f32[6,256,256]{2,1,0:T(8,128)}, u32[]{:S(2)}, u32[]{:S(2)}) %collective-permute-start.20) | collective-permute-done | bytes 1572896 | tf_op jit(solution)/shard_map/ppermute | solution.py:268
  278.3 6.7 %shard_map.98.refs_10_ = f32[4096,512]{1,0:T(8,128)} custom-call(s32[45]{0:T(128)} %concatenate.3.refs_0_, f32[6,256,256]{2,1,0:T(8,128)} %get-tuple-element.55.refs_11_.refs_1_, f32[6,256,256]{2,1,0:T(8,128)} %get-tuple-element.58.refs_2_, f32[8,256,256]{2,1,0:T(8,128)} %collective-permute-done.12.refs_3_.refs_4_, ...), custom_call_target="tpu_custom_call", output_to_operand_aliasing={{}: (10, {})} | custom-call | flops 100000000376832 | bytes 1 | tf_op jit(solution)/shard_map/pallas_call | solution.py:35
  285.0 3.7 %shard_map.99.refs_7_ = f32[4096,512]{1,0:T(8,128)} custom-call(s32[45]{0:T(128)} %concatenate.3.refs_0_, f32[8,256,256]{2,1,0:T(8,128)} %get-tuple-element.49.refs_6_.refs_1_.refs_7_.refs_10_, f32[8,256,256]{2,1,0:T(8,128)} %get-tuple-element.50.refs_2_, f32[8,256,256]{2,1,0:T(8,128)} %collective-permute-done.12.refs_3_.refs_4_, ...), custom_call_target="tpu_custom_call", output_to_operand_aliasing={{}: (10, {})} | custom-call | flops 100000000376832 | bytes 1 | tf_op jit(solution)/shard_map/pallas_call | solution.py:35
  288.8 3.7 %shard_map.100.refs_10_ = f32[4096,512]{1,0:T(8,128)} custom-call(s32[45]{0:T(128)} %concatenate.3.refs_0_, f32[256,512]{1,0:T(8,128)} %get-tuple-element.54.refs_7_.refs_1_, f32[6,256,256]{2,1,0:T(8,128)} %collective-permute-done.19.refs_4_.refs_2_.refs_3_, ...), custom_call_target="tpu_custom_call", output_to_operand_aliasing={{}: (7, {})} | custom-call | flops 100000000376832 | bytes 1 | tf_op jit(solution)/shard_map/pallas_call | solution.py:35
  292.4 7.1 %shard_map.101.refs_10_ = f32[4096,512]{1,0:T(8,128)} custom-call(s32[45]{0:T(128)} %concatenate.3.refs_0_, f32[4,256,256]{2,1,0:T(8,128)} %get-tuple-element.56.refs_11_.refs_1_.refs_7_, f32[4,256,256]{2,1,0:T(8,128)} %get-tuple-element.57.refs_2_, f32[8,256,256]{2,1,0:T(8,128)} %collective-permute-done.12.refs_3_.refs_4_, ...), custom_call_target="tpu_custom_call", output_to_operand_aliasing={{}: (10, {})} | custom-call | flops 100000000376832 | bytes 1 | tf_op jit(solution)/shard_map/pallas_call | solution.py:35
  299.6 3.5 %shard_map.102 = f32[4096,512]{1,0:T(8,128)} custom-call(s32[45]{0:T(128)} %concatenate.3.refs_0_, f32[8,256,256]{2,1,0:T(8,128)} %get-tuple-element.49.refs_6_.refs_1_.refs_7_.refs_10_, f32[8,256,256]{2,1,0:T(8,128)} %get-tuple-element.50.refs_2_, f32[8,256,256]{2,1,0:T(8,128)} %collective-permute-done.12.refs_3_.refs_4_, ...), custom_call_target="tpu_custom_call", output_to_operand_aliasing={{}: (10, {})} | custom-call | flops 100000000376832 | bytes 1 | tf_op jit(solution)/shard_map/pallas_call | solution.py:35
  (26 shorter events, 0.2 us)
Async XLA Ops:
  7.2 2.8 copy-start.2
  7.2 56.5 %all-gather.7.cloned.1.call-start = ((), (), s32[]{:S(2)}) async-start(), calls=%async_computation | async-start | bytes 4718592 | tf_op jit(solution)/shard_map/all_gather | solution.py:314
  8.5 4.6 %collective-permute-start = (f32[512,512]{1,0:T(8,128)S(1)}, f32[512,512]{1,0:T(8,128)S(1)}, u32[]{:S(2)}, u32[]{:S(2)}) collective-permute-start(f32[512,512]{1,0:T(8,128)S(1)} %slice_bitcast_fusion), channel_id=1, source_target_pairs={{0,1},{2,3},{4,5},{6,7},{8,9},{10,11},{12,13},{14,15},{17,16},{19,... | collective-permute-start | bytes 3145736 | tf_op jit(solution)/shard_map/ppermute | solution.py:268
  13.1 1.0 copy-start.1
  18.9 125.4 %all-gather.9.cloned.1.call-start = ((), (), s32[]{:S(2)}) async-start(), calls=%async_computation.1 | async-start | bytes 4718592 | tf_op jit(solution)/shard_map/all_gather | solution.py:314
  19.0 50.4 %collective-permute-start.5 = (f32[256,512]{1,0:T(8,128)}, f32[256,512]{1,0:T(8,128)}, u32[]{:S(2)}, u32[]{:S(2)}) collective-permute-start(f32[256,512]{1,0:T(8,128)} %get-tuple-element.36), channel_id=1, source_target_pairs={{0,8},{1,9},{2,10},{3,11},{4,12},{5,13},{6,14},{7,15},{16,24},{17,... | collective-permute-start | bytes 1572872 | tf_op jit(solution)/shard_map/ppermute | solution.py:268
  20.3 19.3 %collective-permute-start.2 = (f32[512,256]{1,0:T(8,128)}, f32[512,256]{1,0:T(8,128)}, u32[]{:S(2)}, u32[]{:S(2)}) collective-permute-start(f32[512,256]{1,0:T(8,128)} %get-tuple-element.35), channel_id=1, source_target_pairs={{0,1},{1,2},{2,3},{3,4},{4,5},{5,6},{6,7},{7,8},{8,9},{9,10},{10,1... | collective-permute-start | bytes 1572872 | tf_op jit(solution)/shard_map/ppermute | solution.py:268
  23.4 34.0 %collective-permute-start.1 = (f32[256,512]{1,0:T(8,128)}, f32[256,512]{1,0:T(8,128)}, u32[]{:S(2)}, u32[]{:S(2)}) collective-permute-start(f32[256,512]{1,0:T(8,128)} %get-tuple-element.31.refs_1_), channel_id=1, source_target_pairs={{0,2},{1,3},{2,0},{3,1},{4,6},{5,7},{6,4},{7,5},{8,10},{9,11},{10,... | collective-permute-start | bytes 1572872 | tf_op jit(solution)/shard_map/ppermute | solution.py:268
  30.1 33.6 %collective-permute-start.4 = (f32[1,2,256,512]{3,2,1,0:T(8,128)}, f32[1,2,256,512]{3,2,1,0:T(8,128)}, u32[]{:S(2)}, u32[]{:S(2)}) collective-permute-start(f32[1,2,256,512]{3,2,1,0:T(8,128)} %get-tuple-element.37.refs_3_.refs_4_), channel_id=1, source_target_pairs={{6,22},{7,23},{14,30},{15,31},{23,7},{31,15}} | collective-permute-start | bytes 3145736 | tf_op jit(solution)/shard_map/ppermute | solution.py:268
  57.4 4.4 %copy-start = (s32[256]{0:T(256)S(1)}, s32[256]{0:T(256)}, u32[]{:S(2)}) copy-start(s32[256]{0:T(256)} %iota_add_fusion) | copy-start | bytes 3076
  60.5 13.7 %collective-permute-start.6 = (f32[2,256,512]{2,1,0:T(8,128)}, f32[2,256,512]{2,1,0:T(8,128)}, u32[]{:S(2)}, u32[]{:S(2)}) collective-permute-start(f32[2,256,512]{2,1,0:T(8,128)} %shard_map.78.refs_6_.refs_1_.refs_9_), channel_id=1, source_target_pairs={{0,1},{1,0},{2,3},{3,2},{4,5},{5,4},{6,7},{7,6},{8,9},{9,8},{10,11... | collective-permute-start | bytes 3145736 | tf_op jit(solution)/shard_map/ppermute | solution.py:268
  60.5 26.4 %collective-permute-start.3 = (f32[2,256,512]{2,1,0:T(8,128)}, f32[2,256,512]{2,1,0:T(8,128)}, u32[]{:S(2)}, u32[]{:S(2)}) collective-permute-start(f32[2,256,512]{2,1,0:T(8,128)} %shard_map.78.refs_6_.refs_1_.refs_9_), channel_id=1, source_target_pairs={{0,4},{1,5},{2,6},{3,7},{4,8},{5,9},{6,10},{7,11},{8,12},{9,13},{1... | collective-permute-start | bytes 3145736 | tf_op jit(solution)/shard_map/ppermute | solution.py:268
  70.0 148.4 %all-gather.11.cloned.1.call-start = ((), (), s32[]{:S(2)}) async-start(), calls=%async_computation.2 | async-start | bytes 4718592 | tf_op jit(solution)/shard_map/all_gather | solution.py:314
  70.1 27.9 %collective-permute-start.9 = (f32[1,2,256,512]{3,2,1,0:T(8,128)}, f32[1,2,256,512]{3,2,1,0:T(8,128)}, u32[]{:S(2)}, u32[]{:S(2)}) collective-permute-start(f32[1,2,256,512]{3,2,1,0:T(8,128)} %get-tuple-element.41.refs_3_.refs_4_), channel_id=1, source_target_pairs={{4,20},{5,21},{6,22},{7,23},{12,28},{13,29},{14,30},{15,31},{21,5}... | collective-permute-start | bytes 3145736 | tf_op jit(solution)/shard_map/ppermute | solution.py:268
  88.3 14.4 %collective-permute-start.7 = (f32[2,256,512]{2,1,0:T(8,128)}, f32[2,256,512]{2,1,0:T(8,128)}, u32[]{:S(2)}, u32[]{:S(2)}) collective-permute-start(f32[2,256,512]{2,1,0:T(8,128)} %shard_map.82.refs_2_.refs_1_), channel_id=1, source_target_pairs={{0,1},{1,0},{2,3},{3,2},{4,5},{5,4},{6,7},{7,6},{8,9},{9,8},{10,11... | collective-permute-start | bytes 3145736 | tf_op jit(solution)/shard_map/ppermute | solution.py:268
  91.4 60.8 %collective-permute-start.10 = (f32[256,512]{1,0:T(8,128)}, f32[256,512]{1,0:T(8,128)}, u32[]{:S(2)}, u32[]{:S(2)}) collective-permute-start(f32[256,512]{1,0:T(8,128)} %shard_map.83.refs_7_), channel_id=1, source_target_pairs={{0,8},{1,9},{2,10},{3,11},{4,12},{5,13},{6,14},{7,15},{16,24},{17,... | collective-permute-start | bytes 1572872 | tf_op jit(solution)/shard_map/ppermute | solution.py:268
  92.7 51.6 %collective-permute-start.8 = (f32[2,2,256,512]{3,2,1,0:T(8,128)}, f32[2,2,256,512]{3,2,1,0:T(8,128)}, u32[]{:S(2)}, u32[]{:S(2)}) collective-permute-start(f32[2,2,256,512]{3,2,1,0:T(8,128)} %get-tuple-element.40.refs_3_.refs_4_), channel_id=1, source_target_pairs={{0,16},{1,17},{2,18},{3,19},{4,20},{5,21},{6,22},{7,23},{8,24},{9,... | collective-permute-start | bytes 6291464 | tf_op jit(solution)/shard_map/ppermute | solution.py:268
  110.9 45.2 %collective-permute-start.11 = (f32[2048,256]{1,0:T(8,128)}, f32[2048,256]{1,0:T(8,128)}, u32[]{:S(2)}, u32[]{:S(2)}) collective-permute-start(f32[2048,256]{1,0:T(8,128)} %get-tuple-element.48.refs_2_), channel_id=1, source_target_pairs={{0,1},{1,2},{2,3},{3,4},{4,5},{5,6},{6,7},{7,8},{8,9},{9,10},{10,1... | collective-permute-start | bytes 6291464 | tf_op jit(solution)/shard_map/ppermute | solution.py:268
  116.5 54.3 %collective-permute-start.14 = (f32[2048,256]{1,0:T(8,128)}, f32[2048,256]{1,0:T(8,128)}, u32[]{:S(2)}, u32[]{:S(2)}) collective-permute-start(f32[2048,256]{1,0:T(8,128)} %get-tuple-element.44.refs_9_.refs_1_), channel_id=1, source_target_pairs={{1,0},{2,1},{3,2},{4,3},{5,4},{6,5},{7,6},{8,7},{9,8},{10,9},{11,1... | collective-permute-start | bytes 6291464 | tf_op jit(solution)/shard_map/ppermute | solution.py:268
  152.9 48.8 %collective-permute-start.16 = (f32[2,2,256,512]{3,2,1,0:T(8,128)}, f32[2,2,256,512]{3,2,1,0:T(8,128)}, u32[]{:S(2)}, u32[]{:S(2)}) collective-permute-start(f32[2,2,256,512]{3,2,1,0:T(8,128)} %get-tuple-element.53.refs_3_.refs_4_), channel_id=1, source_target_pairs={{8,24},{9,25},{10,26},{11,27},{12,28},{13,29},{14,30},{15,31},{24,... | collective-permute-start | bytes 6291464 | tf_op jit(solution)/shard_map/ppermute | solution.py:268
  162.2 67.9 %collective-permute-start.12 = (f32[8,256,256]{2,1,0:T(8,128)}, f32[8,256,256]{2,1,0:T(8,128)}, u32[]{:S(2)}, u32[]{:S(2)}) collective-permute-start(f32[8,256,256]{2,1,0:T(8,128)} %get-tuple-element.50.refs_2_), channel_id=1, source_target_pairs={{0,1},{1,2},{2,3},{3,4},{4,5},{5,6},{6,7},{7,8},{8,9},{9,10},{10,1... | collective-permute-start | bytes 6291464 | tf_op jit(solution)/shard_map/ppermute | solution.py:268
  168.6 62.2 %collective-permute-start.13 = (f32[8,256,256]{2,1,0:T(8,128)}, f32[8,256,256]{2,1,0:T(8,128)}, u32[]{:S(2)}, u32[]{:S(2)}) collective-permute-start(f32[8,256,256]{2,1,0:T(8,128)} %get-tuple-element.49.refs_6_.refs_1_.refs_7_.refs_10_), channel_id=1, source_target_pairs={{1,0},{2,1},{3,2},{4,3},{5,4},{6,5},{7,6},{8,7},{9,8},{10,9},{11,1... | collective-permute-start | bytes 6291464 | tf_op jit(solution)/shard_map/ppermute | solution.py:268
  178.9 67.8 %collective-permute-start.15 = (f32[2,2,256,512]{3,2,1,0:T(8,128)}, f32[2,2,256,512]{3,2,1,0:T(8,128)}, u32[]{:S(2)}, u32[]{:S(2)}) collective-permute-start(f32[2,2,256,512]{3,2,1,0:T(8,128)} %get-tuple-element.51.refs_3_.refs_4_), channel_id=1, source_target_pairs={{8,24},{9,25},{10,26},{11,27},{12,28},{13,29},{14,30},{15,31},{24,... | collective-permute-start | bytes 6291464 | tf_op jit(solution)/shard_map/ppermute | solution.py:268
  224.8 43.3 %collective-permute-start.19 = (f32[6,256,256]{2,1,0:T(8,128)}, f32[6,256,256]{2,1,0:T(8,128)}, u32[]{:S(2)}, u32[]{:S(2)}) collective-permute-start(f32[6,256,256]{2,1,0:T(8,128)} %get-tuple-element.58.refs_2_), channel_id=1, source_target_pairs={{0,1},{1,2},{2,3},{3,4},{4,5},{5,6},{6,7},{7,8},{8,9},{9,10},{10,1... | collective-permute-start | bytes 4718600 | tf_op jit(solution)/shard_map/ppermute | solution.py:268
  228.2 50.1 %collective-permute-start.20 = (f32[6,256,256]{2,1,0:T(8,128)}, f32[6,256,256]{2,1,0:T(8,128)}, u32[]{:S(2)}, u32[]{:S(2)}) collective-permute-start(f32[6,256,256]{2,1,0:T(8,128)} %get-tuple-element.55.refs_11_.refs_1_), channel_id=1, source_target_pairs={{1,0},{2,1},{3,2},{4,3},{5,4},{6,5},{7,6},{8,7},{9,8},{10,9},{11,1... | collective-permute-start | bytes 4718600 | tf_op jit(solution)/shard_map/ppermute | solution.py:268
  252.3 40.2 %collective-permute-start.18 = (f32[4,256,256]{2,1,0:T(8,128)}, f32[4,256,256]{2,1,0:T(8,128)}, u32[]{:S(2)}, u32[]{:S(2)}) collective-permute-start(f32[4,256,256]{2,1,0:T(8,128)} %get-tuple-element.57.refs_2_), channel_id=1, source_target_pairs={{8,9},{9,10},{10,11},{11,12},{12,13},{13,14},{14,15},{24,25},{25,2... | collective-permute-start | bytes 3145736 | tf_op jit(solution)/shard_map/ppermute | solution.py:268
  259.0 33.4 %collective-permute-start.17 = (f32[4,256,256]{2,1,0:T(8,128)}, f32[4,256,256]{2,1,0:T(8,128)}, u32[]{:S(2)}, u32[]{:S(2)}) collective-permute-start(f32[4,256,256]{2,1,0:T(8,128)} %get-tuple-element.56.refs_11_.refs_1_.refs_7_), channel_id=1, source_target_pairs={{8,7},{9,8},{10,9},{11,10},{12,11},{13,12},{14,13},{15,14},{24,23}... | collective-permute-start | bytes 3145736 | tf_op jit(solution)/shard_map/ppermute | solution.py:268
Sparse Core Ops, SparseCore 0:
  19.0 42.4 all-gather.6
  70.1 37.4 all-gather.8
  153.1 65.3 all-gather.10

commit v4 on v3

--- a/solution.py
+++ b/solution.py
@@ -78,8 +78,8 @@
     out[1] = jnp.where(odd, own[...], across[...])
 
 
-def rest_kernel(info, value, out):
-    del info, value, out
+def rest_kernel(info, *refs):
+    del info, refs
 
 
 def first_kernel(joint, info, seg, col, near, far, prev_top, *rest):
@@ -314,13 +314,16 @@
         mine = lax.all_gather(value, "pcol", axis_index_groups=teams)
         return (mine, lambda q: 2 * q, mine, lambda q: 2 * q + 1)
 
+    def placed_all(values, *after):
+        anywhere = [pl.BlockSpec(memory_space=pl.ANY)] * len(values)
+        shapes = [shape(*value.shape) for value in values]
+        alias = {1 + k: k for k in range(len(values))}
+        values = call(rest_kernel, info, (1,), anywhere, anywhere, shapes, [], values, alias, [*last[-1:], *after])
+        last.append(values[0])
+        return values
+
     def placed(value, *after):
-        anywhere = pl.BlockSpec(memory_space=pl.ANY)
-        value = call(
-            rest_kernel, info, (1,), [anywhere], anywhere, shape(*value.shape), [], (value,), {1: 0}, [*last[-1:], *after]
-        )
-        last.append(value)
-        return value
+        return placed_all([value], *after)[0]
 
     def paired_up(own, across, *after):
         out = call(
@@ -590,8 +593,9 @@
         do_first([1], got[0])
         first_factors.append(gathered(placed(hop_a)))
         do_first([2, 3], [second_factors[0][2]])
-        second_factors += [with_swapped(placed(pieces))] * 2
-        hop_b = hopped(placed(chain_b), 1)
+        pieces, passed_b = placed_all([pieces, chain_b])
+        second_factors += [with_swapped(pieces)] * 2
+        hop_b = hopped(passed_b, 1)
         do_second([0], [0, 1, 2, 3], after=got[1])
         parts = do_rows([second_factors[2][2]])
         do_second([1], [0, 1, 2, 3])

time: 312 us -> 312 us (level)
    pallas_call x27 -> x26, Pallas kernels: 134 us -> 133 us  [call(): pl.pallas_call(run, grid_spec=pltpu.PrefetchScalarGridSpec(num_scalar_pre...]
where the time goes in v4:
time: 312 us; the launch traced here: 309 us
  Pallas kernels  133 us (43%)
  waiting for transfers between devices  97.1 us (31%)
  starting transfers between devices  58.4 us (19%)
  between operations  14.2 us (5%)
  local copies, waits for them, and re-layouts  3.9 us (1%)
    pallas_call x26, Pallas kernels, call(): pl.pallas_call(run, grid_spec=pltpu.PrefetchScalarGridSpec(num_scalar_pre...  133 us
    ppermute x21, waiting for transfers between devices, send(): lax.ppermute(value, GRID, [(a * cols + b, c * cols + d) for (a, b), (c, d...  81.1 us
    ppermute x21, starting transfers between devices, send(): lax.ppermute(value, GRID, [(a * cols + b, c * cols + d) for (a, b), (c, d...  58.2 us
    all_gather x3, waiting for transfers between devices, gathered(): mine = lax.all_gather(value, 'pcol', axis_index_groups=teams)  16 us
  transfers between devices with their start and end apart: 24, of which 10 were waited for; matrix products, arithmetic and copies ran while one was open for 1% of the time, Pallas kernels for 38%

profile of v4, /device:TPU:25, one launch (start us, length us, event | category | flops | bytes accessed | tf_op | source)
XLA Modules:
  0.0 309.0 jit_solution(10119029339471769718)
XLA Ops:
  7.2 1.3 slice_bitcast_fusion
  8.5 1.3 collective-permute-start
  9.9 0.1 reshape.15
  10.0 0.7 concatenate.3.refs_0_
  10.7 0.6 iota_add_fusion
  11.3 1.8 collective-permute-done.refs_2_
  13.1 1.0 copy-done.1
  14.0 4.9 %shard_map.76 = (f32[512,512]{1,0:T(8,128)}, f32[2,256,512]{2,1,0:T(8,128)}, f32[256,512]{1,0:T(8,128)}, f32[256,512]{1,0:T(8,128)}, f32[512,256]{1,0:T(8,128)}, /*index=5*/f32[512,256]{1,0:T(8,128)}) custom-call(s32[45]{0:T(128)} %concatenate.3.refs_0_, f32[2,1,512,512]{3,2,1,0:T(8,128)} %refs_1_.2, f32[512,512]{1,0:T(8,128)} %copy-done.1), custom_call_target="tpu_custom_call" | custom-call | flops 100000000376832 | bytes 1 | tf_op jit(solution)/shard_map/pallas_call | solution.py:35
  18.9 0.0 all-gather.9.cloned.1.call-start
  19.0 1.3 collective-permute-start.5
  20.3 3.2 %collective-permute-start.2 = (f32[512,256]{1,0:T(8,128)}, f32[512,256]{1,0:T(8,128)}, u32[]{:S(2)}, u32[]{:S(2)}) collective-permute-start(f32[512,256]{1,0:T(8,128)} %get-tuple-element.37), channel_id=1, source_target_pairs={{0,1},{1,2},{2,3},{3,4},{4,5},{5,6},{6,7},{7,8},{8,9},{9,10},{10,1... | collective-permute-start | bytes 1572872 | tf_op jit(solution)/shard_map/ppermute | solution.py:268
  23.4 0.1 collective-permute-start.1
  23.5 0.9 broadcast_in_dim.3.refs_5_
  24.4 5.7 %shard_map.77 = (f32[1,2,256,512]{3,2,1,0:T(8,128)}, f32[256,512]{1,0:T(8,128)}) custom-call(s32[45]{0:T(128)} %concatenate.3.refs_0_, f32[4096,512]{1,0:T(8,128)} %bitcast.22, f32[512,512]{1,0:T(8,128)} %get-tuple-element.34.refs_2_.refs_3_, f32[2,256,512]{2,1,0:T(8,128)} %get-tuple-element.35.refs_3_.refs_4_, ...), custom_call_target="tpu_custom_call" | custom-call | flops 100000000376832 | bytes 1 | tf_op jit(solution)/shard_map/pallas_call | solution.py:35
  30.1 1.6 collective-permute-start.4
  31.8 7.8 %collective-permute-done.2.refs_4_ = f32[512,256]{1,0:T(8,128)} collective-permute-done((f32[512,256]{1,0:T(8,128)}, f32[512,256]{1,0:T(8,128)}, u32[]{:S(2)}, u32[]{:S(2)}) %collective-permute-start.2) | collective-permute-done | bytes 524320 | tf_op jit(solution)/shard_map/ppermute | solution.py:268
  39.5 17.9 %collective-permute-done.1.refs_2_ = f32[256,512]{1,0:T(8,128)} collective-permute-done((f32[256,512]{1,0:T(8,128)}, f32[256,512]{1,0:T(8,128)}, u32[]{:S(2)}, u32[]{:S(2)}) %collective-permute-start.1) | collective-permute-done | bytes 524320 | tf_op jit(solution)/shard_map/ppermute | solution.py:268
  57.4 3.1 shard_map.78.refs_6_.refs_1_.refs_9_
  60.5 1.3 collective-permute-start.3
  61.8 1.9 convert_select_fusion.refs_5_.refs_8_
  63.7 5.6 %shard_map.79 = (f32[1,2,256,512]{3,2,1,0:T(8,128)}, f32[256,512]{1,0:T(8,128)}) custom-call(s32[45]{0:T(128)} %concatenate.3.refs_0_, f32[4096,512]{1,0:T(8,128)} %bitcast.23, f32[512,512]{1,0:T(8,128)} %get-tuple-element.34.refs_2_.refs_3_, f32[8,256,512]{2,1,0:T(8,128)} %bitcast.35, f32[8,256,512]{2,1,0:T(8,128)} %bitcast.36, ...), custom_call_target="tpu_custom_call" | custom-call | flops 100000000376832 | bytes 1 | tf_op jit(solution)/shard_map/pallas_call | solution.py:35
  69.3 0.7 shard_map.80.refs_6_
  70.1 4.2 %collective-permute-start.9 = (f32[1,2,256,512]{3,2,1,0:T(8,128)}, f32[1,2,256,512]{3,2,1,0:T(8,128)}, u32[]{:S(2)}, u32[]{:S(2)}) collective-permute-start(f32[1,2,256,512]{3,2,1,0:T(8,128)} %get-tuple-element.44.refs_3_.refs_4_), channel_id=1, source_target_pairs={{4,20},{5,21},{6,22},{7,23},{12,28},{13,29},{14,30},{15,31},{21,5}... | collective-permute-start | bytes 3145736 | tf_op jit(solution)/shard_map/ppermute | solution.py:268
  74.3 7.9 %shard_map.81 = (f32[2,2,256,512]{3,2,1,0:T(8,128)}, f32[256,512]{1,0:T(8,128)}) custom-call(s32[45]{0:T(128)} %concatenate.3.refs_0_, f32[4096,512]{1,0:T(8,128)} %bitcast.24, f32[512,512]{1,0:T(8,128)} %get-tuple-element.34.refs_2_.refs_3_, f32[8,256,512]{2,1,0:T(8,128)} %bitcast.37, f32[8,256,512]{2,1,0:T(8,128)} %bitcast.38, ...), custom_call_target="tpu_custom_call" | custom-call | flops 100000000376832 | bytes 1 | tf_op jit(solution)/shard_map/pallas_call | solution.py:35
  82.2 4.7 %collective-permute-done.3.refs_1_ = f32[2,256,512]{2,1,0:T(8,128)} collective-permute-done((f32[2,256,512]{2,1,0:T(8,128)}, f32[2,256,512]{2,1,0:T(8,128)}, u32[]{:S(2)}, u32[]{:S(2)}) %collective-permute-start.3) | collective-permute-done | bytes 1048608 | tf_op jit(solution)/shard_map/ppermute | solution.py:268
  86.9 0.7 shard_map.82
  87.6 1.3 collective-permute-start.10
  88.9 3.1 %collective-permute-start.7 = (f32[2,256,512]{2,1,0:T(8,128)}, f32[2,256,512]{2,1,0:T(8,128)}, u32[]{:S(2)}, u32[]{:S(2)}) collective-permute-start(f32[2,256,512]{2,1,0:T(8,128)} %get-tuple-element.42.refs_7_.refs_1_), channel_id=1, source_target_pairs={{0,1},{1,0},{2,3},{3,2},{4,5},{5,4},{6,7},{7,6},{8,9},{9,8},{10,11... | collective-permute-start | bytes 3145736 | tf_op jit(solution)/shard_map/ppermute | solution.py:268
  92.0 5.3 %collective-permute-start.8 = (f32[2,2,256,512]{3,2,1,0:T(8,128)}, f32[2,2,256,512]{3,2,1,0:T(8,128)}, u32[]{:S(2)}, u32[]{:S(2)}) collective-permute-start(f32[2,2,256,512]{3,2,1,0:T(8,128)} %get-tuple-element.43.refs_3_.refs_4_), channel_id=1, source_target_pairs={{0,16},{1,17},{2,18},{3,19},{4,20},{5,21},{6,22},{7,23},{8,24},{9,... | collective-permute-start | bytes 6291464 | tf_op jit(solution)/shard_map/ppermute | solution.py:268
  97.3 4.6 %shard_map.83 = (f32[8,256,256]{2,1,0:T(8,128)}, f32[8,256,256]{2,1,0:T(8,128)}) custom-call(s32[45]{0:T(128)} %concatenate.3.refs_0_, f32[2,256,512]{2,1,0:T(8,128)} %shard_map.78.refs_6_.refs_1_.refs_9_, f32[2,256,512]{2,1,0:T(8,128)} %collective-permute-done.6.refs_7_.refs_2_.refs_10_, f32[1,2,256,512]{3,2,1,0:T(8,128)} %get-tuple-element.39.refs_3_.refs_4_, ...), custom_call_target="tpu_custom_call" | custom-call | flops 100000000376832 | bytes 1 | tf_op jit(solution)/shard_map/pallas_call | solution.py:35
  102.0 8.3 %shard_map.84 = (f32[2048,256]{1,0:T(8,128)}, f32[2048,256]{1,0:T(8,128)}) custom-call(s32[45]{0:T(128)} %concatenate.3.refs_0_, f32[1024,512]{1,0:T(8,128)} %refs_1_.3, f32[1024,512]{1,0:T(8,128)} %refs_2_.1, f32[512,512]{1,0:T(8,128)} %get-tuple-element.34.refs_2_.refs_3_, f32[8,256,256]{2,1,0:T(8,128)} %get-tuple-element.45.refs_4_.refs_7_, ...), custom_call_target="tpu_custom_call" | custom-call | flops 100000000376832 | bytes 1 | tf_op jit(solution)/shard_map/pallas_call | solution.py:35
  110.3 5.6 %collective-permute-start.11 = (f32[2048,256]{1,0:T(8,128)}, f32[2048,256]{1,0:T(8,128)}, u32[]{:S(2)}, u32[]{:S(2)}) collective-permute-start(f32[2048,256]{1,0:T(8,128)} %get-tuple-element.52.refs_2_), channel_id=1, source_target_pairs={{0,1},{1,2},{2,3},{3,4},{4,5},{5,6},{6,7},{7,8},{8,9},{9,10},{10,1... | collective-permute-start | bytes 6291464 | tf_op jit(solution)/shard_map/ppermute | solution.py:268
  115.9 1.9 collective-permute-start.14
  117.8 4.5 %shard_map.85 = (f32[8,256,256]{2,1,0:T(8,128)}, f32[8,256,256]{2,1,0:T(8,128)}) custom-call(s32[45]{0:T(128)} %concatenate.3.refs_0_, f32[2,256,512]{2,1,0:T(8,128)} %shard_map.78.refs_6_.refs_1_.refs_9_, f32[2,256,512]{2,1,0:T(8,128)} %collective-permute-done.6.refs_7_.refs_2_.refs_10_, ...), custom_call_target="tpu_custom_call", output_to_operand_aliasing={{0}: (7, {}), {1}: (8, {})} | custom-call | flops 100000000376832 | bytes 1 | tf_op jit(solution)/shard_map/pallas_call | solution.py:35
  122.3 21.3 %collective-permute-done.8.refs_7_.refs_5_.refs_6_ = f32[2,2,256,512]{3,2,1,0:T(8,128)} collective-permute-done((f32[2,2,256,512]{3,2,1,0:T(8,128)}, f32[2,2,256,512]{3,2,1,0:T(8,128)}, u32[]{:S(2)}, u32[]{:S(2)}) %collective-permute-start.8) | collective-permute-done | bytes 2097184 | tf_op jit(solution)/shard_map/ppermute | solution.py:268
  143.6 8.0 %shard_map.86 = (f32[2,2,256,512]{3,2,1,0:T(8,128)}, f32[256,512]{1,0:T(8,128)}) custom-call(s32[45]{0:T(128)} %concatenate.3.refs_0_, f32[4096,512]{1,0:T(8,128)} %bitcast.25, f32[512,512]{1,0:T(8,128)} %get-tuple-element.34.refs_2_.refs_3_, f32[8,256,512]{2,1,0:T(8,128)} %bitcast.27, f32[8,256,512]{2,1,0:T(8,128)} %bitcast.28, ...), custom_call_target="tpu_custom_call" | custom-call | flops 100000000376832 | bytes 1 | tf_op jit(solution)/shard_map/pallas_call | solution.py:35
  151.6 0.7 shard_map.87.refs_11_
  152.3 3.2 %collective-permute-start.16 = (f32[2,2,256,512]{3,2,1,0:T(8,128)}, f32[2,2,256,512]{3,2,1,0:T(8,128)}, u32[]{:S(2)}, u32[]{:S(2)}) collective-permute-start(f32[2,2,256,512]{3,2,1,0:T(8,128)} %get-tuple-element.57.refs_3_.refs_4_), channel_id=1, source_target_pairs={{8,24},{9,25},{10,26},{11,27},{12,28},{13,29},{14,30},{15,31},{24,... | collective-permute-start | bytes 6291464 | tf_op jit(solution)/shard_map/ppermute | solution.py:268
  155.5 6.1 %shard_map.88 = (f32[8,256,256]{2,1,0:T(8,128)}, f32[8,256,256]{2,1,0:T(8,128)}) custom-call(s32[45]{0:T(128)} %concatenate.3.refs_0_, f32[2,256,512]{2,1,0:T(8,128)} %get-tuple-element.42.refs_7_.refs_1_, f32[2,256,512]{2,1,0:T(8,128)} %collective-permute-done.7.refs_5_.refs_2_, ...), custom_call_target="tpu_custom_call", output_to_operand_aliasing={{0}: (7, {}), {1}: (8, {})} | custom-call | flops 100000000376832 | bytes 1 | tf_op jit(solution)/shard_map/pallas_call | solution.py:35
  161.6 6.4 %collective-permute-start.12 = (f32[8,256,256]{2,1,0:T(8,128)}, f32[8,256,256]{2,1,0:T(8,128)}, u32[]{:S(2)}, u32[]{:S(2)}) collective-permute-start(f32[8,256,256]{2,1,0:T(8,128)} %get-tuple-element.54.refs_2_), channel_id=1, source_target_pairs={{0,1},{1,2},{2,3},{3,4},{4,5},{5,6},{6,7},{7,8},{8,9},{9,10},{10,1... | collective-permute-start | bytes 6291464 | tf_op jit(solution)/shard_map/ppermute | solution.py:268
  168.0 2.1 collective-permute-start.13
  170.1 8.1 %shard_map.89 = (f32[2,2,256,512]{3,2,1,0:T(8,128)}, f32[256,512]{1,0:T(8,128)}) custom-call(s32[45]{0:T(128)} %concatenate.3.refs_0_, f32[4096,512]{1,0:T(8,128)} %bitcast.26, f32[512,512]{1,0:T(8,128)} %get-tuple-element.34.refs_2_.refs_3_, f32[8,256,512]{2,1,0:T(8,128)} %bitcast.29, f32[8,256,512]{2,1,0:T(8,128)} %bitcast.30, ...), custom_call_target="tpu_custom_call" | custom-call | flops 100000000376832 | bytes 1 | tf_op jit(solution)/shard_map/pallas_call | solution.py:35
  178.2 2.3 collective-permute-start.15
  180.5 6.1 %shard_map.90.refs_7_ = f32[1024,512]{1,0:T(8,128)} custom-call(s32[45]{0:T(128)} %concatenate.3.refs_0_, f32[2048,256]{1,0:T(8,128)} %get-tuple-element.47.refs_9_.refs_1_, f32[2048,256]{1,0:T(8,128)} %get-tuple-element.52.refs_2_, f32[2048,256]{1,0:T(8,128)} %collective-permute-done.11.refs_12_.refs_3_, ...), custom_call_target="tpu_custom_call" | custom-call | flops 100000000376832 | bytes 1 | tf_op jit(solution)/shard_map/pallas_call | solution.py:35
  186.5 6.0 %shard_map.91.refs_2_ = f32[1024,512]{1,0:T(8,128)} custom-call(s32[45]{0:T(128)} %concatenate.3.refs_0_, f32[2048,256]{1,0:T(8,128)} %get-tuple-element.47.refs_9_.refs_1_, f32[2048,256]{1,0:T(8,128)} %get-tuple-element.52.refs_2_, f32[2048,256]{1,0:T(8,128)} %collective-permute-done.11.refs_12_.refs_3_, ...), custom_call_target="tpu_custom_call" | custom-call | flops 100000000376832 | bytes 1 | tf_op jit(solution)/shard_map/pallas_call | solution.py:35
  192.6 8.5 %collective-permute-done.16.refs_1_ = f32[2,2,256,512]{3,2,1,0:T(8,128)} collective-permute-done((f32[2,2,256,512]{3,2,1,0:T(8,128)}, f32[2,2,256,512]{3,2,1,0:T(8,128)}, u32[]{:S(2)}, u32[]{:S(2)}) %collective-permute-start.16) | collective-permute-done | bytes 2097184 | tf_op jit(solution)/shard_map/ppermute | solution.py:268
  201.1 0.7 shard_map.92.refs_5_.refs_6_
  201.7 16.0 %all-gather.11.cloned.1.call-done = f32[2048,512]{1,0:T(8,128)} async-done(((f32[256,512]{1,0:T(8,128)}), f32[2048,512]{1,0:T(8,128)}) %all-gather.11.cloned.1.call-update) | async-done | bytes 4194320 | tf_op jit(solution)/shard_map/all_gather | solution.py:314
  217.7 6.4 %shard_map.93 = (f32[6,256,256]{2,1,0:T(8,128)}, f32[6,256,256]{2,1,0:T(8,128)}) custom-call(s32[45]{0:T(128)} %concatenate.3.refs_0_, f32[8,256,512]{2,1,0:T(8,128)} %bitcast.31, f32[8,256,512]{2,1,0:T(8,128)} %bitcast.32, f32[2,2,256,512]{3,2,1,0:T(8,128)} %get-tuple-element.57.refs_3_.refs_4_, f32[2,2,256,512]{3,2,1,0:T(8,128)} %get-tuple-element.57.refs_3_.refs_4_, ...), custom_call_target="tpu_custom_call" | custom-call | flops 100000000376832 | bytes 1 | tf_op jit(solution)/shard_map/pallas_call | solution.py:35
  224.2 3.4 %collective-permute-start.19 = (f32[6,256,256]{2,1,0:T(8,128)}, f32[6,256,256]{2,1,0:T(8,128)}, u32[]{:S(2)}, u32[]{:S(2)}) collective-permute-start(f32[6,256,256]{2,1,0:T(8,128)} %get-tuple-element.62.refs_2_), channel_id=1, source_target_pairs={{0,1},{1,2},{2,3},{3,4},{4,5},{5,6},{6,7},{7,8},{8,9},{9,10},{10,1... | collective-permute-start | bytes 4718600 | tf_op jit(solution)/shard_map/ppermute | solution.py:268
  227.5 1.9 collective-permute-start.20
  229.5 0.7 collective-permute-done.13.refs_5_.refs_6_
  230.2 7.5 %shard_map.94.refs_7_.refs_10_ = f32[4096,512]{1,0:T(8,128)} custom-call(s32[45]{0:T(128)} %concatenate.3.refs_0_, f32[8,256,256]{2,1,0:T(8,128)} %get-tuple-element.53.refs_6_.refs_1_.refs_7_.refs_10_, f32[8,256,256]{2,1,0:T(8,128)} %get-tuple-element.54.refs_2_, f32[8,256,256]{2,1,0:T(8,128)} %collective-permute-done.12.refs_3_.refs_4_, ...), custom_call_target="tpu_custom_call" | custom-call | flops 100000000376832 | bytes 1 | tf_op jit(solution)/shard_map/pallas_call | solution.py:35
  237.7 8.3 %collective-permute-done.15.refs_5_.refs_6_ = f32[2,2,256,512]{3,2,1,0:T(8,128)} collective-permute-done((f32[2,2,256,512]{3,2,1,0:T(8,128)}, f32[2,2,256,512]{3,2,1,0:T(8,128)}, u32[]{:S(2)}, u32[]{:S(2)}) %collective-permute-start.15) | collective-permute-done | bytes 2097184 | tf_op jit(solution)/shard_map/ppermute | solution.py:268
  246.0 5.6 %shard_map.95 = (f32[4,256,256]{2,1,0:T(8,128)}, f32[4,256,256]{2,1,0:T(8,128)}) custom-call(s32[45]{0:T(128)} %concatenate.3.refs_0_, f32[8,256,512]{2,1,0:T(8,128)} %bitcast.33, f32[8,256,512]{2,1,0:T(8,128)} %bitcast.34, f32[2,2,256,512]{3,2,1,0:T(8,128)} %get-tuple-element.55.refs_3_.refs_4_, f32[2,2,256,512]{3,2,1,0:T(8,128)} %get-tuple-element.55.refs_3_.refs_4_, ...), custom_call_target="tpu_custom_call" | custom-call | flops 100000000376832 | bytes 1 | tf_op jit(solution)/shard_map/pallas_call | solution.py:35
  251.6 6.8 %collective-permute-start.18 = (f32[4,256,256]{2,1,0:T(8,128)}, f32[4,256,256]{2,1,0:T(8,128)}, u32[]{:S(2)}, u32[]{:S(2)}) collective-permute-start(f32[4,256,256]{2,1,0:T(8,128)} %get-tuple-element.61.refs_2_), channel_id=1, source_target_pairs={{8,9},{9,10},{10,11},{11,12},{12,13},{13,14},{14,15},{24,25},{25,2... | collective-permute-start | bytes 3145736 | tf_op jit(solution)/shard_map/ppermute | solution.py:268
  258.4 2.1 collective-permute-start.17
  260.5 7.0 %shard_map.96.refs_10_ = f32[4096,512]{1,0:T(8,128)} custom-call(s32[45]{0:T(128)} %concatenate.3.refs_0_, f32[8,256,256]{2,1,0:T(8,128)} %get-tuple-element.53.refs_6_.refs_1_.refs_7_.refs_10_, f32[8,256,256]{2,1,0:T(8,128)} %get-tuple-element.54.refs_2_, f32[8,256,256]{2,1,0:T(8,128)} %collective-permute-done.12.refs_3_.refs_4_, ...), custom_call_target="tpu_custom_call", output_to_operand_aliasing={{}: (10, {})} | custom-call | flops 100000000376832 | bytes 1 | tf_op jit(solution)/shard_map/pallas_call | solution.py:35
  267.6 10.1 %collective-permute-done.20.refs_5_.refs_7_.refs_6_.refs_4_ = f32[6,256,256]{2,1,0:T(8,128)} collective-permute-done((f32[6,256,256]{2,1,0:T(8,128)}, f32[6,256,256]{2,1,0:T(8,128)}, u32[]{:S(2)}, u32[]{:S(2)}) %collective-permute-start.20) | collective-permute-done | bytes 1572896 | tf_op jit(solution)/shard_map/ppermute | solution.py:268
  277.7 6.7 %shard_map.97.refs_10_ = f32[4096,512]{1,0:T(8,128)} custom-call(s32[45]{0:T(128)} %concatenate.3.refs_0_, f32[6,256,256]{2,1,0:T(8,128)} %get-tuple-element.59.refs_11_.refs_1_, f32[6,256,256]{2,1,0:T(8,128)} %get-tuple-element.62.refs_2_, f32[8,256,256]{2,1,0:T(8,128)} %collective-permute-done.12.refs_3_.refs_4_, ...), custom_call_target="tpu_custom_call", output_to_operand_aliasing={{}: (10, {})} | custom-call | flops 100000000376832 | bytes 1 | tf_op jit(solution)/shard_map/pallas_call | solution.py:35
  284.4 3.7 %shard_map.98.refs_7_ = f32[4096,512]{1,0:T(8,128)} custom-call(s32[45]{0:T(128)} %concatenate.3.refs_0_, f32[8,256,256]{2,1,0:T(8,128)} %get-tuple-element.53.refs_6_.refs_1_.refs_7_.refs_10_, f32[8,256,256]{2,1,0:T(8,128)} %get-tuple-element.54.refs_2_, f32[8,256,256]{2,1,0:T(8,128)} %collective-permute-done.12.refs_3_.refs_4_, ...), custom_call_target="tpu_custom_call", output_to_operand_aliasing={{}: (10, {})} | custom-call | flops 100000000376832 | bytes 1 | tf_op jit(solution)/shard_map/pallas_call | solution.py:35
  288.1 3.7 %shard_map.99.refs_10_ = f32[4096,512]{1,0:T(8,128)} custom-call(s32[45]{0:T(128)} %concatenate.3.refs_0_, f32[256,512]{1,0:T(8,128)} %get-tuple-element.58.refs_7_.refs_1_, f32[6,256,256]{2,1,0:T(8,128)} %collective-permute-done.19.refs_4_.refs_2_.refs_3_, ...), custom_call_target="tpu_custom_call", output_to_operand_aliasing={{}: (7, {})} | custom-call | flops 100000000376832 | bytes 1 | tf_op jit(solution)/shard_map/pallas_call | solution.py:35
  291.8 7.2 %shard_map.100.refs_10_ = f32[4096,512]{1,0:T(8,128)} custom-call(s32[45]{0:T(128)} %concatenate.3.refs_0_, f32[4,256,256]{2,1,0:T(8,128)} %get-tuple-element.60.refs_11_.refs_1_.refs_7_, f32[4,256,256]{2,1,0:T(8,128)} %get-tuple-element.61.refs_2_, f32[8,256,256]{2,1,0:T(8,128)} %collective-permute-done.12.refs_3_.refs_4_, ...), custom_call_target="tpu_custom_call", output_to_operand_aliasing={{}: (10, {})} | custom-call | flops 100000000376832 | bytes 1 | tf_op jit(solution)/shard_map/pallas_call | solution.py:35
  298.9 3.5 %shard_map.101 = f32[4096,512]{1,0:T(8,128)} custom-call(s32[45]{0:T(128)} %concatenate.3.refs_0_, f32[8,256,256]{2,1,0:T(8,128)} %get-tuple-element.53.refs_6_.refs_1_.refs_7_.refs_10_, f32[8,256,256]{2,1,0:T(8,128)} %get-tuple-element.54.refs_2_, f32[8,256,256]{2,1,0:T(8,128)} %collective-permute-done.12.refs_3_.refs_4_, ...), custom_call_target="tpu_custom_call", output_to_operand_aliasing={{}: (10, {})} | custom-call | flops 100000000376832 | bytes 1 | tf_op jit(solution)/shard_map/pallas_call | solution.py:35
  (25 shorter events, 0.2 us)
Async XLA Ops:
  7.2 2.8 copy-start.2
  7.2 56.5 %all-gather.7.cloned.1.call-start = ((), (), s32[]{:S(2)}) async-start(), calls=%async_computation | async-start | bytes 4718592 | tf_op jit(solution)/shard_map/all_gather | solution.py:314
  8.5 4.6 %collective-permute-start = (f32[512,512]{1,0:T(8,128)S(1)}, f32[512,512]{1,0:T(8,128)S(1)}, u32[]{:S(2)}, u32[]{:S(2)}) collective-permute-start(f32[512,512]{1,0:T(8,128)S(1)} %slice_bitcast_fusion), channel_id=1, source_target_pairs={{0,1},{2,3},{4,5},{6,7},{8,9},{10,11},{12,13},{14,15},{17,16},{19,... | collective-permute-start | bytes 3145736 | tf_op jit(solution)/shard_map/ppermute | solution.py:268
  13.1 1.0 copy-start.1
  18.9 124.7 %all-gather.9.cloned.1.call-start = ((), (), s32[]{:S(2)}) async-start(), calls=%async_computation.1 | async-start | bytes 4718592 | tf_op jit(solution)/shard_map/all_gather | solution.py:314
  19.0 50.3 %collective-permute-start.5 = (f32[256,512]{1,0:T(8,128)}, f32[256,512]{1,0:T(8,128)}, u32[]{:S(2)}, u32[]{:S(2)}) collective-permute-start(f32[256,512]{1,0:T(8,128)} %get-tuple-element.38), channel_id=1, source_target_pairs={{0,8},{1,9},{2,10},{3,11},{4,12},{5,13},{6,14},{7,15},{16,24},{17,... | collective-permute-start | bytes 1572872 | tf_op jit(solution)/shard_map/ppermute | solution.py:268
  20.3 19.3 %collective-permute-start.2 = (f32[512,256]{1,0:T(8,128)}, f32[512,256]{1,0:T(8,128)}, u32[]{:S(2)}, u32[]{:S(2)}) collective-permute-start(f32[512,256]{1,0:T(8,128)} %get-tuple-element.37), channel_id=1, source_target_pairs={{0,1},{1,2},{2,3},{3,4},{4,5},{5,6},{6,7},{7,8},{8,9},{9,10},{10,1... | collective-permute-start | bytes 1572872 | tf_op jit(solution)/shard_map/ppermute | solution.py:268
  23.4 34.0 %collective-permute-start.1 = (f32[256,512]{1,0:T(8,128)}, f32[256,512]{1,0:T(8,128)}, u32[]{:S(2)}, u32[]{:S(2)}) collective-permute-start(f32[256,512]{1,0:T(8,128)} %get-tuple-element.33.refs_1_.refs_2_), channel_id=1, source_target_pairs={{0,2},{1,3},{2,0},{3,1},{4,6},{5,7},{6,4},{7,5},{8,10},{9,11},{10,... | collective-permute-start | bytes 1572872 | tf_op jit(solution)/shard_map/ppermute | solution.py:268
  30.1 33.6 %collective-permute-start.4 = (f32[1,2,256,512]{3,2,1,0:T(8,128)}, f32[1,2,256,512]{3,2,1,0:T(8,128)}, u32[]{:S(2)}, u32[]{:S(2)}) collective-permute-start(f32[1,2,256,512]{3,2,1,0:T(8,128)} %get-tuple-element.39.refs_3_.refs_4_), channel_id=1, source_target_pairs={{6,22},{7,23},{14,30},{15,31},{23,7},{31,15}} | collective-permute-start | bytes 3145736 | tf_op jit(solution)/shard_map/ppermute | solution.py:268
  57.4 4.4 %copy-start = (s32[256]{0:T(256)S(1)}, s32[256]{0:T(256)}, u32[]{:S(2)}) copy-start(s32[256]{0:T(256)} %iota_add_fusion) | copy-start | bytes 3076
  60.5 13.8 %collective-permute-start.6 = (f32[2,256,512]{2,1,0:T(8,128)}, f32[2,256,512]{2,1,0:T(8,128)}, u32[]{:S(2)}, u32[]{:S(2)}) collective-permute-start(f32[2,256,512]{2,1,0:T(8,128)} %shard_map.78.refs_6_.refs_1_.refs_9_), channel_id=1, source_target_pairs={{0,1},{1,0},{2,3},{3,2},{4,5},{5,4},{6,7},{7,6},{8,9},{9,8},{10,11... | collective-permute-start | bytes 3145736 | tf_op jit(solution)/shard_map/ppermute | solution.py:268
  60.5 26.4 %collective-permute-start.3 = (f32[2,256,512]{2,1,0:T(8,128)}, f32[2,256,512]{2,1,0:T(8,128)}, u32[]{:S(2)}, u32[]{:S(2)}) collective-permute-start(f32[2,256,512]{2,1,0:T(8,128)} %shard_map.78.refs_6_.refs_1_.refs_9_), channel_id=1, source_target_pairs={{0,4},{1,5},{2,6},{3,7},{4,8},{5,9},{6,10},{7,11},{8,12},{9,13},{1... | collective-permute-start | bytes 3145736 | tf_op jit(solution)/shard_map/ppermute | solution.py:268
  70.0 147.7 %all-gather.11.cloned.1.call-start = ((), (), s32[]{:S(2)}) async-start(), calls=%async_computation.2 | async-start | bytes 4718592 | tf_op jit(solution)/shard_map/all_gather | solution.py:314
  70.1 27.3 %collective-permute-start.9 = (f32[1,2,256,512]{3,2,1,0:T(8,128)}, f32[1,2,256,512]{3,2,1,0:T(8,128)}, u32[]{:S(2)}, u32[]{:S(2)}) collective-permute-start(f32[1,2,256,512]{3,2,1,0:T(8,128)} %get-tuple-element.44.refs_3_.refs_4_), channel_id=1, source_target_pairs={{4,20},{5,21},{6,22},{7,23},{12,28},{13,29},{14,30},{15,31},{21,5}... | collective-permute-start | bytes 3145736 | tf_op jit(solution)/shard_map/ppermute | solution.py:268
  87.6 64.0 %collective-permute-start.10 = (f32[256,512]{1,0:T(8,128)}, f32[256,512]{1,0:T(8,128)}, u32[]{:S(2)}, u32[]{:S(2)}) collective-permute-start(f32[256,512]{1,0:T(8,128)} %get-tuple-element.50), channel_id=1, source_target_pairs={{0,8},{1,9},{2,10},{3,11},{4,12},{5,13},{6,14},{7,15},{16,24},{17,... | collective-permute-start | bytes 1572872 | tf_op jit(solution)/shard_map/ppermute | solution.py:268
  88.9 13.1 %collective-permute-start.7 = (f32[2,256,512]{2,1,0:T(8,128)}, f32[2,256,512]{2,1,0:T(8,128)}, u32[]{:S(2)}, u32[]{:S(2)}) collective-permute-start(f32[2,256,512]{2,1,0:T(8,128)} %get-tuple-element.42.refs_7_.refs_1_), channel_id=1, source_target_pairs={{0,1},{1,0},{2,3},{3,2},{4,5},{5,4},{6,7},{7,6},{8,9},{9,8},{10,11... | collective-permute-start | bytes 3145736 | tf_op jit(solution)/shard_map/ppermute | solution.py:268
  92.0 51.6 %collective-permute-start.8 = (f32[2,2,256,512]{3,2,1,0:T(8,128)}, f32[2,2,256,512]{3,2,1,0:T(8,128)}, u32[]{:S(2)}, u32[]{:S(2)}) collective-permute-start(f32[2,2,256,512]{3,2,1,0:T(8,128)} %get-tuple-element.43.refs_3_.refs_4_), channel_id=1, source_target_pairs={{0,16},{1,17},{2,18},{3,19},{4,20},{5,21},{6,22},{7,23},{8,24},{9,... | collective-permute-start | bytes 6291464 | tf_op jit(solution)/shard_map/ppermute | solution.py:268
  110.3 45.2 %collective-permute-start.11 = (f32[2048,256]{1,0:T(8,128)}, f32[2048,256]{1,0:T(8,128)}, u32[]{:S(2)}, u32[]{:S(2)}) collective-permute-start(f32[2048,256]{1,0:T(8,128)} %get-tuple-element.52.refs_2_), channel_id=1, source_target_pairs={{0,1},{1,2},{2,3},{3,4},{4,5},{5,6},{6,7},{7,8},{8,9},{9,10},{10,1... | collective-permute-start | bytes 6291464 | tf_op jit(solution)/shard_map/ppermute | solution.py:268
  115.9 54.2 %collective-permute-start.14 = (f32[2048,256]{1,0:T(8,128)}, f32[2048,256]{1,0:T(8,128)}, u32[]{:S(2)}, u32[]{:S(2)}) collective-permute-start(f32[2048,256]{1,0:T(8,128)} %get-tuple-element.47.refs_9_.refs_1_), channel_id=1, source_target_pairs={{1,0},{2,1},{3,2},{4,3},{5,4},{6,5},{7,6},{8,7},{9,8},{10,9},{11,1... | collective-permute-start | bytes 6291464 | tf_op jit(solution)/shard_map/ppermute | solution.py:268
  152.3 48.8 %collective-permute-start.16 = (f32[2,2,256,512]{3,2,1,0:T(8,128)}, f32[2,2,256,512]{3,2,1,0:T(8,128)}, u32[]{:S(2)}, u32[]{:S(2)}) collective-permute-start(f32[2,2,256,512]{3,2,1,0:T(8,128)} %get-tuple-element.57.refs_3_.refs_4_), channel_id=1, source_target_pairs={{8,24},{9,25},{10,26},{11,27},{12,28},{13,29},{14,30},{15,31},{24,... | collective-permute-start | bytes 6291464 | tf_op jit(solution)/shard_map/ppermute | solution.py:268
  161.6 67.9 %collective-permute-start.12 = (f32[8,256,256]{2,1,0:T(8,128)}, f32[8,256,256]{2,1,0:T(8,128)}, u32[]{:S(2)}, u32[]{:S(2)}) collective-permute-start(f32[8,256,256]{2,1,0:T(8,128)} %get-tuple-element.54.refs_2_), channel_id=1, source_target_pairs={{0,1},{1,2},{2,3},{3,4},{4,5},{5,6},{6,7},{7,8},{8,9},{9,10},{10,1... | collective-permute-start | bytes 6291464 | tf_op jit(solution)/shard_map/ppermute | solution.py:268
  168.0 62.2 %collective-permute-start.13 = (f32[8,256,256]{2,1,0:T(8,128)}, f32[8,256,256]{2,1,0:T(8,128)}, u32[]{:S(2)}, u32[]{:S(2)}) collective-permute-start(f32[8,256,256]{2,1,0:T(8,128)} %get-tuple-element.53.refs_6_.refs_1_.refs_7_.refs_10_), channel_id=1, source_target_pairs={{1,0},{2,1},{3,2},{4,3},{5,4},{6,5},{7,6},{8,7},{9,8},{10,9},{11,1... | collective-permute-start | bytes 6291464 | tf_op jit(solution)/shard_map/ppermute | solution.py:268
  178.2 67.8 %collective-permute-start.15 = (f32[2,2,256,512]{3,2,1,0:T(8,128)}, f32[2,2,256,512]{3,2,1,0:T(8,128)}, u32[]{:S(2)}, u32[]{:S(2)}) collective-permute-start(f32[2,2,256,512]{3,2,1,0:T(8,128)} %get-tuple-element.55.refs_3_.refs_4_), channel_id=1, source_target_pairs={{8,24},{9,25},{10,26},{11,27},{12,28},{13,29},{14,30},{15,31},{24,... | collective-permute-start | bytes 6291464 | tf_op jit(solution)/shard_map/ppermute | solution.py:268
  224.2 43.4 %collective-permute-start.19 = (f32[6,256,256]{2,1,0:T(8,128)}, f32[6,256,256]{2,1,0:T(8,128)}, u32[]{:S(2)}, u32[]{:S(2)}) collective-permute-start(f32[6,256,256]{2,1,0:T(8,128)} %get-tuple-element.62.refs_2_), channel_id=1, source_target_pairs={{0,1},{1,2},{2,3},{3,4},{4,5},{5,6},{6,7},{7,8},{8,9},{9,10},{10,1... | collective-permute-start | bytes 4718600 | tf_op jit(solution)/shard_map/ppermute | solution.py:268
  227.5 50.1 %collective-permute-start.20 = (f32[6,256,256]{2,1,0:T(8,128)}, f32[6,256,256]{2,1,0:T(8,128)}, u32[]{:S(2)}, u32[]{:S(2)}) collective-permute-start(f32[6,256,256]{2,1,0:T(8,128)} %get-tuple-element.59.refs_11_.refs_1_), channel_id=1, source_target_pairs={{1,0},{2,1},{3,2},{4,3},{5,4},{6,5},{7,6},{8,7},{9,8},{10,9},{11,1... | collective-permute-start | bytes 4718600 | tf_op jit(solution)/shard_map/ppermute | solution.py:268
  251.6 40.2 %collective-permute-start.18 = (f32[4,256,256]{2,1,0:T(8,128)}, f32[4,256,256]{2,1,0:T(8,128)}, u32[]{:S(2)}, u32[]{:S(2)}) collective-permute-start(f32[4,256,256]{2,1,0:T(8,128)} %get-tuple-element.61.refs_2_), channel_id=1, source_target_pairs={{8,9},{9,10},{10,11},{11,12},{12,13},{13,14},{14,15},{24,25},{25,2... | collective-permute-start | bytes 3145736 | tf_op jit(solution)/shard_map/ppermute | solution.py:268
  258.4 33.4 %collective-permute-start.17 = (f32[4,256,256]{2,1,0:T(8,128)}, f32[4,256,256]{2,1,0:T(8,128)}, u32[]{:S(2)}, u32[]{:S(2)}) collective-permute-start(f32[4,256,256]{2,1,0:T(8,128)} %get-tuple-element.60.refs_11_.refs_1_.refs_7_), channel_id=1, source_target_pairs={{8,7},{9,8},{10,9},{11,10},{12,11},{13,12},{14,13},{15,14},{24,23}... | collective-permute-start | bytes 3145736 | tf_op jit(solution)/shard_map/ppermute | solution.py:268
Sparse Core Ops, SparseCore 0:
  19.0 42.4 all-gather.6
  70.1 42.2 all-gather.8
  152.4 65.3 all-gather.10
